TPU v7x, 32 devices: a whole 2x2x4 slice. The times are simulated.
32 devices in a mesh: proto: 8 (over y, x, core), batch: 4 (over z).
Axes of the slice: x: 2, y: 2, z: 4, core: 2. Of those that a mesh axis runs over, the one named last changes fastest.
Arguments:
- teacher_feats: bfloat16 [1024, 512], P('batch'), may hold values from -200 to 200
- student_feats: bfloat16 [1024, 512], P('batch'), may hold values from -200 to 200
- proto_weight: bfloat16 [512, 65536], P(None, 'proto'), may hold values from -40 to 40
Outputs:
- grad_weight: bfloat16 [512, 65536], P('batch', 'proto')
- grad_student: float32 [1024, 512], P('batch')
- loss: float32 [], replicated
All inputs are finite; a program needn't handle non-finite values.
Results may differ from a plain program's by a relative error of at most 0.012.
Values may be sent and summed in bfloat16 or wider, within the bound.
No kernel may reach another device: no remote copies, remote signals or barrier semaphores. Data moves between devices by JAX's collectives and lax.ppermute only.
A program may use at most 128 MiB of HBM per device.

v0:
```python
import jax
import jax.numpy as jnp
from jax import lax
from jax.sharding import PartitionSpec as P

SWEEPS = 3


TEMP_TEACHER = 0.04
TEMP_STUDENT = 0.1


def swapped(value, axis, stride):
    mask = 2**stride
    pairs = [(source, source ^ mask) for source in range(lax.axis_size(axis))]
    return lax.ppermute(value, axis, pairs)


def unit_rows(values):
    wide = values.astype(jnp.float32)
    length = jnp.sqrt(jnp.sum(wide * wide, axis=-1, keepdims=True) + 1e-06)
    return (wide / length, length)


def local(teacher_feats, student_feats, proto_weight):
    swap_bit = lax.axis_size("batch").bit_length() - 2
    rows_here = teacher_feats.shape[0]
    total_rows = rows_here * lax.axis_size("batch")
    protos_all = proto_weight.shape[1] * lax.axis_size("proto")
    teacher_unit, _ = unit_rows(teacher_feats)
    student_unit, student_len = unit_rows(student_feats)
    student_half = student_unit.astype(jnp.bfloat16)
    teacher_logits = (
        jnp.dot(teacher_unit.astype(jnp.bfloat16), proto_weight, preferred_element_type=jnp.float32)
        / TEMP_TEACHER
    )
    student_logits = (
        jnp.dot(student_half, proto_weight, preferred_element_type=jnp.float32) / TEMP_STUDENT
    )
    teach_max, stud_max = lax.pmax(
        (jnp.max(teacher_logits, axis=1), jnp.max(student_logits, axis=1)), "proto"
    )
    teach_total, stud_total = lax.psum(
        (
            jnp.sum(jnp.exp(teacher_logits - teach_max[:, None]), axis=1),
            jnp.sum(jnp.exp(student_logits - stud_max[:, None]), axis=1),
        ),
        "proto",
    )
    prob = jnp.exp(teacher_logits - teach_max[:, None]) / teach_total[:, None]
    row_scale = jnp.ones((rows_here,), jnp.float32)
    col_scale = jnp.ones((proto_weight.shape[1],), jnp.float32)
    for sweep in range(SWEEPS):
        col_scale = 1.0 / lax.psum(
            jnp.dot(row_scale, prob, precision=lax.Precision.HIGHEST).astype(jnp.bfloat16), "batch"
        ).astype(jnp.float32)
        row_scale = 1.0 / lax.psum(
            jnp.dot(prob, col_scale, precision=lax.Precision.HIGHEST), "proto"
        )
    paired = prob * row_scale[:, None] * col_scale[None, :]
    paired = swapped(paired, "batch", swap_bit)
    log_total = stud_max + jnp.log(stud_total)
    student_prob = jnp.exp(student_logits - log_total[:, None])
    loss_part = jnp.sum(paired * (log_total[:, None] - student_logits))
    dlogits = (protos_all * (student_prob - paired)).astype(jnp.bfloat16)
    grad_weight = lax.psum_scatter(
        lax.dot_general(
            student_half, dlogits, (((0,), (0,)), ((), ())), preferred_element_type=jnp.float32
        ),
        "batch",
        scatter_dimension=0,
        tiled=True,
    ).astype(jnp.bfloat16)
    local_back = lax.dot_general(
        dlogits, proto_weight, (((1,), (1,)), ((), ())), preferred_element_type=jnp.float32
    )
    back_sum = lax.psum(local_back, "proto")
    loss = lax.psum(loss_part, ("proto", "batch")) / total_rows
    grad_rows = (
        back_sum - student_unit * jnp.sum(student_unit * back_sum, axis=-1, keepdims=True)
    ) / student_len
    return (grad_weight, grad_rows, loss)


def solution(mesh):
    return jax.shard_map(
        local,
        mesh=mesh,
        in_specs=(P("batch", None), P("batch", None), P(None, "proto")),
        out_specs=(P("batch", "proto"), P("batch", None), P()),
        check_vma=False,
    )
```

profile of v0, /device:TPU:0, one launch (start us, length us, event | category | flops | bytes accessed | tf_op | source)
XLA Modules:
  0.0 877.8 jit_solution(18377148251569747004)
XLA Ops:
  10.4 9.3 %fusion.13 = (f32[256]{0:T(256)S(1)}, f32[256,8192]{1,0:T(8,128)}) fusion(bf16[512,8192]{1,0:T(8,128)(2,1)} %param.5, bf16[256,512]{1,0:T(8,128)(2,1)} %param.3, f32[256]{0:T(256)S(1)} %add_sqrt_fusion), kind=kOutput, calls=%fused_computation.34 | convolution fusion | flops 2152070912 | bytes 17041408 | tf_op jit(solution)/shard_map/dot_general | solution.py:34
  19.7 5.8 fusion.14
  25.6 15.1 %all-reduce.1 = (f32[256]{0:T(256)S(1)}, f32[256]{0:T(256)S(1)}) all-reduce(f32[256]{0:T(256)S(1)} %get-tuple-element.9, f32[256]{0:T(256)S(1)} %get-tuple-element.11), channel_id=1, replica_groups=mesh['proto'=8,'batch'=4] {'proto'}, use_global_device_ids=true, to_apply=%region_7.0 | all-reduce | flops 512 | bytes 4096 | tf_op jit(solution)/shard_map/pmax | solution.py:40
  40.7 7.1 exponential_reduce_fusion
  47.8 11.8 %psum.71 = f32[256]{0:T(256)S(1)} all-reduce(f32[256]{0:T(256)S(1)} %get-tuple-element.14), channel_id=1, replica_groups=mesh['proto'=8,'batch'=4] {'proto'}, use_global_device_ids=true, to_apply=%region_9.0 | all-reduce | flops 256 | bytes 2048 | tf_op jit(solution)/shard_map/psum | solution.py:43
  59.6 4.1 fusion
  66.9 4.0 fusion.10
  71.0 19.3 %psum.72 = bf16[8192]{0:T(1024)(128)(2,1)S(1)} all-reduce(bf16[8192]{0:T(1024)(128)(2,1)S(1)} %convert_element_type.40), channel_id=1, replica_groups=mesh['proto'=8,'batch'=4] {'batch'}, use_global_device_ids=true, to_apply=%region_10.0 | all-reduce | flops 8192 | bytes 32768 | tf_op jit(solution)/shard_map/psum | solution.py:54
  90.3 8.9 %fusion.15 = f32[1,256]{1,0:T(1,128)S(1)} fusion(f32[256,8192]{1,0:T(8,128)} %copy-done, f32[8192,1]{0,1:T(1,128)S(1)} %bitcast.28), kind=kOutput, calls=%fused_computation.36 | convolution fusion | flops 25165824 | bytes 8422400 | tf_op jit(solution)/shard_map/dot_general | solution.py:58
  99.2 11.8 %psum.73 = f32[256]{0:T(256)S(1)} all-reduce(f32[256]{0:T(256)S(1)} %bitcast.34), channel_id=1, replica_groups=mesh['proto'=8,'batch'=4] {'proto'}, use_global_device_ids=true, to_apply=%region_11.0 | all-reduce | flops 256 | bytes 2048 | tf_op jit(solution)/shard_map/psum | solution.py:57
  111.0 7.4 fusion.16
  118.4 15.5 %psum.74 = bf16[8192]{0:T(1024)(128)(2,1)S(1)} all-reduce(bf16[8192]{0:T(1024)(128)(2,1)S(1)} %convert_element_type.42), channel_id=1, replica_groups=mesh['proto'=8,'batch'=4] {'batch'}, use_global_device_ids=true, to_apply=%region_12.0 | all-reduce | flops 8192 | bytes 32768 | tf_op jit(solution)/shard_map/psum | solution.py:54
  133.9 8.9 %fusion.17 = f32[1,256]{1,0:T(1,128)S(1)} fusion(f32[256,8192]{1,0:T(8,128)} %copy-done, f32[8192,1]{0,1:T(1,128)S(1)} %bitcast.30), kind=kOutput, calls=%fused_computation.38 | convolution fusion | flops 25165824 | bytes 8422400 | tf_op jit(solution)/shard_map/dot_general | solution.py:58
  142.8 12.0 %psum.75 = f32[256]{0:T(256)S(1)} all-reduce(f32[256]{0:T(256)S(1)} %bitcast.36), channel_id=1, replica_groups=mesh['proto'=8,'batch'=4] {'proto'}, use_global_device_ids=true, to_apply=%region_13.0 | all-reduce | flops 256 | bytes 2048 | tf_op jit(solution)/shard_map/psum | solution.py:57
  154.8 7.4 fusion.18
  162.3 16.3 %psum.76 = bf16[8192]{0:T(1024)(128)(2,1)S(1)} all-reduce(bf16[8192]{0:T(1024)(128)(2,1)S(1)} %convert_element_type.44), channel_id=1, replica_groups=mesh['proto'=8,'batch'=4] {'batch'}, use_global_device_ids=true, to_apply=%region_14.0 | all-reduce | flops 8192 | bytes 32768 | tf_op jit(solution)/shard_map/psum | solution.py:54
  178.6 8.9 %fusion.19 = f32[1,256]{1,0:T(1,128)S(1)} fusion(f32[256,8192]{1,0:T(8,128)} %copy-done, f32[8192,1]{0,1:T(1,128)S(1)} %bitcast.27), kind=kOutput, calls=%fused_computation.40 | convolution fusion | flops 25165824 | bytes 8422400 | tf_op jit(solution)/shard_map/dot_general | solution.py:58
  187.5 12.1 %all-reduce = (f32[256]{0:T(256)S(1)}, f32[256]{0:T(256)S(1)}) all-reduce(f32[256]{0:T(256)S(1)} %bitcast.33, f32[256]{0:T(256)S(1)} %get-tuple-element.13), channel_id=1, replica_groups=mesh['proto'=8,'batch'=4] {'proto'}, use_global_device_ids=true, to_apply=%region_15.0 | all-reduce | flops 512 | bytes 4096 | tf_op jit(solution)/shard_map/psum | solution.py:57
  199.5 4.4 multiply_multiply_fusion
  204.1 361.6 %collective-permute-done = f32[256,8192]{1,0:T(8,128)S(1)} collective-permute-done((f32[256,8192]{1,0:T(8,128)S(1)}, f32[256,8192]{1,0:T(8,128)S(1)}, u32[]{:S(2)}, u32[]{:S(2)}) %collective-permute-start) | collective-permute-done | bytes 8388640 | tf_op jit(solution)/shard_map/ppermute | solution.py:16
  565.6 5.3 multiply_reduce_fusion
  576.1 10.4 %fusion.7 = f32[512,8192]{1,0:T(8,128)} fusion(bf16[256,8192]{1,0:T(8,128)(2,1)} %copy-done.1, bf16[256,512]{1,0:T(8,128)(2,1)S(1)} %copy-done.2, f32[256]{0:T(256)S(1)} %add_sqrt_fusion.1), kind=kOutput, calls=%fused_computation.19 | convolution fusion | flops 2147876864 | bytes 21234688 | tf_op jit(solution)/shard_map/dot_general | solution.py:67
  586.5 40.0 %psum.79 = f32[]{:T(128)} all-reduce(f32[]{:T(128)} %get-tuple-element.7), channel_id=1, replica_groups=mesh['proto'=8,'batch'=4] {'proto','batch'}, use_global_device_ids=true, to_apply=%region_20.0 | all-reduce | flops 1 | bytes 8 | tf_op jit(solution)/shard_map/psum | solution.py:78
  631.2 233.9 %reduce-scatter.2.cloned.1.call-done = f32[128,8192]{1,0:T(8,128)} async-done(((f32[512,8192]{1,0:T(8,128)}), f32[128,8192]{1,0:T(8,128)}) %reduce-scatter.2.cloned.1.call-update) | async-done | bytes 4194320 | tf_op jit(solution)/shard_map/reduce_scatter | solution.py:66
  (40 shorter events, 18.8 us)
Async XLA Ops:
  8.0 620.0 %all-reduce.4.cloned.1.call-start = ((), (), s32[]{:S(2)}) async-start(), calls=%async_computation.2 | async-start | bytes 1048576 | tf_op jit(solution)/shard_map/psum | solution.py:77
  9.1 10.6 %slice-start = ((s8[8388608]{0:T(1024)(128)(4,1)}), s8[4194304]{0:T(1024)(128)(4,1)S(1)}, s32[]{:S(2)}) async-start(s8[8388608]{0:T(1024)(128)(4,1)} %bitcast.38), calls=%async_computation.3 | async-start | bytes 8388608
  10.4 9.3 %copy-start.2 = (bf16[256,512]{1,0:T(8,128)(2,1)S(1)}, bf16[256,512]{1,0:T(8,128)(2,1)}, u32[]{:S(2)}) copy-start(bf16[256,512]{1,0:T(8,128)(2,1)} %param.4) | copy-start | bytes 786436
  10.4 9.3 %slice-start.1 = ((s8[8388608]{0:T(1024)(128)(4,1)}), s8[4194304]{0:T(1024)(128)(4,1)S(1)}, s32[]{:S(2)}) async-start(s8[8388608]{0:T(1024)(128)(4,1)} %bitcast.38), calls=%async_computation.4 | async-start | bytes 8388608
  63.7 3.2 copy-start
  203.9 361.7 %collective-permute-start = (f32[256,8192]{1,0:T(8,128)S(1)}, f32[256,8192]{1,0:T(8,128)S(1)}, u32[]{:S(2)}, u32[]{:S(2)}) collective-permute-start(f32[256,8192]{1,0:T(8,128)S(1)} %multiply_multiply_fusion), channel_id=1, source_target_pairs={{0,2},{1,3},{2,0},{3,1},{4,6},{5,7},{6,4},{7,5},{8,10},{9,11},{10,... | collective-permute-start | bytes 25165832 | tf_op jit(solution)/shard_map/ppermute | solution.py:16
  204.0 368.8 %slice-start.2 = ((s8[8388608]{0:T(1024)(128)(4,1)}), s8[4194304]{0:T(1024)(128)(4,1)S(1)}, s32[]{:S(2)}) async-start(s8[8388608]{0:T(1024)(128)(4,1)} %bitcast.40), calls=%async_computation.5 | async-start | bytes 8388608
  204.1 368.8 %slice-start.3 = ((s8[8388608]{0:T(1024)(128)(4,1)}), s8[4194304]{0:T(1024)(128)(4,1)S(1)}, s32[]{:S(2)}) async-start(s8[8388608]{0:T(1024)(128)(4,1)} %bitcast.40), calls=%async_computation.6 | async-start | bytes 8388608
  570.9 1.9 copy-start.1
  576.0 289.0 %reduce-scatter.2.cloned.1.call-start = ((), (), s32[]{:S(2)}) async-start(), calls=%async_computation.1 | async-start | bytes 20971520 | tf_op jit(solution)/shard_map/reduce_scatter | solution.py:66
Sparse Core Ops, SparseCore 0:
  576.2 51.7 all-reduce.3
Sparse Core Ops, SparseCore 1:
  586.6 278.4 reduce-scatter.1
where the time goes:
time: 886 us; the launch traced here: 878 us
  waiting for transfers between devices  596 us (67%)
  blocking collectives  154 us (17%)
  matrix products  74.2 us (8%)
  other arithmetic  30.4 us (3%)
  between operations  17.8 us (2%)
    ppermute x1, waiting for transfers between devices, swapped(): return lax.ppermute(value, axis, pairs)  362 us
    reduce_scatter x1, waiting for transfers between devices, local(): lax.psum_scatter(lax.dot_general(student_half, dlogits, (((0,), (0,)), ((...  234 us
    psum x3, blocking collectives, local(): lax.psum(jnp.dot(row_scale, prob, precision=lax.Precision.HIGHEST).astype...  51.1 us
    psum x1, blocking collectives, local(): loss = lax.psum(loss_part, ('proto', 'batch')) / total_rows  40 us
    psum x3, blocking collectives, local(): lax.psum(jnp.dot(prob, col_scale, precision=lax.Precision.HIGHEST), 'proto')  35.9 us
    dot_general x3, matrix products, local(): jnp.dot(prob, col_scale, precision=lax.Precision.HIGHEST)  26.7 us
    dot_general x3, matrix products, local(): jnp.dot(row_scale, prob, precision=lax.Precision.HIGHEST)  18.9 us
  transfers between devices with their start and end apart: 3, of which 3 were waited for; matrix products, arithmetic and copies ran while one was open for 2% of the time, Pallas kernels for 0%

commit v1 on v0

v1 whole, which is shorter than its diff:
```python
import functools
import math

import jax
import jax.numpy as jnp
from jax import lax
from jax.experimental import pallas as pl
from jax.experimental.pallas import tpu as pltpu
from jax.sharding import PartitionSpec as P

SWEEPS = 3
TEMP_TEACHER = 0.04
TEMP_STUDENT = 0.1
LOG2E = math.log2(math.e)
SCALE_TEACHER = LOG2E / TEMP_TEACHER
SCALE_STUDENT = LOG2E / TEMP_STUDENT
LANES = 128
GROUP = 128
TILE = 256
F32 = jnp.float32
BF16 = jnp.bfloat16


def unit_rows(values):
    wide = values.astype(F32)
    length = jnp.sqrt(jnp.sum(wide * wide, axis=-1, keepdims=True) + 1e-06)
    return wide / length, length


def diagonal():
    shape = (LANES, LANES)
    return lax.broadcasted_iota(jnp.int32, shape, 0) == lax.broadcasted_iota(jnp.int32, shape, 1)


def to_column(row):
    spread = jnp.where(diagonal(), jnp.broadcast_to(row, (LANES, LANES)), 0.0)
    return jnp.sum(spread, axis=1, keepdims=True)


def to_row(column):
    spread = jnp.where(diagonal(), jnp.broadcast_to(column, (LANES, LANES)), 0.0)
    return jnp.sum(spread, axis=0, keepdims=True)


def spread_rows(ref, rows):
    for a in range(rows.shape[0]):
        ref[a * LANES : (a + 1) * LANES, :] = jnp.broadcast_to(
            to_column(rows[a : a + 1, :]), (LANES, LANES)
        )


def pack_rows(ref, columns):
    for a in range(columns.shape[0] // LANES):
        ref[a : a + 1, :] = to_row(columns[a * LANES : (a + 1) * LANES, :])


def lane_tiles(values):
    return [values[:, t * LANES : (t + 1) * LANES] for t in range(values.shape[1] // LANES)]


def fold(values):
    return functools.reduce(jnp.add, lane_tiles(values))


def column_sums(values):
    rows, cols = values.shape
    return jnp.sum(values.reshape(rows // 8, 8, cols), axis=0)


def tree(values):
    while len(values) > 1:
        values = [a + b for a, b in zip(values[::2], values[1::2])]
    return values[0]


def nt_dot(a, b):
    return lax.dot_general(a, b, (((1,), (1,)), ((), ())), preferred_element_type=F32)


def groups_of(total):
    return [slice(g * GROUP, (g + 1) * GROUP) for g in range(total // GROUP)]


def unit_kernel(place_ref, t_ref, s_ref, t_unit, s_unit, t_half, s_half):
    half = t_half.shape[0]
    mine = pl.ds(pl.multiple_of(place_ref[2] * half, half), half)
    for raw, unit, part in ((t_ref, t_unit, t_half), (s_ref, s_unit, s_half)):
        unit[...] = unit_rows(raw[...])[0].astype(BF16)
        part[...] = unit[mine, :]


def stats_kernel(t_ref, s_ref, w_ref, out_ref, top, total):
    step = pl.program_id(0)

    @pl.when(step == 0)
    def _():
        top[...] = jnp.full(top.shape, -1e30, F32)
        total[...] = jnp.zeros(total.shape, F32)

    for which, (unit, scale) in enumerate(((t_ref, SCALE_TEACHER), (s_ref, SCALE_STUDENT))):
        logits = jnp.dot(unit[...], w_ref[...], preferred_element_type=F32) * scale
        tiles = lane_tiles(logits)
        old = top[which]
        new = functools.reduce(jnp.maximum, tiles, old)
        sums = total[which] * jnp.exp2(old - new)
        for tile in tiles:
            sums = sums + jnp.exp2(tile - new)
        top[which] = new
        total[which] = sums

    @pl.when(step == pl.num_programs(0) - 1)
    def _():
        quarter = out_ref.shape[0] // 4
        for which in range(2):
            lanes = top[which]
            peak = jnp.max(lanes, axis=1, keepdims=True)
            sums = jnp.sum(total[which] * jnp.exp2(lanes - peak), axis=1, keepdims=True)
            for k, column in enumerate((peak, sums)):
                first = (2 * which + k) * quarter
                pack_rows(out_ref.at[first : first + quarter], column)


def merge_kernel(*refs):
    *stats, out_ref = refs
    out_ref[...] = jnp.zeros(out_ref.shape, F32)
    quarter = stats[0].shape[0] // 4
    for which in range(2):
        first = 2 * which * quarter
        tops = [ref[first : first + quarter, :] for ref in stats]
        top = functools.reduce(jnp.maximum, tops)
        total = tree(
            [
                ref[first + quarter : first + 2 * quarter, :] * jnp.exp2(peak - top)
                for ref, peak in zip(stats, tops)
            ]
        )
        out_ref[which * quarter : (which + 1) * quarter, :] = top + jnp.log2(total)


def gather_units(place_ref, unit, own_ref, mine, other):
    own = own_ref.shape[0]
    half = own // 2
    unit[:own, :] = own_ref[...]
    core = place_ref[2]
    for g, (a, b) in enumerate(zip(mine, other)):
        start = (g + 1) * own
        unit[pl.ds(pl.multiple_of(start + core * half, half), half), :] = a[...]
        unit[pl.ds(pl.multiple_of(start + (1 - core) * half, half), half), :] = b[...]


def spread_logs(lse, logs, which, shift=0.0):
    quarter = lse.shape[0] // (len(logs) * LANES)
    own = quarter * LANES
    for g, ref in enumerate(logs):
        rows = ref[which * quarter : (which + 1) * quarter, :] - shift
        spread_rows(lse.at[g * own : (g + 1) * own], rows)


def probabilities(unit, w_ref, lse, logits, scale, prob_ref, after):
    rows = unit.shape[0]
    count = w_ref.shape[1] // TILE

    def product(n):
        logits[n % 2] = jnp.dot(
            unit[...], w_ref[:, n * TILE : (n + 1) * TILE], preferred_element_type=F32
        )

    product(0)
    for n in range(count):
        if n + 1 < count:
            product(n + 1)
        here = slice(n * TILE, (n + 1) * TILE)
        sums = jnp.zeros((8, TILE), F32)
        for g in groups_of(rows):
            shift = lse[g, :]
            prob = jnp.concatenate(
                [jnp.exp2(tile * scale - shift) for tile in lane_tiles(logits[n % 2, g, :])], axis=1
            )
            if after is not None:
                sums = sums + column_sums(prob)
            prob_ref[g, here] = prob.astype(BF16)
        if after is not None:
            after(here, 1.0 / jnp.sum(sums, axis=0, keepdims=True))


def add_row_sums(rows, prob_ref, here, scale):
    for g in groups_of(rows.shape[0]):
        rows[g, :] += fold(prob_ref[g, here].astype(F32) * scale)


def teacher_kernel(groups, place_ref, own_ref, *refs):
    mine, refs = refs[: groups - 1], refs[groups - 1 :]
    other, refs = refs[: groups - 1], refs[groups - 1 :]
    logs, refs = refs[:groups], refs[groups:]
    w_ref, prob_ref, sums_ref, unit, lse, rows, logits = refs
    step = pl.program_id(0)

    @pl.when(step == 0)
    def _():
        gather_units(place_ref, unit, own_ref, mine, other)
        spread_logs(lse, logs, 0)
        rows[...] = jnp.zeros(rows.shape, F32)

    probabilities(
        unit, w_ref, lse, logits, SCALE_TEACHER, prob_ref,
        lambda here, scale: add_row_sums(rows, prob_ref, here, scale),
    )

    @pl.when(step == pl.num_programs(0) - 1)
    def _():
        pack_rows(sums_ref, jnp.sum(rows[...], axis=1, keepdims=True))


def row_scales(sums, tiles):
    return 1.0 / tree([ref[:tiles, :] for ref in sums])


def sweep(prob_ref, weight, rows, use):
    for n in range(prob_ref.shape[1] // TILE):
        here = slice(n * TILE, (n + 1) * TILE)
        sums = jnp.zeros((8, TILE), F32)
        for g in groups_of(prob_ref.shape[0]):
            shift = weight[g, :]
            tiles = lane_tiles(prob_ref[g, here].astype(F32))
            sums = sums + column_sums(jnp.concatenate([tile * shift for tile in tiles], axis=1))
        scale = 1.0 / jnp.sum(sums, axis=0, keepdims=True)
        add_row_sums(rows, prob_ref, here, scale)
        if use is not None:
            use(here, scale)


def sweep_kernel(parts, prob_ref, *refs):
    sums, (sums_ref, weight, rows) = refs[:parts], refs[parts:]
    step = pl.program_id(0)

    @pl.when(step == 0)
    def _():
        spread_rows(weight, row_scales(sums, sums_ref.shape[0]))
        rows[...] = jnp.zeros(rows.shape, F32)

    sweep(prob_ref, weight, rows, None)

    @pl.when(step == pl.num_programs(0) - 1)
    def _():
        pack_rows(sums_ref, jnp.sum(rows[...], axis=1, keepdims=True))


def split_rows(place_ref, back, outs):
    for s, out in enumerate(outs):
        share = out.shape[0]
        start = jnp.bitwise_xor(place_ref[1], s) * share
        out[...] = back[pl.ds(pl.multiple_of(start, share), share), :].astype(BF16)


def last_sweep_kernel(parts, place_ref, prob_ref, w_ref, s_ref, *refs):
    sums, refs = refs[:parts], refs[parts:]
    sums_ref, scale_ref, *outs = refs[: 2 + parts]
    weight, rows, back, scaled = refs[2 + parts :]
    step = pl.program_id(0)
    total_rows, own = prob_ref.shape[0], back.shape[0]
    tiles = total_rows // LANES

    @pl.when(step == 0)
    def _():
        spread_rows(weight, row_scales(sums, tiles))
        rows[...] = jnp.zeros(rows.shape, F32)
        back[...] = jnp.zeros(back.shape, F32)

    partner = slice(total_rows // 2, total_rows // 2 + own)

    def use(here, scale):
        scale_ref[:, here] = scale
        scaled[:, here] = (prob_ref[partner, here].astype(F32) * scale).astype(BF16)

    sweep(prob_ref, weight, rows, use)
    back[...] += nt_dot(scaled[...], w_ref[...])

    @pl.when(step == pl.num_programs(0) - 1)
    def _():
        sums_ref[...] = jnp.zeros(sums_ref.shape, F32)
        pack_rows(sums_ref.at[:tiles], jnp.sum(rows[...], axis=1, keepdims=True))
        split_rows(place_ref, back, outs)
        inner = jnp.sum(s_ref[...].astype(F32) * back[...], axis=1, keepdims=True)
        pack_rows(sums_ref.at[tiles : tiles + own // LANES], inner)


def student_kernel(parts, groups, log_protos, place_ref, own_ref, *refs):
    mine, refs = refs[: groups - 1], refs[groups - 1 :]
    other, refs = refs[: groups - 1], refs[groups - 1 :]
    logs, refs = refs[:groups], refs[groups:]
    w_ref, grad_ref, feat_ref, *refs = refs
    outs, refs = refs[:parts], refs[parts:]
    unit, turned, lse, prob, back, logits = refs
    step = pl.program_id(0)
    feats, own = feat_ref.shape[0], back.shape[0]

    @pl.when(step == 0)
    def _():
        gather_units(place_ref, unit, own_ref, mine, other)
        for g in groups_of(unit.shape[0]):
            turned[:, g] = jnp.transpose(unit[g, :].astype(F32)).astype(BF16)
        feat_ref[...] = turned[pl.ds(pl.multiple_of(place_ref[0] * feats, feats), feats), :]
        spread_logs(lse, logs, 1, log_protos)
        back[...] = jnp.zeros(back.shape, F32)

    probabilities(unit, w_ref, lse, logits, SCALE_STUDENT, prob, None)
    grad_ref[...] = jnp.dot(feat_ref[...], prob[...], preferred_element_type=F32)
    back[...] += nt_dot(prob[:own, :], w_ref[...])

    @pl.when(step == pl.num_programs(0) - 1)
    def _():
        split_rows(place_ref, back, outs)


def grad_kernel(parts, protos, prob_ref, feat_ref, part_ref, scale_ref, *refs):
    sums, (out_ref, scaled) = refs[:parts], refs[parts:]

    @pl.when(pl.program_id(0) == 0)
    def _():
        tiles = prob_ref.shape[0] // LANES
        rows = row_scales(sums, tiles) * protos
        for a in range(tiles):
            other = (a + tiles // 2) % tiles
            feat = feat_ref[:, other * LANES : (other + 1) * LANES].astype(F32)
            scaled[:, a * LANES : (a + 1) * LANES] = (feat * rows[a : a + 1, :]).astype(BF16)

    paired = jnp.dot(scaled[...], prob_ref[...], preferred_element_type=F32)
    out_ref[...] = (part_ref[...] - paired * scale_ref[...]).astype(BF16)


def loss_part_kernel(parts, tiles, *refs):
    sums, (logs_ref, out_ref) = refs[:parts], refs[parts:]
    quarter = logs_ref.shape[0] // 4
    total = tree([ref[...] for ref in sums])
    first = tiles // 2
    scale = 1.0 / total[first : first + quarter, :]
    inner = total[tiles : tiles + quarter, :]
    log_total = logs_ref[quarter : 2 * quarter, :] / LOG2E
    terms = log_total - scale * inner / TEMP_STUDENT
    out_ref[...] = jnp.broadcast_to(jnp.sum(terms), out_ref.shape)


def rows_kernel(parts, protos, place_ref, s_ref, *refs):
    student, paired, sums = refs[:parts], refs[parts : 2 * parts], refs[2 * parts : 3 * parts]
    out_ref, weight = refs[3 * parts :]
    share, quarter = out_ref.shape[0], weight.shape[0] // LANES
    tiles = sums[0].shape[0] - 8
    scale = 1.0 / tree([ref[tiles // 2 : tiles // 2 + quarter, :] for ref in sums])
    spread_rows(weight, scale)
    mine = pl.ds(pl.multiple_of(place_ref[1] * share, share), share)
    factor = weight[mine, :1] * protos
    total = tree([ref[...].astype(F32) for ref in student])
    total = total - tree([ref[...].astype(F32) for ref in paired]) * factor
    unit, length = unit_rows(s_ref[mine, :])
    out_ref[...] = (total - unit * jnp.sum(unit * total, axis=-1, keepdims=True)) / length


def join_kernel(place_ref, *refs):
    *blocks, out_ref = refs
    for s, ref in enumerate(blocks):
        share = ref.shape[0]
        start = jnp.bitwise_xor(place_ref[1], s) * share
        out_ref[pl.ds(pl.multiple_of(start, share), share), :] = ref[...]


def whole(array):
    rank = len(array.shape)
    return pl.BlockSpec(array.shape, lambda i: (0,) * rank)


def fixed(*shape):
    return pl.BlockSpec(shape, lambda i: (0,) * len(shape))


def columns(rows, cols):
    return pl.BlockSpec((rows, cols), lambda i: (0, i))


SMEM = pl.BlockSpec(memory_space=pltpu.SMEM)
VMEM = pl.BlockSpec(memory_space=pltpu.VMEM)


def params(mib=None):
    if mib is None:
        return pltpu.CompilerParams()
    return pltpu.CompilerParams(
        dimension_semantics=("arbitrary",), vmem_limit_bytes=mib * 2**20
    )


def cost(flops, nbytes, exps=0):
    return pl.CostEstimate(flops=int(flops), bytes_accessed=int(nbytes), transcendentals=int(exps))


def swapped(values, axis):
    n = lax.axis_size(axis)
    return [values[0]] + [
        lax.ppermute(values[s], axis, [(i, i ^ s) for i in range(n)]) for s in range(1, n)
    ]


def following(value, axis):
    n = lax.axis_size(axis)
    return [lax.ppermute(value, axis, [(i, (i - s) % n) for i in range(n)]) for s in range(1, n)]


def gathered(half):
    mine = following(half, "batch")
    pairs = [(i, i ^ 1) for i in range(lax.axis_size("proto"))]
    return mine + [lax.ppermute(part, "proto", pairs) for part in mine]


def local(teacher_feats, student_feats, proto_weight):
    parts, groups = lax.axis_size("proto"), lax.axis_size("batch")
    own, width = teacher_feats.shape
    local_protos = proto_weight.shape[1]
    rows = own * groups
    protos = local_protos * parts
    feats = width // groups
    share = own // parts
    tiles = rows // LANES
    place = jnp.stack(
        [lax.axis_index("batch"), lax.axis_index("proto"), lax.axis_index("proto") % 2]
    ).astype(jnp.int32)
    struct = jax.ShapeDtypeStruct
    spread = pltpu.VMEM((rows, LANES), F32)
    weight_bytes = 2 * width * local_protos
    prob_bytes = 2 * rows * local_protos

    unit = struct((own, width), BF16)
    half = struct((own // 2, width), BF16)
    teacher, student, teacher_half, student_half = pl.pallas_call(
        unit_kernel,
        in_specs=[SMEM, VMEM, VMEM],
        out_shape=[unit, unit, half, half],
        cost_estimate=cost(8 * own * width, 6 * own * width),
        name="unit_rows",
    )(place, teacher_feats, student_feats)
    teacher_all = gathered(teacher_half)
    student_all = gathered(student_half)

    chunk = 1024
    grid = (local_protos // chunk,)
    stats = pl.pallas_call(
        stats_kernel,
        grid=grid,
        in_specs=[whole(teacher), whole(student), columns(width, chunk)],
        out_specs=fixed(4 * own // LANES, LANES),
        out_shape=struct((4 * own // LANES, LANES), F32),
        scratch_shapes=[pltpu.VMEM((2, own, LANES), F32), pltpu.VMEM((2, own, LANES), F32)],
        compiler_params=params(56),
        cost_estimate=cost(4 * own * width * local_protos, weight_bytes),
        name="row_stats",
    )(teacher, student, proto_weight)
    logs = pl.pallas_call(
        merge_kernel, out_shape=struct(stats.shape, F32), name="merge_stats"
    )(*swapped([stats] * parts, "proto"))
    logs_all = [logs] + following(logs, "batch")

    sums_struct = struct((tiles, LANES), F32)
    prob, sums = pl.pallas_call(
        functools.partial(teacher_kernel, groups),
        grid=grid,
        in_specs=[SMEM, whole(teacher)]
        + [whole(x) for x in teacher_all]
        + [whole(x) for x in logs_all]
        + [columns(width, chunk)],
        out_specs=[columns(rows, chunk), fixed(tiles, LANES)],
        out_shape=[struct((rows, local_protos), BF16), sums_struct],
        scratch_shapes=[
            pltpu.VMEM((rows, width), BF16), spread, spread, pltpu.VMEM((2, rows, TILE), F32),
        ],
        compiler_params=params(56),
        cost_estimate=cost(2 * rows * width * local_protos, prob_bytes),
        name="teacher_prob",
    )(place, teacher, *teacher_all, *logs_all, proto_weight)

    block = struct((share, width), BF16)
    grad_part, feat, *back_student = pl.pallas_call(
        functools.partial(student_kernel, parts, groups, math.log2(protos)),
        grid=grid,
        in_specs=[SMEM, whole(student)]
        + [whole(x) for x in student_all]
        + [whole(x) for x in logs_all]
        + [columns(width, chunk)],
        out_specs=[columns(feats, chunk), fixed(feats, rows)] + [fixed(share, width)] * parts,
        out_shape=[struct((feats, local_protos), F32), struct((feats, rows), BF16)]
        + [block] * parts,
        scratch_shapes=[
            pltpu.VMEM((rows, width), BF16),
            pltpu.VMEM((width, rows), BF16),
            spread,
            pltpu.VMEM((rows, chunk), BF16),
            pltpu.VMEM((own, width), F32),
            pltpu.VMEM((2, rows, TILE), F32),
        ],
        compiler_params=params(56),
        cost_estimate=cost(3 * rows * width * local_protos, weight_bytes),
        name="student_side",
    )(place, student, *student_all, *logs_all, proto_weight)
    back_student = swapped(back_student, "proto")

    for _ in range(SWEEPS - 2):
        sums_all = swapped([sums] * parts, "proto")
        sums = pl.pallas_call(
            functools.partial(sweep_kernel, parts),
            grid=grid,
            in_specs=[columns(rows, chunk)] + [whole(x) for x in sums_all],
            out_specs=fixed(tiles, LANES),
            out_shape=sums_struct,
            scratch_shapes=[spread, spread],
            compiler_params=params(56),
            cost_estimate=cost(4 * rows * local_protos, prob_bytes),
            name="sweep",
        )(prob, *sums_all)
    sums_all = swapped([sums] * parts, "proto")
    sums, col_scale, *back_paired = pl.pallas_call(
        functools.partial(last_sweep_kernel, parts),
        grid=grid,
        in_specs=[SMEM, columns(rows, chunk), columns(width, chunk), whole(student)]
        + [whole(x) for x in sums_all],
        out_specs=[fixed(tiles + 8, LANES), columns(1, chunk)] + [fixed(share, width)] * parts,
        out_shape=[struct((tiles + 8, LANES), F32), struct((1, local_protos), F32)]
        + [block] * parts,
        scratch_shapes=[
            spread, spread, pltpu.VMEM((own, width), F32), pltpu.VMEM((own, chunk), BF16),
        ],
        compiler_params=params(56),
        cost_estimate=cost(2 * own * width * local_protos, prob_bytes),
        name="last_sweep",
    )(place, prob, proto_weight, student, *sums_all)
    sums_all = swapped([sums] * parts, "proto")
    back_paired = swapped(back_paired, "proto")

    loss_part = pl.pallas_call(
        functools.partial(loss_part_kernel, parts, tiles),
        out_shape=struct((8, LANES), F32),
        name="loss_part",
    )(*sums_all, logs)
    loss = tree([x[0, 0] for x in swapped([loss_part] * groups, "batch")]) / rows

    grad_rows = pl.pallas_call(
        functools.partial(rows_kernel, parts, float(protos)),
        in_specs=[SMEM] + [VMEM] * (1 + 3 * parts),
        out_shape=struct((share, width), F32),
        scratch_shapes=[pltpu.VMEM((own, LANES), F32)],
        name="row_grads",
    )(place, student_feats, *back_student, *back_paired, *sums_all)
    grad_rows = pl.pallas_call(
        join_kernel,
        in_specs=[SMEM] + [VMEM] * parts,
        out_shape=struct((own, width), F32),
        name="join_rows",
    )(place, *swapped([grad_rows] * parts, "proto"))

    grad_weight = pl.pallas_call(
        functools.partial(grad_kernel, parts, float(protos)),
        grid=grid,
        in_specs=[
            columns(rows, chunk), whole(feat), columns(feats, chunk), columns(1, chunk),
        ]
        + [whole(x) for x in sums_all],
        out_specs=columns(feats, chunk),
        out_shape=struct((feats, local_protos), BF16),
        scratch_shapes=[pltpu.VMEM((feats, rows), BF16)],
        compiler_params=params(56),
        cost_estimate=cost(2 * feats * rows * local_protos, prob_bytes),
        name="weight_grads",
    )(prob, feat, grad_part, col_scale, *sums_all)
    return grad_weight, grad_rows, loss


def solution(mesh):
    return jax.shard_map(
        local,
        mesh=mesh,
        in_specs=(P("batch", None), P("batch", None), P(None, "proto")),
        out_specs=(P("batch", "proto"), P("batch", None), P()),
        check_vma=False,
    )
```

time: 886 us -> 224 us (0.25)
  waiting for transfers between devices: 596 us -> 44.6 us
  blocking collectives: 154 us -> 0 us
  Pallas kernels: 0 us -> 98.9 us
  matrix products: 74.2 us -> 0 us
  starting transfers between devices: 0.15 us -> 65 us
  other arithmetic: 30.4 us -> 0.67 us
  between operations: 17.8 us -> 5.09 us
    ppermute x1 -> x67, waiting for transfers between devices: 362 us -> 44.6 us  [the longest x52 29.5 us: swapped(): lax.ppermute(values[s], axis, [(i, i ^ s) for i in range(n)])]
    reduce_scatter x1 -> x0, waiting for transfers between devices: 234 us -> none  [local(): lax.psum_scatter(lax.dot_general(student_half, dlogits, (((0,), (0,)), ((...]
    psum x8 -> x0, blocking collectives: 139 us -> none  [the longest x3 51.1 us: local(): lax.psum(jnp.dot(row_scale, prob, precision=lax.Precision.HIGHEST).astype...]
    pallas_call x0 -> x11, Pallas kernels: none -> 98.9 us  [the longest x1 19.5 us: local(): pl.pallas_call(functools.partial(teacher_kernel, groups), grid=grid, in_s...]
    dot_general x10 -> x0, matrix products: 74.2 us -> none  [the longest x3 26.7 us: local(): jnp.dot(prob, col_scale, precision=lax.Precision.HIGHEST)]
    ppermute x1 -> x67, starting transfers between devices: 0.07 us -> 65 us  [the longest x52 50.6 us: swapped(): lax.ppermute(values[s], axis, [(i, i ^ s) for i in range(n)])]
    reduce_sum x5 -> x0, other arithmetic: 16 us -> none  [the longest x1 7.12 us: local(): jnp.sum(jnp.exp(student_logits - stud_max[:, None]), axis=1)]
    pmax x1 -> x0, blocking collectives: 15.1 us -> none  [local(): lax.pmax((jnp.max(teacher_logits, axis=1), jnp.max(student_logits, axis=1...]
  transfers between devices with their start and end apart: 3 -> 67, of which waited for: 3 -> 24; matrix products, arithmetic and copies ran while one was open for 2% -> 1% of each run, Pallas kernels for 0% -> 42%
where the time goes in v1:
time: 224 us; the launch traced here: 223 us
  Pallas kernels  98.9 us (44%)
  starting transfers between devices  65 us (29%)
  waiting for transfers between devices  44.6 us (20%)
  local copies, waits for them, and re-layouts  8.74 us (4%)
  between operations  5.09 us (2%)
    ppermute x52, starting transfers between devices, swapped(): lax.ppermute(values[s], axis, [(i, i ^ s) for i in range(n)])  50.6 us
    ppermute x52, waiting for transfers between devices, swapped(): lax.ppermute(values[s], axis, [(i, i ^ s) for i in range(n)])  29.5 us
    pallas_call x1, Pallas kernels, local(): pl.pallas_call(functools.partial(teacher_kernel, groups), grid=grid, in_s...  19.5 us
    pallas_call x1, Pallas kernels, local(): pl.pallas_call(functools.partial(student_kernel, parts, groups, math.log2...  18.7 us
    pallas_call x1, Pallas kernels, local(): pl.pallas_call(functools.partial(last_sweep_kernel, parts), grid=grid, in...  16.3 us
    ppermute x9, waiting for transfers between devices, following(): lax.ppermute(value, axis, [(i, (i - s) % n) for i in range(n)])  15 us
    ppermute x9, starting transfers between devices, following(): lax.ppermute(value, axis, [(i, (i - s) % n) for i in range(n)])  13.1 us
    pallas_call x1, Pallas kernels, local(): pl.pallas_call(functools.partial(sweep_kernel, parts), grid=grid, in_spec...  12.8 us
  transfers between devices with their start and end apart: 67, of which 24 were waited for; matrix products, arithmetic and copies ran while one was open for 1% of the time, Pallas kernels for 42%

profile of v1, /device:TPU:0, one launch (start us, length us, event | category | flops | bytes accessed | tf_op | source)
XLA Modules:
  0.0 223.0 jit_solution(1649976054836276771)
XLA Ops:
  1.3 2.1 unit_rows.1
  3.4 5.0 %collective-permute-start = (bf16[128,512]{1,0:T(8,128)(2,1)}, bf16[128,512]{1,0:T(8,128)(2,1)S(1)}, u32[]{:S(2)}, u32[]{:S(2)}) collective-permute-start(bf16[128,512]{1,0:T(8,128)(2,1)} %get-tuple-element.30), channel_id=1, source_target_pairs={{0,3},{1,0},{2,1},{3,2},{4,7},{5,4},{6,5},{7,6},{8,11},{9,8},{10,9... | collective-permute-start | bytes 393224 | tf_op jit(solution)/shard_map/ppermute | solution.py:404
  9.4 3.2 %collective-permute-done.refs_0_ = bf16[128,512]{1,0:T(8,128)(2,1)S(1)} collective-permute-done((bf16[128,512]{1,0:T(8,128)(2,1)}, bf16[128,512]{1,0:T(8,128)(2,1)S(1)}, u32[]{:S(2)}, u32[]{:S(2)}) %collective-permute-start) | collective-permute-done | bytes 131104 | tf_op jit(solution)/shard_map/ppermute | solution.py:404
  12.7 7.2 %collective-permute-done.1.refs_1_ = bf16[128,512]{1,0:T(8,128)(2,1)S(1)} collective-permute-done((bf16[128,512]{1,0:T(8,128)(2,1)}, bf16[128,512]{1,0:T(8,128)(2,1)S(1)}, u32[]{:S(2)}, u32[]{:S(2)}) %collective-permute-start.1) | collective-permute-done | bytes 131104 | tf_op jit(solution)/shard_map/ppermute | solution.py:404
  20.4 11.0 %row_stats.1.refs_0_ = f32[8,128]{1,0:T(8,128)} custom-call(bf16[256,512]{1,0:T(8,128)(2,1)} %get-tuple-element.29.t_ref.own_ref, bf16[256,512]{1,0:T(8,128)(2,1)} %get-tuple-element.31.s_ref.own_ref, bf16[512,8192]{1,0:T(8,128)(2,1)} %w_ref.3), custom_call_target="tpu_custom_call" | custom-call | flops 4294967296 | bytes 8388608 | tf_op jit(solution)/shard_map/row_stats/pallas_call | solution.py:444
  34.7 2.2 collective-permute-start.12
  40.3 2.3 %collective-permute-done.7.refs_2_ = f32[8,128]{1,0:T(8,128)S(1)} collective-permute-done((f32[8,128]{1,0:T(8,128)}, f32[8,128]{1,0:T(8,128)S(1)}, u32[]{:S(2)}, u32[]{:S(2)}) %collective-permute-start.7) | collective-permute-done | bytes 4128 | tf_op jit(solution)/shard_map/ppermute | solution.py:398
  44.1 2.3 %collective-permute-done.9.refs_4_ = f32[8,128]{1,0:T(8,128)S(1)} collective-permute-done((f32[8,128]{1,0:T(8,128)}, f32[8,128]{1,0:T(8,128)S(1)}, u32[]{:S(2)}, u32[]{:S(2)}) %collective-permute-start.9) | collective-permute-done | bytes 4128 | tf_op jit(solution)/shard_map/ppermute | solution.py:398
  57.9 2.1 collective-permute-start.17
  61.4 19.5 %teacher_prob.1 = (bf16[1024,8192]{1,0:T(8,128)(2,1)}, f32[8,128]{1,0:T(8,128)}) custom-call(s32[3]{0:T(128)} %pad_add_fusion.place_ref, bf16[256,512]{1,0:T(8,128)(2,1)} %get-tuple-element.29.t_ref.own_ref, bf16[128,512]{1,0:T(8,128)(2,1)} %copy-done.54, bf16[128,512]{1,0:T(8,128)(2,1)} %copy-done.55, bf16[128,512]{1,0:T(8,128)(2,1)} %copy-done.56, ...), custom_call_target="tpu_custom_call" | custom-call | flops 8589934592 | bytes 16777216 | tf_op jit(solution)/shard_map/teacher_prob/pallas_call | solution.py:461
  88.7 2.4 %collective-permute-start.27 = (f32[8,128]{1,0:T(8,128)}, f32[8,128]{1,0:T(8,128)S(1)}, u32[]{:S(2)}, u32[]{:S(2)}) collective-permute-start(f32[8,128]{1,0:T(8,128)} %get-tuple-element.36.refs_0_), channel_id=1, source_target_pairs={{0,24},{4,28},{8,16},{12,20},{16,8},{20,12},{24,0},{28,4},{1,25},{... | collective-permute-start | bytes 12296 | tf_op jit(solution)/shard_map/ppermute | solution.py:398
  91.1 2.3 %collective-permute-done.27.refs_6_ = f32[8,128]{1,0:T(8,128)S(1)} collective-permute-done((f32[8,128]{1,0:T(8,128)}, f32[8,128]{1,0:T(8,128)S(1)}, u32[]{:S(2)}, u32[]{:S(2)}) %collective-permute-start.27) | collective-permute-done | bytes 4128 | tf_op jit(solution)/shard_map/ppermute | solution.py:398
  95.9 12.8 %sweep.1.refs_0_ = f32[8,128]{1,0:T(8,128)} custom-call(bf16[1024,8192]{1,0:T(8,128)(2,1)} %get-tuple-element.32.prob_ref, f32[8,128]{1,0:T(8,128)} %get-tuple-element.36.refs_0_, f32[8,128]{1,0:T(8,128)} %copy-done.29, f32[8,128]{1,0:T(8,128)} %copy-done.30, f32[8,128]{1,0:T(8,128)} %copy-done.31, f32[8,128]{1,0:T(8,128)} %copy-done.32, ...), custom_call_target="tpu_custom_call" | custom-call | flops 33554432 | bytes 16777216 | tf_op jit(solution)/shard_map/sweep/pallas_call | solution.py:505
  112.9 2.1 collective-permute-start.35
  118.1 16.3 %last_sweep.1 = (f32[16,128]{1,0:T(8,128)}, f32[1,8192]{1,0:T(1,128)}, bf16[32,512]{1,0:T(8,128)(2,1)}, bf16[32,512]{1,0:T(8,128)(2,1)}, bf16[32,512]{1,0:T(8,12...) custom-call(s32[3]{0:T(128)} %pad_add_fusion.place_ref, ...), custom_call_target="tpu_custom_call" | custom-call | flops 2147483648 | bytes 16777216 | tf_op jit(solution)/shard_map/last_sweep/pallas_call | solution.py:517
  138.0 18.7 %student_side.1 = (f32[128,8192]{1,0:T(8,128)}, bf16[128,1024]{1,0:T(8,128)(2,1)}, bf16[32,512]{1,0:T(8,128)(2,1)}, bf16[32,512]{1,0:T(8,128)(2,1)}, bf16[32,512...) custom-call(s32[3]{0:T(128)} %pad_add_fusion.place_ref, ...), custom_call_target="tpu_custom_call" | custom-call | flops 12884901888 | bytes 8388608 | tf_op jit(solution)/shard_map/student_side/pallas_call | solution.py:479
  160.6 2.4 %collective-permute-done.40.refs_5_.refs_21_ = f32[16,128]{1,0:T(8,128)S(1)} collective-permute-done((f32[16,128]{1,0:T(8,128)S(1)}, f32[16,128]{1,0:T(8,128)S(1)}, u32[]{:S(2)}, u32[]{:S(2)}) %collective-permute-start.40) | collective-permute-done | bytes 8224 | tf_op jit(solution)/shard_map/ppermute | solution.py:398
  164.8 2.8 %collective-permute-done.41.refs_6_.refs_22_ = f32[16,128]{1,0:T(8,128)S(1)} collective-permute-done((f32[16,128]{1,0:T(8,128)S(1)}, f32[16,128]{1,0:T(8,128)S(1)}, u32[]{:S(2)}, u32[]{:S(2)}) %collective-permute-start.41) | collective-permute-done | bytes 8224 | tf_op jit(solution)/shard_map/ppermute | solution.py:398
  168.0 3.5 %collective-permute-done.42.refs_7_.refs_23_ = f32[16,128]{1,0:T(8,128)S(1)} collective-permute-done((f32[16,128]{1,0:T(8,128)S(1)}, f32[16,128]{1,0:T(8,128)S(1)}, u32[]{:S(2)}, u32[]{:S(2)}) %collective-permute-start.42) | collective-permute-done | bytes 8224 | tf_op jit(solution)/shard_map/ppermute | solution.py:398
  181.6 2.8 %collective-permute-done.55.refs_14_ = bf16[32,512]{1,0:T(8,128)(2,1)S(1)} collective-permute-done((bf16[32,512]{1,0:T(8,128)(2,1)S(1)}, bf16[32,512]{1,0:T(8,128)(2,1)S(1)}, u32[]{:S(2)}, u32[]{:S(2)}) %collective-permute-start.55) | collective-permute-done | bytes 32800 | tf_op jit(solution)/shard_map/ppermute | solution.py:398
  185.4 2.1 row_grads.1.refs_0_
  191.1 3.0 %collective-permute-start.66 = (f32[8,128]{1,0:T(8,128)}, f32[8,128]{1,0:T(8,128)S(1)}, u32[]{:S(2)}, u32[]{:S(2)}) collective-permute-start(f32[8,128]{1,0:T(8,128)} %loss_part.1), channel_id=1, source_target_pairs={{0,3},{1,2},{2,1},{3,0},{4,7},{5,6},{6,5},{7,4},{8,11},{9,10},{10,... | collective-permute-start | bytes 12296 | tf_op jit(solution)/shard_map/ppermute | solution.py:398
  199.4 2.1 collective-permute-start.63
  201.6 11.6 %weight_grads.1 = bf16[128,8192]{1,0:T(8,128)(2,1)} custom-call(bf16[1024,8192]{1,0:T(8,128)(2,1)} %get-tuple-element.32.prob_ref, bf16[128,1024]{1,0:T(8,128)(2,1)} %get-tuple-element.34.feat_ref, f32[128,8192]{1,0:T(8,128)} %get-tuple-element.35.part_ref, f32[1,8192]{1,0:T(1,128)} %get-tuple-element.37.scale_ref, ...), custom_call_target="tpu_custom_call" | custom-call | flops 2147483648 | bytes 16777216 | tf_op jit(solution)/shard_map/weight_grads/pallas_call | solution.py:556
  (272 shorter events, 76.2 us)
Async XLA Ops:
  8.4 11.4 %collective-permute-start.2 = (bf16[128,512]{1,0:T(8,128)(2,1)}, bf16[128,512]{1,0:T(8,128)(2,1)S(1)}, u32[]{:S(2)}, u32[]{:S(2)}) collective-permute-start(bf16[128,512]{1,0:T(8,128)(2,1)} %get-tuple-element.30), channel_id=1, source_target_pairs={{0,1},{1,2},{2,3},{3,0},{4,5},{5,6},{6,7},{7,4},{8,9},{9,10},{10,1... | collective-permute-start | bytes 393224 | tf_op jit(solution)/shard_map/ppermute | solution.py:404
  12.7 47.3 %collective-permute-start.3 = (bf16[128,512]{1,0:T(8,128)(2,1)S(1)}, bf16[128,512]{1,0:T(8,128)(2,1)S(1)}, u32[]{:S(2)}, u32[]{:S(2)}) collective-permute-start(bf16[128,512]{1,0:T(8,128)(2,1)S(1)} %collective-permute-done.refs_0_), channel_id=1, source_target_pairs={{0,4},{4,0},{8,12},{12,8},{16,20},{20,16},{24,28},{28,24},{1,5},{5... | collective-permute-start | bytes 393224 | tf_op jit(solution)/shard_map/ppermute | solution.py:410
  19.8 40.3 %collective-permute-start.4 = (bf16[128,512]{1,0:T(8,128)(2,1)S(1)}, bf16[128,512]{1,0:T(8,128)(2,1)S(1)}, u32[]{:S(2)}, u32[]{:S(2)}) collective-permute-start(bf16[128,512]{1,0:T(8,128)(2,1)S(1)} %collective-permute-done.1.refs_1_), channel_id=1, source_target_pairs={{0,4},{4,0},{8,12},{12,8},{16,20},{20,16},{24,28},{28,24},{1,5},{5... | collective-permute-start | bytes 393224 | tf_op jit(solution)/shard_map/ppermute | solution.py:410
  19.9 40.3 %collective-permute-start.5 = (bf16[128,512]{1,0:T(8,128)(2,1)S(1)}, bf16[128,512]{1,0:T(8,128)(2,1)S(1)}, u32[]{:S(2)}, u32[]{:S(2)}) collective-permute-start(bf16[128,512]{1,0:T(8,128)(2,1)S(1)} %collective-permute-done.2.refs_2_), channel_id=1, source_target_pairs={{0,4},{4,0},{8,12},{12,8},{16,20},{20,16},{24,28},{28,24},{1,5},{5... | collective-permute-start | bytes 393224 | tf_op jit(solution)/shard_map/ppermute | solution.py:410
  54.9 54.4 %collective-permute-start.16 = (bf16[128,512]{1,0:T(8,128)(2,1)S(1)}, bf16[128,512]{1,0:T(8,128)(2,1)S(1)}, u32[]{:S(2)}, u32[]{:S(2)}) collective-permute-start(bf16[128,512]{1,0:T(8,128)(2,1)S(1)} %copy-done.50), channel_id=1, source_target_pairs={{0,3},{1,0},{2,1},{3,2},{4,7},{5,4},{6,5},{7,6},{8,11},{9,8},{10,9... | collective-permute-start | bytes 393224 | tf_op jit(solution)/shard_map/ppermute | solution.py:404
  57.9 52.7 %collective-permute-start.17 = (bf16[128,512]{1,0:T(8,128)(2,1)S(1)}, bf16[128,512]{1,0:T(8,128)(2,1)S(1)}, u32[]{:S(2)}, u32[]{:S(2)}) collective-permute-start(bf16[128,512]{1,0:T(8,128)(2,1)S(1)} %copy-done.50), channel_id=1, source_target_pairs={{0,2},{1,3},{2,0},{3,1},{4,6},{5,7},{6,4},{7,5},{8,10},{9,11},{10,... | collective-permute-start | bytes 393224 | tf_op jit(solution)/shard_map/ppermute | solution.py:404
  60.0 51.1 %collective-permute-start.18 = (bf16[128,512]{1,0:T(8,128)(2,1)S(1)}, bf16[128,512]{1,0:T(8,128)(2,1)S(1)}, u32[]{:S(2)}, u32[]{:S(2)}) collective-permute-start(bf16[128,512]{1,0:T(8,128)(2,1)S(1)} %copy-done.50), channel_id=1, source_target_pairs={{0,1},{1,2},{2,3},{3,0},{4,5},{5,6},{6,7},{7,4},{8,9},{9,10},{10,1... | collective-permute-start | bytes 393224 | tf_op jit(solution)/shard_map/ppermute | solution.py:404
  115.0 20.7 %collective-permute-start.19 = (bf16[128,512]{1,0:T(8,128)(2,1)S(1)}, bf16[128,512]{1,0:T(8,128)(2,1)S(1)}, u32[]{:S(2)}, u32[]{:S(2)}) collective-permute-start(bf16[128,512]{1,0:T(8,128)(2,1)S(1)} %collective-permute-done.16.refs_0_), channel_id=1, source_target_pairs={{0,4},{4,0},{8,12},{12,8},{16,20},{20,16},{24,28},{28,24},{1,5},{5... | collective-permute-start | bytes 393224 | tf_op jit(solution)/shard_map/ppermute | solution.py:410
  115.3 21.2 %collective-permute-start.20 = (bf16[128,512]{1,0:T(8,128)(2,1)S(1)}, bf16[128,512]{1,0:T(8,128)(2,1)S(1)}, u32[]{:S(2)}, u32[]{:S(2)}) collective-permute-start(bf16[128,512]{1,0:T(8,128)(2,1)S(1)} %collective-permute-done.17.refs_1_), channel_id=1, source_target_pairs={{0,4},{4,0},{8,12},{12,8},{16,20},{20,16},{24,28},{28,24},{1,5},{5... | collective-permute-start | bytes 393224 | tf_op jit(solution)/shard_map/ppermute | solution.py:410
  115.5 21.8 %collective-permute-start.21 = (bf16[128,512]{1,0:T(8,128)(2,1)S(1)}, bf16[128,512]{1,0:T(8,128)(2,1)S(1)}, u32[]{:S(2)}, u32[]{:S(2)}) collective-permute-start(bf16[128,512]{1,0:T(8,128)(2,1)S(1)} %collective-permute-done.18.refs_2_), channel_id=1, source_target_pairs={{0,4},{4,0},{8,12},{12,8},{16,20},{20,16},{24,28},{28,24},{1,5},{5... | collective-permute-start | bytes 393224 | tf_op jit(solution)/shard_map/ppermute | solution.py:410
  134.5 22.5 %collective-permute-start.36 = (f32[16,128]{1,0:T(8,128)}, f32[16,128]{1,0:T(8,128)S(1)}, u32[]{:S(2)}, u32[]{:S(2)}) collective-permute-start(f32[16,128]{1,0:T(8,128)} %get-tuple-element.38.refs_0_.refs_16_), channel_id=1, source_target_pairs={{0,4},{4,0},{8,12},{12,8},{16,20},{20,16},{24,28},{28,24},{1,5},{5... | collective-permute-start | bytes 24584 | tf_op jit(solution)/shard_map/ppermute | solution.py:398
  134.6 24.0 %collective-permute-start.37 = (f32[16,128]{1,0:T(8,128)}, f32[16,128]{1,0:T(8,128)S(1)}, u32[]{:S(2)}, u32[]{:S(2)}) collective-permute-start(f32[16,128]{1,0:T(8,128)} %get-tuple-element.38.refs_0_.refs_16_), channel_id=1, source_target_pairs={{0,8},{4,12},{8,0},{12,4},{16,24},{20,28},{24,16},{28,20},{1,9},{5... | collective-permute-start | bytes 24584 | tf_op jit(solution)/shard_map/ppermute | solution.py:398
  135.6 23.0 %collective-permute-start.38 = (f32[16,128]{1,0:T(8,128)}, f32[16,128]{1,0:T(8,128)S(1)}, u32[]{:S(2)}, u32[]{:S(2)}) collective-permute-start(f32[16,128]{1,0:T(8,128)} %get-tuple-element.38.refs_0_.refs_16_), channel_id=1, source_target_pairs={{0,12},{4,8},{8,4},{12,0},{16,28},{20,24},{24,20},{28,16},{1,13},{... | collective-permute-start | bytes 24584 | tf_op jit(solution)/shard_map/ppermute | solution.py:398
  136.4 23.4 %collective-permute-start.39 = (f32[16,128]{1,0:T(8,128)}, f32[16,128]{1,0:T(8,128)S(1)}, u32[]{:S(2)}, u32[]{:S(2)}) collective-permute-start(f32[16,128]{1,0:T(8,128)} %get-tuple-element.38.refs_0_.refs_16_), channel_id=1, source_target_pairs={{0,16},{4,20},{8,24},{12,28},{16,0},{20,4},{24,8},{28,12},{1,17},{... | collective-permute-start | bytes 24584 | tf_op jit(solution)/shard_map/ppermute | solution.py:398
  156.7 14.8 %collective-permute-start.43 = (bf16[32,512]{1,0:T(8,128)(2,1)}, bf16[32,512]{1,0:T(8,128)(2,1)S(1)}, u32[]{:S(2)}, u32[]{:S(2)}) collective-permute-start(bf16[32,512]{1,0:T(8,128)(2,1)} %get-tuple-element.40), channel_id=1, source_target_pairs={{0,4},{4,0},{8,12},{12,8},{16,20},{20,16},{24,28},{28,24},{1,5},{5... | collective-permute-start | bytes 98312 | tf_op jit(solution)/shard_map/ppermute | solution.py:398
  157.0 16.4 %collective-permute-start.44 = (bf16[32,512]{1,0:T(8,128)(2,1)}, bf16[32,512]{1,0:T(8,128)(2,1)S(1)}, u32[]{:S(2)}, u32[]{:S(2)}) collective-permute-start(bf16[32,512]{1,0:T(8,128)(2,1)} %get-tuple-element.41), channel_id=1, source_target_pairs={{0,8},{4,12},{8,0},{12,4},{16,24},{20,28},{24,16},{28,20},{1,9},{5... | collective-permute-start | bytes 98312 | tf_op jit(solution)/shard_map/ppermute | solution.py:398
  158.5 16.3 %collective-permute-start.45 = (bf16[32,512]{1,0:T(8,128)(2,1)}, bf16[32,512]{1,0:T(8,128)(2,1)S(1)}, u32[]{:S(2)}, u32[]{:S(2)}) collective-permute-start(bf16[32,512]{1,0:T(8,128)(2,1)} %get-tuple-element.42), channel_id=1, source_target_pairs={{0,12},{4,8},{8,4},{12,0},{16,28},{20,24},{24,20},{28,16},{1,13},{... | collective-permute-start | bytes 98312 | tf_op jit(solution)/shard_map/ppermute | solution.py:398
  158.7 16.3 %collective-permute-start.46 = (bf16[32,512]{1,0:T(8,128)(2,1)}, bf16[32,512]{1,0:T(8,128)(2,1)S(1)}, u32[]{:S(2)}, u32[]{:S(2)}) collective-permute-start(bf16[32,512]{1,0:T(8,128)(2,1)} %get-tuple-element.43), channel_id=1, source_target_pairs={{0,16},{4,20},{8,24},{12,28},{16,0},{20,4},{24,8},{28,12},{1,17},{... | collective-permute-start | bytes 98312 | tf_op jit(solution)/shard_map/ppermute | solution.py:398
  187.6 11.8 %collective-permute-start.58 = (f32[32,512]{1,0:T(8,128)}, f32[32,512]{1,0:T(8,128)S(1)}, u32[]{:S(2)}, u32[]{:S(2)}) collective-permute-start(f32[32,512]{1,0:T(8,128)} %row_grads.1.refs_0_), channel_id=1, source_target_pairs={{0,8},{4,12},{8,0},{12,4},{16,24},{20,28},{24,16},{28,20},{1,9},{5... | collective-permute-start | bytes 196616 | tf_op jit(solution)/shard_map/ppermute | solution.py:398
  195.0 23.6 %collective-permute-start.59 = (f32[32,512]{1,0:T(8,128)}, f32[32,512]{1,0:T(8,128)S(1)}, u32[]{:S(2)}, u32[]{:S(2)}) collective-permute-start(f32[32,512]{1,0:T(8,128)} %row_grads.1.refs_0_), channel_id=1, source_target_pairs={{0,12},{4,8},{8,4},{12,0},{16,28},{20,24},{24,20},{28,16},{1,13},{... | collective-permute-start | bytes 196616 | tf_op jit(solution)/shard_map/ppermute | solution.py:398
  196.7 21.9 %collective-permute-start.60 = (f32[32,512]{1,0:T(8,128)}, f32[32,512]{1,0:T(8,128)S(1)}, u32[]{:S(2)}, u32[]{:S(2)}) collective-permute-start(f32[32,512]{1,0:T(8,128)} %row_grads.1.refs_0_), channel_id=1, source_target_pairs={{0,16},{4,20},{8,24},{12,28},{16,0},{20,4},{24,8},{28,12},{1,17},{... | collective-permute-start | bytes 196616 | tf_op jit(solution)/shard_map/ppermute | solution.py:398
  198.0 20.6 %collective-permute-start.61 = (f32[32,512]{1,0:T(8,128)}, f32[32,512]{1,0:T(8,128)S(1)}, u32[]{:S(2)}, u32[]{:S(2)}) collective-permute-start(f32[32,512]{1,0:T(8,128)} %row_grads.1.refs_0_), channel_id=1, source_target_pairs={{0,20},{4,16},{8,28},{12,24},{16,4},{20,0},{24,12},{28,8},{1,21},{... | collective-permute-start | bytes 196616 | tf_op jit(solution)/shard_map/ppermute | solution.py:398
  198.1 20.6 %collective-permute-start.62 = (f32[32,512]{1,0:T(8,128)}, f32[32,512]{1,0:T(8,128)S(1)}, u32[]{:S(2)}, u32[]{:S(2)}) collective-permute-start(f32[32,512]{1,0:T(8,128)} %row_grads.1.refs_0_), channel_id=1, source_target_pairs={{0,24},{4,28},{8,16},{12,20},{16,8},{20,12},{24,0},{28,4},{1,25},{... | collective-permute-start | bytes 196616 | tf_op jit(solution)/shard_map/ppermute | solution.py:398
  199.4 19.3 %collective-permute-start.63 = (f32[32,512]{1,0:T(8,128)}, f32[32,512]{1,0:T(8,128)S(1)}, u32[]{:S(2)}, u32[]{:S(2)}) collective-permute-start(f32[32,512]{1,0:T(8,128)} %row_grads.1.refs_0_), channel_id=1, source_target_pairs={{0,28},{4,24},{8,20},{12,16},{16,12},{20,8},{24,4},{28,0},{1,29},{... | collective-permute-start | bytes 196616 | tf_op jit(solution)/shard_map/ppermute | solution.py:398
  (116 other events, 1191.9 us)

commit v2 on v0

v2 whole, which is shorter than its diff:
```python
import functools
import math

import jax
import jax.numpy as jnp
from jax import lax
from jax.experimental import pallas as pl
from jax.experimental.pallas import tpu as pltpu
from jax.sharding import PartitionSpec as P

SWEEPS = 3
TEMP_TEACHER = 0.04
TEMP_STUDENT = 0.1
LOG2E = math.log2(math.e)
SCALE_TEACHER = LOG2E / TEMP_TEACHER
SCALE_STUDENT = LOG2E / TEMP_STUDENT
LANES = 128
WIDE = 1024
F32 = jnp.float32
BF16 = jnp.bfloat16


def unit_rows(values):
    wide = values.astype(F32)
    length = jnp.sqrt(jnp.sum(wide * wide, axis=-1, keepdims=True) + 1e-06)
    return wide / length, length


def diagonal():
    shape = (LANES, LANES)
    return lax.broadcasted_iota(jnp.int32, shape, 0) == lax.broadcasted_iota(jnp.int32, shape, 1)


def to_column(row):
    spread = jnp.where(diagonal(), jnp.broadcast_to(row, (LANES, LANES)), 0.0)
    return jnp.sum(spread, axis=1, keepdims=True)


def to_row(column):
    spread = jnp.where(diagonal(), jnp.broadcast_to(column, (LANES, LANES)), 0.0)
    return jnp.sum(spread, axis=0, keepdims=True)


def spread_rows(ref, rows):
    for a in range(rows.shape[0]):
        ref[a * LANES : (a + 1) * LANES, :] = jnp.broadcast_to(
            to_column(rows[a : a + 1, :]), (LANES, LANES)
        )


def pack_rows(ref, columns):
    for a in range(columns.shape[0] // LANES):
        ref[a : a + 1, :] = to_row(columns[a * LANES : (a + 1) * LANES, :])


def lane_tiles(values):
    return [values[:, t * LANES : (t + 1) * LANES] for t in range(values.shape[1] // LANES)]


def fold(values):
    return functools.reduce(jnp.add, lane_tiles(values))


def column_sums(values):
    rows, cols = values.shape
    return jnp.sum(values.reshape(rows // 8, 8, cols), axis=0)


def nt_dot(a, b):
    return lax.dot_general(a, b, (((1,), (1,)), ((), ())), preferred_element_type=F32)


def add_up(values):
    return functools.reduce(jnp.add, values)


def stats_kernel(t_ref, s_ref, w_ref, t_exp, s_exp, out_ref, unit, logits, top, total):
    chunk = 512
    cols = w_ref.shape[1]
    pieces = [slice(c, c + chunk) for c in range(0, cols, chunk)]
    quarter = out_ref.shape[1] // 4
    outs = (t_exp, s_exp)
    scales = (SCALE_TEACHER, SCALE_STUDENT)
    for which, ref in enumerate((t_ref, s_ref)):
        unit[which] = unit_rows(ref[...])[0].astype(BF16)
    top[...] = jnp.full(top.shape, -1e30, F32)
    total[...] = jnp.zeros(total.shape, F32)

    def product(which, here):
        values = jnp.dot(unit[which], w_ref[:, here], preferred_element_type=F32) * scales[which]
        logits[which, :, here] = values
        top[which] = functools.reduce(jnp.maximum, lane_tiles(values), top[which])

    def peak(which):
        return jnp.max(top[which], axis=1, keepdims=True)

    def raised(which, here, shift):
        values = jnp.exp2(logits[which, :, here] - shift)
        outs[which][:, here] = values.astype(BF16)
        total[which] += fold(values)

    for here in pieces:
        product(0, here)
    peaks = [peak(0)]
    shift = jnp.broadcast_to(peaks[0], (peaks[0].shape[0], chunk))
    for here in pieces:
        product(1, here)
        raised(0, here, shift)
    peaks.append(peak(1))
    shift = jnp.broadcast_to(peaks[1], (peaks[1].shape[0], chunk))
    for here in pieces:
        raised(1, here, shift)
    for which in range(2):
        sums = jnp.sum(total[which], axis=1, keepdims=True)
        for k, column in enumerate((peaks[which], sums)):
            first = (2 * which + k) * quarter
            pack_rows(out_ref.at[0, first : first + quarter], column)
    for p in range(1, out_ref.shape[0]):
        out_ref[p] = out_ref[0]


def merged(stats_ref, which):
    parts, height, _ = stats_ref.shape
    quarter = height // 4
    first = 2 * which * quarter
    tops = [stats_ref[p, first : first + quarter, :] for p in range(parts)]
    top = functools.reduce(jnp.maximum, tops)
    sums = [
        stats_ref[p, first + quarter : first + 2 * quarter, :] * jnp.exp2(tops[p] - top)
        for p in range(parts)
    ]
    return top + jnp.log2(add_up(sums))


def column_pass(exp_ref, weight, out_ref):
    rows, cols = exp_ref.shape
    for a in range(cols // WIDE):
        sums = jnp.zeros((8, WIDE), F32)
        for g in range(0, rows, 16):
            shift = weight[g : g + 16, :]
            tiles = lane_tiles(exp_ref[g : g + 16, a * WIDE : (a + 1) * WIDE].astype(F32))
            sums = sums + column_sums(jnp.concatenate([tile * shift for tile in tiles], axis=1))
        out_ref[0, a : a + 1, :] = jnp.sum(sums, axis=0, keepdims=True)


def repeat(out_ref):
    for p in range(1, out_ref.shape[0]):
        out_ref[p] = out_ref[0]


def first_column_kernel(place_ref, stats_ref, exp_ref, factor_ref, out_ref, weight):
    height = stats_ref.shape[1]
    quarter = height // 4
    parts_rows = exp_ref.shape[1] // WIDE
    own = stats_ref[pl.ds(place_ref[1], 1)][0]
    factor_ref[...] = jnp.zeros(factor_ref.shape, F32)
    out_ref[0, parts_rows:, :] = jnp.zeros((out_ref.shape[1] - parts_rows, WIDE), F32)
    for which in range(2):
        log_sum = merged(stats_ref, which)
        factor_ref[which * quarter : (which + 1) * quarter, :] = jnp.exp2(
            own[2 * which * quarter : (2 * which + 1) * quarter, :] - log_sum
        )
        for a in range(quarter):
            lanes = slice((which * quarter + a) * LANES, (which * quarter + a + 1) * LANES)
            out_ref[0, parts_rows : parts_rows + 1, lanes] = log_sum[a : a + 1, :]
    spread_rows(weight, factor_ref[:quarter, :])
    column_pass(exp_ref, weight, out_ref)
    repeat(out_ref)


def column_kernel(sums_ref, factor_ref, exp_ref, out_ref, weight):
    parts = sums_ref.shape[0]
    quarter = exp_ref.shape[0] // LANES
    scale = 1.0 / add_up([sums_ref[p, :quarter, :] for p in range(parts)])
    spread_rows(weight, scale * factor_ref[:quarter, :])
    column_pass(exp_ref, weight, out_ref)
    repeat(out_ref)


def column_scales(cols_ref, height):
    return 1.0 / add_up([cols_ref[g, :height, :] for g in range(cols_ref.shape[0])])


def row_kernel(cols_ref, factor_ref, exp_ref, out_ref, scales):
    rows, cols = exp_ref.shape
    quarter = rows // LANES
    scales[...] = column_scales(cols_ref, cols // WIDE)
    out_ref[0] = jnp.zeros(out_ref.shape[1:], F32)
    for q in range(quarter):
        sums = []
        for g in range(q * LANES, (q + 1) * LANES, 32):
            total = jnp.zeros((32, LANES), F32)
            for a in range(cols // WIDE):
                tiles = lane_tiles(exp_ref[g : g + 32, a * WIDE : (a + 1) * WIDE].astype(F32))
                for t, tile in enumerate(tiles):
                    total = total + tile * scales[a : a + 1, t * LANES : (t + 1) * LANES]
            sums.append(jnp.sum(total, axis=1, keepdims=True))
        row = to_row(jnp.concatenate(sums, axis=0))
        out_ref[0, q : q + 1, :] = row * factor_ref[q : q + 1, :]
    repeat(out_ref)


def relative_units(place_ref, all_ref, unit, groups, first):
    own = all_ref.shape[0] // groups
    for g in range(first, groups):
        start = lax.rem(place_ref[0] + g, groups) * own
        raw = all_ref[pl.ds(pl.multiple_of(start, own), own), :]
        unit[(g - first) * own : (g - first + 1) * own, :] = unit_rows(raw)[0].astype(BF16)


def relative_logs(place_ref, cols_ref, lse, which, height, shift=0.0):
    groups = cols_ref.shape[0]
    own = lse.shape[0] // (groups - 1)
    quarter = own // LANES
    for g in range(1, groups):
        there = cols_ref[pl.ds(lax.rem(place_ref[0] + g, groups), 1)][0]
        for a in range(quarter):
            first = (which * quarter + a) * LANES
            row = there[height : height + 1, first : first + LANES] - shift
            start = ((g - 1) * quarter + a) * LANES
            lse[start : start + LANES, :] = jnp.broadcast_to(to_column(row), (LANES, LANES))


def probabilities(unit, w_ref, lse, scale, prob_ref):
    for n in range(0, w_ref.shape[1], 256):
        logits = jnp.dot(unit[...], w_ref[:, n : n + 256], preferred_element_type=F32)
        for k, tile in enumerate(lane_tiles(logits)):
            lanes = slice(n + k * LANES, n + (k + 1) * LANES)
            prob_ref[:, lanes] = jnp.exp2(tile * scale - lse[...]).astype(BF16)


def others_kernel(groups, height, place_ref, all_ref, cols_ref, w_ref, prob_ref, unit, lse):
    @pl.when(pl.program_id(0) == 0)
    def _():
        relative_units(place_ref, all_ref, unit, groups, 1)
        relative_logs(place_ref, cols_ref, lse, 0, height)

    probabilities(unit, w_ref, lse, SCALE_TEACHER, prob_ref)


def student_kernel(
    groups, height, log_protos, place_ref, all_ref, cols_ref, factor_ref, w_ref, exp_ref,
    grad_ref, feat_ref, back_ref, unit, turned, scaled, lse, prob, back,
):
    step = pl.program_id(0)
    feats, own = feat_ref.shape[0], back.shape[0]
    quarter = own // LANES
    protos = 2.0**log_protos

    @pl.when(step == 0)
    def _():
        relative_units(place_ref, all_ref, unit, groups, 0)
        for g in range(0, unit.shape[0], LANES):
            half = unit[g : g + LANES, :].astype(F32)
            turned[:, g : g + LANES] = jnp.transpose(half).astype(BF16)
        feat_ref[...] = turned[pl.ds(pl.multiple_of(place_ref[0] * feats, feats), feats), :]
        relative_logs(place_ref, cols_ref, lse, 1, height, log_protos)
        back[...] = jnp.zeros(back.shape, F32)
        for a in range(quarter):
            lanes = slice(a * LANES, (a + 1) * LANES)
            factor = factor_ref[quarter + a : quarter + a + 1, :] * protos
            scaled[:, lanes] = (feat_ref[:, lanes].astype(F32) * factor).astype(BF16)

    probabilities(unit.at[own:], w_ref, lse, SCALE_STUDENT, prob)
    grad_ref[...] = jnp.dot(scaled[...], exp_ref[...], preferred_element_type=F32) + jnp.dot(
        feat_ref[:, own:], prob[...], preferred_element_type=F32
    )
    back[...] += nt_dot(exp_ref[...], w_ref[...])

    @pl.when(step == pl.num_programs(0) - 1)
    def _():
        for a in range(quarter):
            here = slice(a * LANES, (a + 1) * LANES)
            factor = to_column(factor_ref[quarter + a : quarter + a + 1, :] * protos)
            back_ref[here, :] = (back[here, :] * factor).astype(BF16)


def last_kernel(
    cols_ref, factor_ref, s_ref, student_ref, exp_ref, prob_ref, w_ref,
    sums_ref, scale_ref, back_ref, scales, rows, back, scaled,
):
    step = pl.program_id(0)
    own, others = exp_ref.shape[0], prob_ref.shape[0]
    tiles = (own + others) // LANES
    quarter = own // LANES

    @pl.when(step == 0)
    def _():
        scales[...] = column_scales(cols_ref, scales.shape[0])
        scale_ref[...] = scales[...]
        rows[...] = jnp.zeros(rows.shape, F32)
        back[...] = jnp.zeros(back.shape, F32)

    scale = scales[pl.ds(step, 1), :]
    for ref, first in ((exp_ref, 0), (prob_ref, own)):
        for g in range(0, ref.shape[0], 64):
            here = slice(first + g, first + g + 64)
            rows[here, :] += fold(ref[g : g + 64, :].astype(F32) * scale)
    partner = (own + others) // 2 - own
    for g in range(0, own, 64):
        values = prob_ref[partner + g : partner + g + 64, :].astype(F32) * scale
        scaled[g : g + 64, :] = values.astype(BF16)
    back[...] += nt_dot(scaled[...], w_ref[...])

    @pl.when(step == pl.num_programs(0) - 1)
    def _():
        sums_ref[...] = jnp.zeros(sums_ref.shape, F32)
        pack_rows(sums_ref.at[0, :tiles], jnp.sum(rows[...], axis=1, keepdims=True))
        sums_ref[0, :quarter, :] = sums_ref[0, :quarter, :] * factor_ref[:quarter, :]
        half = unit_rows(s_ref[...])[0].astype(BF16).astype(F32)
        inner = jnp.sum(half * back[...], axis=1, keepdims=True)
        pack_rows(sums_ref.at[0, tiles : tiles + quarter], inner)
        repeat(sums_ref)
        share = back_ref.shape[1] // 2
        for p in range(back_ref.shape[0]):
            here = slice(p * share, (p + 1) * share)
            back_ref[p, :share, :] = student_ref[here, :]
            back_ref[p, share:, :] = back[here, :].astype(BF16)


def all_row_scales(sums_ref, tiles):
    return 1.0 / add_up([sums_ref[p, :tiles, :] for p in range(sums_ref.shape[0])])


def rows_kernel(tiles, protos, height, place_ref, s_ref, back_ref, sums_ref, cols_ref, out_ref, loss_ref, weight):
    parts, double, _ = back_ref.shape
    share = double // 2
    quarter = weight.shape[0] // LANES
    first = tiles // 2
    totals = add_up([sums_ref[p] for p in range(parts)])
    scale = 1.0 / totals[first : first + quarter, :]
    spread_rows(weight, scale)
    mine = pl.ds(pl.multiple_of(place_ref[1] * share, share), share)
    total = add_up([back_ref[p, :share, :].astype(F32) for p in range(parts)])
    paired = add_up([back_ref[p, share:, :].astype(F32) for p in range(parts)])
    total = total - paired * (weight[mine, :1] * protos)
    unit, length = unit_rows(s_ref[mine, :])
    out_ref[0] = (total - unit * jnp.sum(unit * total, axis=-1, keepdims=True)) / length
    repeat(out_ref)
    logs = cols_ref[pl.ds(place_ref[0], 1)][0]
    terms = jnp.zeros((1, LANES), F32)
    for a in range(quarter):
        lanes = slice((quarter + a) * LANES, (quarter + a + 1) * LANES)
        inner = totals[tiles + a : tiles + a + 1, :] * scale[a : a + 1, :]
        terms = terms + logs[height : height + 1, lanes] / LOG2E - inner / TEMP_STUDENT
    loss_ref[...] = jnp.broadcast_to(jnp.sum(terms), loss_ref.shape)


def grad_kernel(protos, exp_ref, prob_ref, feat_ref, part_ref, scale_ref, sums_ref, factor_ref, out_ref, scaled):
    own = exp_ref.shape[0]

    @pl.when(pl.program_id(0) == 0)
    def _():
        tiles = (own + prob_ref.shape[0]) // LANES
        rows = all_row_scales(sums_ref, tiles) * protos
        for a in range(tiles):
            other = (a + tiles // 2) % tiles
            feat = feat_ref[:, other * LANES : (other + 1) * LANES].astype(F32)
            row = rows[a : a + 1, :]
            if a < own // LANES:
                row = row * factor_ref[a : a + 1, :]
            scaled[:, a * LANES : (a + 1) * LANES] = (feat * row).astype(BF16)

    paired = jnp.dot(scaled[:, :own], exp_ref[...], preferred_element_type=F32)
    paired = paired + jnp.dot(scaled[:, own:], prob_ref[...], preferred_element_type=F32)
    scale = scale_ref[pl.ds(pl.program_id(0), 1), :]
    out_ref[...] = (part_ref[...] - paired * scale).astype(BF16)


def whole(array):
    rank = len(array.shape)
    return pl.BlockSpec(array.shape, lambda i: (0,) * rank)


def fixed(*shape):
    return pl.BlockSpec(shape, lambda i: (0,) * len(shape))


def columns(rows, cols):
    return pl.BlockSpec((rows, cols), lambda i: (0, i))


SMEM = pl.BlockSpec(memory_space=pltpu.SMEM)
VMEM = pl.BlockSpec(memory_space=pltpu.VMEM)


def params(mib):
    return pltpu.CompilerParams(vmem_limit_bytes=mib * 2**20)


def cost(flops, nbytes, exps=0):
    return pl.CostEstimate(flops=int(flops), bytes_accessed=int(nbytes), transcendentals=int(exps))


def exchange(value, axis):
    return lax.all_to_all(value, axis, 0, 0)


def local(teacher_feats, student_feats, proto_weight):
    parts, groups = lax.axis_size("proto"), lax.axis_size("batch")
    own, width = teacher_feats.shape
    local_protos = proto_weight.shape[1]
    rows = own * groups
    protos = local_protos * parts
    feats = width // groups
    share = own // parts
    tiles = rows // LANES
    height = local_protos // WIDE
    place = jnp.stack([lax.axis_index("batch"), lax.axis_index("proto")]).astype(jnp.int32)
    struct = jax.ShapeDtypeStruct
    weight_bytes = 2 * width * local_protos
    exp_bytes = 2 * own * local_protos
    others_bytes = 2 * (rows - own) * local_protos
    spread = pltpu.VMEM((own, LANES), F32)

    teacher_all = lax.all_gather(teacher_feats, "batch", tiled=True)
    student_all = lax.all_gather(student_feats, "batch", tiled=True)

    exp_struct = struct((own, local_protos), BF16)
    teacher_exp, student_exp, stats = pl.pallas_call(
        stats_kernel,
        in_specs=[VMEM] * 3,
        out_specs=[VMEM] * 3,
        out_shape=[exp_struct, exp_struct, struct((parts, 4 * own // LANES, LANES), F32)],
        scratch_shapes=[
            pltpu.VMEM((2, own, width), BF16),
            pltpu.VMEM((2, own, local_protos), F32),
            pltpu.VMEM((2, own, LANES), F32),
            pltpu.VMEM((2, own, LANES), F32),
        ],
        compiler_params=params(48),
        cost_estimate=cost(4 * own * width * local_protos, weight_bytes),
        name="own_rows",
    )(teacher_feats, student_feats, proto_weight)
    stats = exchange(stats, "proto")

    message = struct((groups, height + 8, WIDE), F32)
    factor, cols = pl.pallas_call(
        first_column_kernel,
        in_specs=[SMEM, VMEM, VMEM],
        out_specs=[VMEM] * 2,
        out_shape=[struct((8, LANES), F32), message],
        scratch_shapes=[spread],
        compiler_params=params(16),
        cost_estimate=cost(2 * own * local_protos, exp_bytes),
        name="first_columns",
    )(place, stats, teacher_exp)
    cols = exchange(cols, "batch")
    logs = cols

    for _ in range(SWEEPS - 1):
        sums = pl.pallas_call(
            row_kernel,
            in_specs=[VMEM] * 3,
            out_specs=VMEM,
            out_shape=struct((parts, 8, LANES), F32),
            scratch_shapes=[pltpu.VMEM((height, WIDE), F32)],
            compiler_params=params(16),
            cost_estimate=cost(2 * own * local_protos, exp_bytes),
            name="rows",
        )(cols, factor, teacher_exp)
        sums = exchange(sums, "proto")
        cols = pl.pallas_call(
            column_kernel,
            in_specs=[VMEM] * 3,
            out_specs=VMEM,
            out_shape=struct((groups, height, WIDE), F32),
            scratch_shapes=[spread],
            compiler_params=params(16),
            cost_estimate=cost(2 * own * local_protos, exp_bytes),
            name="columns",
        )(sums, factor, teacher_exp)
        cols = exchange(cols, "batch")

    grid = (height,)
    prob = pl.pallas_call(
        functools.partial(others_kernel, groups, height),
        grid=grid,
        in_specs=[SMEM, whole(teacher_all), whole(logs), columns(width, WIDE)],
        out_specs=columns(rows - own, WIDE),
        out_shape=struct((rows - own, local_protos), BF16),
        scratch_shapes=[pltpu.VMEM((rows - own, width), BF16), pltpu.VMEM((rows - own, LANES), F32)],
        compiler_params=params(40),
        cost_estimate=cost(2 * (rows - own) * width * local_protos, others_bytes),
        name="other_teachers",
    )(place, teacher_all, logs, proto_weight)

    grad_part, feat, back_student = pl.pallas_call(
        functools.partial(student_kernel, groups, height, math.log2(protos)),
        grid=grid,
        in_specs=[
            SMEM, whole(student_all), whole(logs), whole(factor), columns(width, WIDE),
            columns(own, WIDE),
        ],
        out_specs=[columns(feats, WIDE), fixed(feats, rows), fixed(own, width)],
        out_shape=[
            struct((feats, local_protos), F32), struct((feats, rows), BF16), struct((own, width), BF16),
        ],
        scratch_shapes=[
            pltpu.VMEM((rows, width), BF16),
            pltpu.VMEM((width, rows), BF16),
            pltpu.VMEM((feats, own), BF16),
            pltpu.VMEM((rows - own, LANES), F32),
            pltpu.VMEM((rows - own, WIDE), BF16),
            pltpu.VMEM((own, width), F32),
        ],
        compiler_params=params(40),
        cost_estimate=cost(3 * rows * width * local_protos, weight_bytes),
        name="student_side",
    )(place, student_all, logs, factor, proto_weight, student_exp)

    sums_shape = (parts, tiles + 8, LANES)
    back_shape = (parts, 2 * share, width)
    sums, col_scale, back = pl.pallas_call(
        last_kernel,
        grid=grid,
        in_specs=[
            whole(cols), whole(factor), whole(student_feats), whole(back_student),
            columns(own, WIDE), columns(rows - own, WIDE), columns(width, WIDE),
        ],
        out_specs=[fixed(*sums_shape), fixed(height, WIDE), fixed(*back_shape)],
        out_shape=[struct(sums_shape, F32), struct((height, WIDE), F32), struct(back_shape, BF16)],
        scratch_shapes=[
            pltpu.VMEM((height, WIDE), F32),
            pltpu.VMEM((rows, LANES), F32),
            pltpu.VMEM((own, width), F32),
            pltpu.VMEM((own, WIDE), BF16),
        ],
        compiler_params=params(40),
        cost_estimate=cost(2 * own * width * local_protos, others_bytes),
        name="last_rows",
    )(cols, factor, student_feats, back_student, teacher_exp, prob, proto_weight)
    sums = exchange(sums, "proto")
    back = exchange(back, "proto")

    grad_rows, loss_part = pl.pallas_call(
        functools.partial(rows_kernel, tiles, float(protos), height),
        in_specs=[SMEM] + [VMEM] * 4,
        out_specs=[VMEM] * 2,
        out_shape=[struct((parts, share, width), F32), struct((groups, 8, LANES), F32)],
        scratch_shapes=[spread],
        name="row_grads",
    )(place, student_feats, back, sums, logs)
    grad_rows = exchange(grad_rows, "proto").reshape(own, width)
    loss = jnp.sum(exchange(loss_part, "batch")[:, 0, 0]) / rows

    grad_weight = pl.pallas_call(
        functools.partial(grad_kernel, float(protos)),
        grid=grid,
        in_specs=[
            columns(own, WIDE), columns(rows - own, WIDE), whole(feat), columns(feats, WIDE),
            whole(col_scale), whole(sums), whole(factor),
        ],
        out_specs=columns(feats, WIDE),
        out_shape=struct((feats, local_protos), BF16),
        scratch_shapes=[pltpu.VMEM((feats, rows), BF16)],
        compiler_params=params(40),
        cost_estimate=cost(2 * feats * rows * local_protos, others_bytes),
        name="weight_grads",
    )(teacher_exp, prob, feat, grad_part, col_scale, sums, factor)
    return grad_weight, grad_rows, loss


def solution(mesh):
    return jax.shard_map(
        local,
        mesh=mesh,
        in_specs=(P("batch", None), P("batch", None), P(None, "proto")),
        out_specs=(P("batch", "proto"), P("batch", None), P()),
        check_vma=False,
    )
```

time: 886 us -> 208 us (0.23)
  waiting for transfers between devices: 596 us -> 14.7 us
  blocking collectives: 154 us -> 58.3 us
  matrix products: 74.2 us -> 0 us
  Pallas kernels: 0 us -> 69.9 us
  other arithmetic: 30.4 us -> 0.68 us
  local copies, waits for them, and re-layouts: 5.17 us -> 29.9 us
  starting transfers between devices: 0.15 us -> 16.9 us
    ppermute x1 -> x0, waiting for transfers between devices: 362 us -> none  [swapped(): return lax.ppermute(value, axis, pairs)]
    reduce_scatter x1 -> x0, waiting for transfers between devices: 234 us -> none  [local(): lax.psum_scatter(lax.dot_general(student_half, dlogits, (((0,), (0,)), ((...]
    psum x8 -> x0, blocking collectives: 139 us -> none  [the longest x3 51.1 us: local(): lax.psum(jnp.dot(row_scale, prob, precision=lax.Precision.HIGHEST).astype...]
    dot_general x10 -> x0, matrix products: 74.2 us -> none  [the longest x3 26.7 us: local(): jnp.dot(prob, col_scale, precision=lax.Precision.HIGHEST)]
    pallas_call x0 -> x11, Pallas kernels: none -> 69.9 us  [the longest x1 16.2 us: local(): pl.pallas_call(functools.partial(student_kernel, groups, height, math.log...]
    all_to_all x0 -> x6, blocking collectives: none -> 58.3 us  [exchange(): return lax.all_to_all(value, axis, 0, 0)]
    unnamed x14 -> x37, local copies, waits for them, and re-layouts: 5.17 us -> 29.9 us
    all_to_all x0 -> x4, starting transfers between devices: none -> 16.8 us  [exchange(): return lax.all_to_all(value, axis, 0, 0)]
  transfers between devices with their start and end apart: 3 -> 6, of which waited for: 3 -> 2; matrix products, arithmetic and copies ran while one was open for 2% -> 0% of each run, Pallas kernels for 0% -> 27%
where the time goes in v2:
time: 208 us; the launch traced here: 206 us
  Pallas kernels  69.9 us (34%)
  blocking collectives  58.3 us (28%)
  local copies, waits for them, and re-layouts  29.9 us (14%)
  starting transfers between devices  16.9 us (8%)
  between operations  15.9 us (8%)
  waiting for transfers between devices  14.7 us (7%)
    all_to_all x6, blocking collectives, exchange(): return lax.all_to_all(value, axis, 0, 0)  58.3 us
    unnamed x37, local copies, waits for them, and re-layouts  29.9 us
    all_to_all x4, starting transfers between devices, exchange(): return lax.all_to_all(value, axis, 0, 0)  16.8 us
    pallas_call x1, Pallas kernels, local(): pl.pallas_call(functools.partial(student_kernel, groups, height, math.log...  16.2 us
    all_to_all x4, waiting for transfers between devices, exchange(): return lax.all_to_all(value, axis, 0, 0)  13.3 us
    pallas_call x1, Pallas kernels, local(): pl.pallas_call(stats_kernel, in_specs=[VMEM] * 3, out_specs=[VMEM] * 3, o...  11.8 us
    pallas_call x1, Pallas kernels, local(): pl.pallas_call(last_kernel, grid=grid, in_specs=[whole(cols), whole(facto...  11.7 us
    pallas_call x1, Pallas kernels, local(): pl.pallas_call(functools.partial(others_kernel, groups, height), grid=gri...  11.1 us
  transfers between devices with their start and end apart: 6, of which 2 were waited for; matrix products, arithmetic and copies ran while one was open for 0% of the time, Pallas kernels for 27%

profile of v2, /device:TPU:0, one launch (start us, length us, event | category | flops | bytes accessed | tf_op | source)
XLA Modules:
  0.0 206.3 jit_solution(6499699905080110961)
XLA Ops:
  9.8 11.8 %own_rows.1 = (bf16[256,8192]{1,0:T(8,128)(2,1)S(1)}, bf16[256,8192]{1,0:T(8,128)(2,1)}, f32[8,8,128]{2,1,0:T(8,128)}) custom-call(bf16[256,512]{1,0:T(8,128)(2,1)S(1)} %copy-done.13, bf16[256,512]{1,0:T(8,128)(2,1)S(1)} %copy-done.9, bf16[512,8192]{1,0:T(8,128)(2,1)} %w_ref.7), custom_call_target="tpu_custom_call" | custom-call | flops 4294967296 | bytes 8388608 | tf_op jit(solution)/shard_map/own_rows/pallas_call | solution.py:420
  23.6 5.2 %all-to-all-start = ((f32[8,8,128]{2,1,0:T(8,128)}), f32[8,8,128]{2,1,0:T(8,128)S(1)}, u32[]{:S(2)}, u32[]{:S(2)}) async-start(f32[8,8,128]{2,1,0:T(8,128)} %get-tuple-element.17), calls=%async_computation | async-start | bytes 65536 | tf_op jit(solution)/shard_map/all_to_all | solution.py:396
  28.8 4.8 %all-to-all-done.stats_ref = f32[8,8,128]{2,1,0:T(8,128)S(1)} async-done(((f32[8,8,128]{2,1,0:T(8,128)}), f32[8,8,128]{2,1,0:T(8,128)S(1)}, u32[]{:S(2)}, u32[]{:S(2)}) %all-to-all-start) | async-done | bytes 32800 | tf_op jit(solution)/shard_map/all_to_all | solution.py:396
  33.6 2.2 %copy-done.1 = bf16[256,8192]{1,0:T(8,128)(2,1)S(1)} copy-done((bf16[256,8192]{1,0:T(8,128)(2,1)S(1)}, bf16[256,8192]{1,0:T(8,128)(2,1)}, u32[]{:S(2)}) %copy-start.1) | copy-done | bytes 4194328
  35.8 2.2 %first_columns.1 = (f32[8,128]{1,0:T(8,128)S(1)}, f32[4,16,1024]{2,1,0:T(8,128)}) custom-call(s32[2]{0:T(128)S(1)} %pad_add_fusion.place_ref, f32[8,8,128]{2,1,0:T(8,128)S(1)} %all-to-all-done.stats_ref, bf16[256,8192]{1,0:T(8,128)(2,1)S(1)} %copy-done.1), custom_call_target="tpu_custom_call" | custom-call | flops 4194304 | bytes 4194304 | tf_op jit(solution)/shard_map/first_columns/pallas_call | solution.py:438
  38.1 4.8 %all-to-all-start.1 = ((f32[4,16,1024]{2,1,0:T(8,128)}), f32[4,16,1024]{2,1,0:T(8,128)S(1)}, u32[]{:S(2)}, u32[]{:S(2)}) async-start(f32[4,16,1024]{2,1,0:T(8,128)} %get-tuple-element.18), calls=%async_computation.1 | async-start | bytes 524288 | tf_op jit(solution)/shard_map/all_to_all | solution.py:396
  43.6 8.5 %all-to-all-done.1.cols_ref = f32[4,16,1024]{2,1,0:T(8,128)S(1)} async-done(((f32[4,16,1024]{2,1,0:T(8,128)}), f32[4,16,1024]{2,1,0:T(8,128)S(1)}, u32[]{:S(2)}, u32[]{:S(2)}) %all-to-all-start.1) | async-done | bytes 262176 | tf_op jit(solution)/shard_map/all_to_all | solution.py:396
  52.1 2.4 %copy-done.2 = bf16[256,8192]{1,0:T(8,128)(2,1)S(1)} copy-done((bf16[256,8192]{1,0:T(8,128)(2,1)S(1)}, bf16[256,8192]{1,0:T(8,128)(2,1)}, u32[]{:S(2)}) %copy-start.2) | copy-done | bytes 4194328
  55.6 7.2 %all_to_all.50.sums_ref = f32[8,8,128]{2,1,0:T(8,128)S(1)} all-to-all(f32[8,8,128]{2,1,0:T(8,128)S(1)} %rows.2), channel_id=1, replica_groups=mesh['proto'=8,'batch'=4] {'proto'}, dimensions={0} | all-to-all | bytes 65536 | tf_op jit(solution)/shard_map/all_to_all | solution.py:396
  63.8 12.1 %all_to_all.51.cols_ref = f32[4,8,1024]{2,1,0:T(8,128)S(1)} all-to-all(f32[4,8,1024]{2,1,0:T(8,128)S(1)} %columns.2), channel_id=1, replica_groups=mesh['proto'=8,'batch'=4] {'batch'}, dimensions={0} | all-to-all | bytes 262144 | tf_op jit(solution)/shard_map/all_to_all | solution.py:396
  77.0 7.5 %all_to_all.52.sums_ref = f32[8,8,128]{2,1,0:T(8,128)S(1)} all-to-all(f32[8,8,128]{2,1,0:T(8,128)S(1)} %rows.3), channel_id=1, replica_groups=mesh['proto'=8,'batch'=4] {'proto'}, dimensions={0} | all-to-all | bytes 65536 | tf_op jit(solution)/shard_map/all_to_all | solution.py:396
  86.2 3.3 %all-to-all-start.5 = ((f32[4,8,1024]{2,1,0:T(8,128)}), f32[4,8,1024]{2,1,0:T(8,128)S(1)}, u32[]{:S(2)}, u32[]{:S(2)}) async-start(f32[4,8,1024]{2,1,0:T(8,128)} %columns.3), calls=%async_computation.5 | async-start | bytes 262144 | tf_op jit(solution)/shard_map/all_to_all | solution.py:396
  90.8 2.2 %copy-done.17 = bf16[256,8192]{1,0:T(8,128)(2,1)S(1)} copy-done((bf16[256,8192]{1,0:T(8,128)(2,1)S(1)}, bf16[256,8192]{1,0:T(8,128)(2,1)}, u32[]{:S(2)}) %copy-start.17) | copy-done | bytes 4194328
  93.0 16.2 %student_side.1 = (f32[128,8192]{1,0:T(8,128)S(1)}, bf16[128,1024]{1,0:T(8,128)(2,1)S(1)}, bf16[256,512]{1,0:T(8,128)(2,1)S(1)}) custom-call(s32[2]{0:T(128)S(1)} %pad_add_fusion.place_ref, bf16[1024,512]{1,0:T(8,128)(2,1)S(1)} %copy-done.15, f32[4,16,1024]{2,1,0:T(8,128)S(1)} %all-to-all-done.1.cols_ref, f32[8,128]{1,0:T(8,128)S(1)} %get-tuple-element.19.factor_ref, ...), custom_call_target="tpu_custom_call" | custom-call | flops 12884901888 | bytes 8388608 | tf_op jit(solution)/shard_map/student_side/pallas_call | solution.py:488
  111.1 3.4 %copy-done.5 = bf16[512,8192]{1,0:T(8,128)(2,1)S(1)} copy-done((bf16[512,8192]{1,0:T(8,128)(2,1)S(1)}, bf16[512,8192]{1,0:T(8,128)(2,1)}, u32[]{:S(2)}) %copy-start.5) | copy-done | bytes 8388632
  115.7 11.1 %other_teachers.1.prob_ref = bf16[768,8192]{1,0:T(8,128)(2,1)} custom-call(s32[2]{0:T(128)S(1)} %pad_add_fusion.place_ref, bf16[1024,512]{1,0:T(8,128)(2,1)S(1)} %copy-done.16, f32[4,16,1024]{2,1,0:T(8,128)S(1)} %all-to-all-done.1.cols_ref, bf16[512,8192]{1,0:T(8,128)(2,1)S(1)} %copy-done.5), custom_call_target="tpu_custom_call" | custom-call | flops 6442450944 | bytes 12582912 | tf_op jit(solution)/shard_map/other_teachers/pallas_call | solution.py:476
  129.1 3.4 %copy-done.6 = bf16[512,8192]{1,0:T(8,128)(2,1)S(1)} copy-done((bf16[512,8192]{1,0:T(8,128)(2,1)S(1)}, bf16[512,8192]{1,0:T(8,128)(2,1)}, u32[]{:S(2)}) %copy-start.6) | copy-done | bytes 8388632
  132.5 11.7 %last_rows.1 = (f32[8,16,128]{2,1,0:T(8,128)S(1)}, f32[8,1024]{1,0:T(8,128)S(1)}, bf16[8,64,512]{2,1,0:T(8,128)(2,1)S(1)}) custom-call(f32[4,8,1024]{2,1,0:T(8,128)S(1)} %all-to-all-done.5.cols_ref, f32[8,128]{1,0:T(8,128)S(1)} %get-tuple-element.19.factor_ref, bf16[256,512]{1,0:T(8,128)(2,1)S(1)} %copy-done.10, ...), custom_call_target="tpu_custom_call" | custom-call | flops 2147483648 | bytes 12582912 | tf_op jit(solution)/shard_map/last_rows/pallas_call | solution.py:514
  144.2 8.1 %all_to_all.53.sums_ref = f32[8,16,128]{2,1,0:T(8,128)} all-to-all(f32[8,16,128]{2,1,0:T(8,128)S(1)} %get-tuple-element.25), channel_id=1, replica_groups=mesh['proto'=8,'batch'=4] {'proto'}, dimensions={0} | all-to-all | bytes 131072 | tf_op jit(solution)/shard_map/all_to_all | solution.py:396
  152.3 12.8 %all_to_all.54.back_ref = bf16[8,64,512]{2,1,0:T(8,128)(2,1)} all-to-all(bf16[8,64,512]{2,1,0:T(8,128)(2,1)S(1)} %get-tuple-element.26), channel_id=1, replica_groups=mesh['proto'=8,'batch'=4] {'proto'}, dimensions={0} | all-to-all | bytes 1048576 | tf_op jit(solution)/shard_map/all_to_all | solution.py:396
  165.1 2.3 %row_grads.1 = (f32[8,32,512]{2,1,0:T(8,128)}, f32[4,8,128]{2,1,0:T(8,128)}) custom-call(s32[2]{0:T(128)} %copy-done.14, bf16[256,512]{1,0:T(8,128)(2,1)} %s_ref.5, bf16[8,64,512]{2,1,0:T(8,128)(2,1)} %all_to_all.54.back_ref, f32[8,16,128]{2,1,0:T(8,128)} %all_to_all.53.sums_ref, f32[4,16,1024]{2,1,0:T(8,128)} %copy-done.11), custom_call_target="tpu_custom_call" | custom-call | tf_op jit(solution)/shard_map/row_grads/pallas_call | solution.py:536
  167.4 10.6 %all_to_all.55 = f32[4,8,128]{2,1,0:T(8,128)S(1)} all-to-all(f32[4,8,128]{2,1,0:T(8,128)} %get-tuple-element.28), channel_id=1, replica_groups=mesh['proto'=8,'batch'=4] {'batch'}, dimensions={0} | all-to-all | bytes 32768 | tf_op jit(solution)/shard_map/all_to_all | solution.py:396
  178.0 3.5 %all-to-all-start.8 = ((f32[8,32,512]{2,1,0:T(8,128)}), f32[8,32,512]{2,1,0:T(8,128)S(1)}, u32[]{:S(2)}, u32[]{:S(2)}) async-start(f32[8,32,512]{2,1,0:T(8,128)} %get-tuple-element.27), calls=%async_computation.8 | async-start | bytes 1048576 | tf_op jit(solution)/shard_map/all_to_all | solution.py:396
  186.7 9.6 %weight_grads.1 = bf16[128,8192]{1,0:T(8,128)(2,1)} custom-call(bf16[256,8192]{1,0:T(8,128)(2,1)S(1)} %copy-done.4, bf16[768,8192]{1,0:T(8,128)(2,1)} %other_teachers.1.prob_ref, bf16[128,1024]{1,0:T(8,128)(2,1)S(1)} %get-tuple-element.21.feat_ref, f32[128,8192]{1,0:T(8,128)S(1)} %copy-done.8, f32[8,1024]{1,0:T(8,128)S(1)} %get-tuple-element.24.scale_ref, ...), custom_call_target="tpu_custom_call" | custom-call | flops 2147483648 | bytes 12582912 | tf_op jit(solution)/shard_map/weight_grads/pallas_call | solution.py:547
  (46 shorter events, 23.4 us)
Async XLA Ops:
  7.2 82.4 %all-gather.5.cloned.1.call-start = ((), (), s32[]{:S(2)}) async-start(), calls=%async_computation.11 | async-start | bytes 1310720 | tf_op jit(solution)/shard_map/all_gather | solution.py:417
  7.9 1.0 copy-start.9
  8.9 0.9 copy-start.13
  21.6 1.9 copy-start
  23.6 10.0 %all-to-all-start = ((f32[8,8,128]{2,1,0:T(8,128)}), f32[8,8,128]{2,1,0:T(8,128)S(1)}, u32[]{:S(2)}, u32[]{:S(2)}) async-start(f32[8,8,128]{2,1,0:T(8,128)} %get-tuple-element.17), calls=%async_computation | async-start | bytes 65536 | tf_op jit(solution)/shard_map/all_to_all | solution.py:396
  28.8 82.3 %copy-start.14 = (s32[2]{0:T(128)}, s32[2]{0:T(128)S(1)}, u32[]{:S(2)}) copy-start(s32[2]{0:T(128)S(1)} %pad_add_fusion.place_ref) | copy-start | bytes 28
  33.6 2.2 %copy-start.1 = (bf16[256,8192]{1,0:T(8,128)(2,1)S(1)}, bf16[256,8192]{1,0:T(8,128)(2,1)}, u32[]{:S(2)}) copy-start(bf16[256,8192]{1,0:T(8,128)(2,1)} %copy-done) | copy-start | bytes 12582916
  38.1 14.1 %all-to-all-start.1 = ((f32[4,16,1024]{2,1,0:T(8,128)}), f32[4,16,1024]{2,1,0:T(8,128)S(1)}, u32[]{:S(2)}, u32[]{:S(2)}) async-start(f32[4,16,1024]{2,1,0:T(8,128)} %get-tuple-element.18), calls=%async_computation.1 | async-start | bytes 524288 | tf_op jit(solution)/shard_map/all_to_all | solution.py:396
  42.9 68.2 %all-gather.3.cloned.1.call-start = ((), (), s32[]{:S(2)}) async-start(), calls=%async_computation.10 | async-start | bytes 1310720 | tf_op jit(solution)/shard_map/all_gather | solution.py:416
  52.1 59.0 %copy-start.11 = (f32[4,16,1024]{2,1,0:T(8,128)}, f32[4,16,1024]{2,1,0:T(8,128)S(1)}, u32[]{:S(2)}) copy-start(f32[4,16,1024]{2,1,0:T(8,128)S(1)} %all-to-all-done.1.cols_ref) | copy-start | bytes 786436
  52.1 2.4 %copy-start.2 = (bf16[256,8192]{1,0:T(8,128)(2,1)S(1)}, bf16[256,8192]{1,0:T(8,128)(2,1)}, u32[]{:S(2)}) copy-start(bf16[256,8192]{1,0:T(8,128)(2,1)} %copy-done) | copy-start | bytes 12582916
  86.2 40.7 %all-to-all-start.5 = ((f32[4,8,1024]{2,1,0:T(8,128)}), f32[4,8,1024]{2,1,0:T(8,128)S(1)}, u32[]{:S(2)}, u32[]{:S(2)}) async-start(f32[4,8,1024]{2,1,0:T(8,128)} %columns.3), calls=%async_computation.5 | async-start | bytes 262144 | tf_op jit(solution)/shard_map/all_to_all | solution.py:396
  89.5 1.2 copy-start.15
  90.8 2.2 %copy-start.17 = (bf16[256,8192]{1,0:T(8,128)(2,1)S(1)}, bf16[256,8192]{1,0:T(8,128)(2,1)}, u32[]{:S(2)}) copy-start(bf16[256,8192]{1,0:T(8,128)(2,1)} %get-tuple-element.20.exp_ref) | copy-start | bytes 12582916
  109.2 2.0 copy-start.7
  111.1 3.4 %copy-start.5 = (bf16[512,8192]{1,0:T(8,128)(2,1)S(1)}, bf16[512,8192]{1,0:T(8,128)(2,1)}, u32[]{:S(2)}) copy-start(bf16[512,8192]{1,0:T(8,128)(2,1)} %w_ref.7) | copy-start | bytes 25165828
  114.5 1.2 copy-start.16
  115.7 11.2 %copy-start.10 = (bf16[256,512]{1,0:T(8,128)(2,1)S(1)}, bf16[256,512]{1,0:T(8,128)(2,1)}, u32[]{:S(2)}) copy-start(bf16[256,512]{1,0:T(8,128)(2,1)} %s_ref.5) | copy-start | bytes 786436
  126.9 2.2 %copy-start.3 = (bf16[256,8192]{1,0:T(8,128)(2,1)S(1)}, bf16[256,8192]{1,0:T(8,128)(2,1)}, u32[]{:S(2)}) copy-start(bf16[256,8192]{1,0:T(8,128)(2,1)} %copy-done) | copy-start | bytes 12582916
  129.1 3.4 %copy-start.6 = (bf16[512,8192]{1,0:T(8,128)(2,1)S(1)}, bf16[512,8192]{1,0:T(8,128)(2,1)}, u32[]{:S(2)}) copy-start(bf16[512,8192]{1,0:T(8,128)(2,1)} %w_ref.7) | copy-start | bytes 25165828
  178.0 19.6 %all-to-all-start.8 = ((f32[8,32,512]{2,1,0:T(8,128)}), f32[8,32,512]{2,1,0:T(8,128)S(1)}, u32[]{:S(2)}, u32[]{:S(2)}) async-start(f32[8,32,512]{2,1,0:T(8,128)} %get-tuple-element.27), calls=%async_computation.8 | async-start | bytes 1048576 | tf_op jit(solution)/shard_map/all_to_all | solution.py:396
  181.5 2.2 %copy-start.4 = (bf16[256,8192]{1,0:T(8,128)(2,1)S(1)}, bf16[256,8192]{1,0:T(8,128)(2,1)}, u32[]{:S(2)}) copy-start(bf16[256,8192]{1,0:T(8,128)(2,1)} %copy-done) | copy-start | bytes 12582916
  183.7 2.2 %copy-start.8 = (f32[128,8192]{1,0:T(8,128)S(1)}, f32[128,8192]{1,0:T(8,128)}, u32[]{:S(2)}) copy-start(f32[128,8192]{1,0:T(8,128)} %copy-done.7) | copy-start | bytes 12582916
  185.9 0.8 copy-start.12
Sparse Core Ops, SparseCore 0:
  9.6 30.6 all-gather.4
  45.3 30.8 all-gather.2

commit v3 on v2

v3 whole, which is shorter than its diff:
```python
import functools
import math

import jax
import jax.numpy as jnp
from jax import lax
from jax.experimental import pallas as pl
from jax.experimental.pallas import tpu as pltpu
from jax.sharding import PartitionSpec as P

SWEEPS = 3
TEMP_TEACHER = 0.04
TEMP_STUDENT = 0.1
LOG2E = math.log2(math.e)
SCALE_TEACHER = LOG2E / TEMP_TEACHER
SCALE_STUDENT = LOG2E / TEMP_STUDENT
LANES = 128
WIDE = 1024
VMEM_MIB = 60
F32 = jnp.float32
BF16 = jnp.bfloat16


def unit_rows(values):
    wide = values.astype(F32)
    length = jnp.sqrt(jnp.sum(wide * wide, axis=-1, keepdims=True) + 1e-06)
    return wide / length, length


def diagonal():
    shape = (LANES, LANES)
    return lax.broadcasted_iota(jnp.int32, shape, 0) == lax.broadcasted_iota(jnp.int32, shape, 1)


def to_column(row):
    spread = jnp.where(diagonal(), jnp.broadcast_to(row, (LANES, LANES)), 0.0)
    return jnp.sum(spread, axis=1, keepdims=True)


def to_row(column):
    spread = jnp.where(diagonal(), jnp.broadcast_to(column, (LANES, LANES)), 0.0)
    return jnp.sum(spread, axis=0, keepdims=True)


def spread_rows(ref, rows):
    for a in range(rows.shape[0]):
        ref[a * LANES : (a + 1) * LANES, :] = jnp.broadcast_to(
            to_column(rows[a : a + 1, :]), (LANES, LANES)
        )


def pack_rows(ref, columns):
    for a in range(columns.shape[0] // LANES):
        ref[a : a + 1, :] = to_row(columns[a * LANES : (a + 1) * LANES, :])


def lane_tiles(values):
    return [values[:, t * LANES : (t + 1) * LANES] for t in range(values.shape[1] // LANES)]


def fold(values):
    return functools.reduce(jnp.add, lane_tiles(values))


def column_sums(values):
    rows, cols = values.shape
    return jnp.sum(values.reshape(rows // 8, 8, cols), axis=0)


def nt_dot(a, b):
    return lax.dot_general(a, b, (((1,), (1,)), ((), ())), preferred_element_type=F32)


def add_up(values):
    return functools.reduce(jnp.add, values)


def repeat(out_ref):
    for p in range(1, out_ref.shape[0]):
        out_ref[p] = out_ref[0]


def unit_kernel(t_ref, s_ref, t_unit, s_unit, s_out):
    t_unit[...] = unit_rows(t_ref[...])[0].astype(BF16)
    half = unit_rows(s_ref[...])[0].astype(BF16)
    s_unit[...] = half
    for g in range(s_out.shape[0]):
        s_out[g] = half


def stats_kernel(
    t_ref, s_ref, w_hbm, t_out, s_out, out_ref, w_ref, exps, logits, top, total, w_sem, out_sem
):
    chunk = 512
    cols = w_ref.shape[1]
    pieces = [slice(c, c + chunk) for c in range(0, cols, chunk)]
    quarter = out_ref.shape[1] // 4
    units = (t_ref, s_ref)
    outs = (t_out, s_out)
    scales = (SCALE_TEACHER, SCALE_STUDENT)
    loads = [
        pltpu.make_async_copy(
            w_hbm.at[:, c : c + WIDE], w_ref.at[:, c : c + WIDE], w_sem.at[c // WIDE]
        )
        for c in range(0, cols, WIDE)
    ]
    stores = [
        pltpu.make_async_copy(exps.at[which], outs[which], out_sem.at[which]) for which in range(2)
    ]
    for load in loads:
        load.start()
    top[...] = jnp.full(top.shape, -1e30, F32)
    total[...] = jnp.zeros(total.shape, F32)

    def product(which, here):
        values = jnp.dot(units[which][...], w_ref[:, here], preferred_element_type=F32) * scales[which]
        logits[which, :, here] = values
        top[which] = functools.reduce(jnp.maximum, lane_tiles(values), top[which])

    def peak(which):
        return jnp.max(top[which], axis=1, keepdims=True)

    def raised(which, here, shift):
        values = jnp.exp2(logits[which, :, here] - shift)
        exps[which, :, here] = values.astype(BF16)
        total[which] += fold(values)

    for k, here in enumerate(pieces):
        if here.start % WIDE == 0:
            loads[here.start // WIDE].wait()
        product(0, here)
    peaks = [peak(0)]
    shift = jnp.broadcast_to(peaks[0], (peaks[0].shape[0], chunk))
    for here in pieces:
        product(1, here)
        raised(0, here, shift)
    stores[0].start()
    peaks.append(peak(1))
    shift = jnp.broadcast_to(peaks[1], (peaks[1].shape[0], chunk))
    for here in pieces:
        raised(1, here, shift)
    stores[1].start()
    for which in range(2):
        sums = jnp.sum(total[which], axis=1, keepdims=True)
        for k, column in enumerate((peaks[which], sums)):
            first = (2 * which + k) * quarter
            pack_rows(out_ref.at[0, first : first + quarter], column)
    repeat(out_ref)
    for store in stores:
        store.wait()


def merged(stats_ref, which):
    parts, height, _ = stats_ref.shape
    quarter = height // 4
    first = 2 * which * quarter
    tops = [stats_ref[p, first : first + quarter, :] for p in range(parts)]
    top = functools.reduce(jnp.maximum, tops)
    sums = [
        stats_ref[p, first + quarter : first + 2 * quarter, :] * jnp.exp2(tops[p] - top)
        for p in range(parts)
    ]
    return top + jnp.log2(add_up(sums))


def column_pass(exp_ref, weight, out_ref):
    rows, cols = exp_ref.shape
    first = pl.program_id(0) * (cols // LANES)
    for a in range(0, cols, WIDE):
        sums = jnp.zeros((8, WIDE), F32)
        for g in range(0, rows, 16):
            shift = weight[g : g + 16, :]
            tiles = lane_tiles(exp_ref[g : g + 16, a : a + WIDE].astype(F32))
            sums = sums + column_sums(jnp.concatenate([tile * shift for tile in tiles], axis=1))
        sums = jnp.sum(sums, axis=0, keepdims=True)
        block = jnp.concatenate(lane_tiles(sums), axis=0)
        start = pl.multiple_of(first + a // LANES, 8)
        for g in range(out_ref.shape[0]):
            out_ref[g, pl.ds(start, WIDE // LANES), :] = block


def first_column_kernel(place_ref, stats_ref, exp_ref, factor_ref, out_ref, weight):
    @pl.when(pl.program_id(0) == 0)
    def _():
        quarter = stats_ref.shape[1] // 4
        height = out_ref.shape[1] - 8
        own = stats_ref[pl.ds(place_ref[1], 1)][0]
        factor_ref[...] = jnp.zeros(factor_ref.shape, F32)
        out_ref[0, height:, :] = jnp.zeros((8, LANES), F32)
        for which in range(2):
            log_sum = merged(stats_ref, which)
            here = slice(which * quarter, (which + 1) * quarter)
            factor_ref[here, :] = jnp.exp2(
                own[2 * which * quarter : (2 * which + 1) * quarter, :] - log_sum
            )
            out_ref[0, height + here.start : height + here.stop, :] = log_sum
        for g in range(1, out_ref.shape[0]):
            out_ref[g, height:, :] = out_ref[0, height:, :]
        spread_rows(weight, factor_ref[:quarter, :])

    column_pass(exp_ref, weight, out_ref)


def column_kernel(sums_ref, factor_ref, token_ref, exp_ref, out_ref, weight):
    @pl.when(pl.program_id(0) == 0)
    def _():
        quarter = weight.shape[0] // LANES
        scale = 1.0 / add_up([sums_ref[p, :quarter, :] for p in range(sums_ref.shape[0])])
        spread_rows(weight, scale * factor_ref[:quarter, :])

    column_pass(exp_ref, weight, out_ref)


def column_scales(cols_ref, height):
    return 1.0 / add_up([cols_ref[g, :height, :] for g in range(cols_ref.shape[0])])


def add_row_sums(rows, ref, first, scales, start, step):
    for g in range(0, ref.shape[0], step):
        total = rows[first + g : first + g + step, :]
        for t, tile in enumerate(lane_tiles(ref[g : g + step, :].astype(F32))):
            total = total + tile * scales[pl.ds(start + t, 1), :]
        rows[first + g : first + g + step, :] = total


def row_kernel(cols_ref, factor_ref, token_ref, exp_ref, out_ref, scales, rows):
    step = pl.program_id(0)

    @pl.when(step == 0)
    def _():
        scales[...] = column_scales(cols_ref, scales.shape[0])
        rows[...] = jnp.zeros(rows.shape, F32)

    add_row_sums(rows, exp_ref, 0, scales, step * (exp_ref.shape[1] // LANES), 32)

    @pl.when(step == pl.num_programs(0) - 1)
    def _():
        quarter = rows.shape[0] // LANES
        out_ref[0] = jnp.zeros(out_ref.shape[1:], F32)
        pack_rows(out_ref.at[0, :quarter], jnp.sum(rows[...], axis=1, keepdims=True))
        out_ref[0, :quarter, :] = out_ref[0, :quarter, :] * factor_ref[:quarter, :]
        repeat(out_ref)


def relative(place_ref, g, groups):
    return pl.ds(lax.rem(place_ref[0] + g, groups), 1)


def relative_logs(place_ref, logs_ref, lse, which, shift=0.0):
    groups = logs_ref.shape[0]
    own = lse.shape[0] // (groups - 1)
    quarter = own // LANES
    height = logs_ref.shape[1] - 8
    for g in range(1, groups):
        there = logs_ref[relative(place_ref, g, groups)][0]
        first = height + which * quarter
        spread_rows(lse.at[(g - 1) * own : g * own], there[first : first + quarter, :] - shift)


def probabilities(place_ref, all_ref, w_ref, lse, scale, prob_ref, use):
    groups, own, _ = all_ref.shape
    for g in range(1, groups):
        unit = all_ref[relative(place_ref, g, groups)][0]
        here = slice((g - 1) * own, g * own)
        for n in range(0, w_ref.shape[1], 512):
            logits = jnp.dot(unit, w_ref[:, n : n + 512], preferred_element_type=F32)
            shift = lse[here, :]
            tiles = [jnp.exp2(tile * scale - shift) for tile in lane_tiles(logits)]
            for k, tile in enumerate(tiles):
                prob_ref[here, n + k * LANES : n + (k + 1) * LANES] = tile.astype(BF16)
            if use is not None:
                use(g, n, tiles)


def own_back_kernel(protos, factor_ref, t_unit, w_ref, exp_ref, back_ref, t_out, back):
    step = pl.program_id(0)

    @pl.when(step == 0)
    def _():
        back[...] = jnp.zeros(back.shape, F32)
        for g in range(t_out.shape[0]):
            t_out[g] = t_unit[...]

    back[...] += nt_dot(exp_ref[...], w_ref[...])

    @pl.when(step == pl.num_programs(0) - 1)
    def _():
        quarter = back.shape[0] // LANES
        for a in range(quarter):
            here = slice(a * LANES, (a + 1) * LANES)
            factor = to_column(factor_ref[quarter + a : quarter + a + 1, :] * protos)
            back_ref[here, :] = (back[here, :] * factor).astype(BF16)


def feature_kernel(place_ref, all_ref, feat_ref, turned):
    groups, own, _ = all_ref.shape
    feats = feat_ref.shape[0]
    for g in range(groups):
        half = all_ref[relative(place_ref, g, groups)][0].astype(F32)
        for a in range(0, own, LANES):
            first = g * own + a
            turned[:, first : first + LANES] = jnp.transpose(half[a : a + LANES, :]).astype(BF16)
    feat_ref[...] = turned[pl.ds(pl.multiple_of(place_ref[0] * feats, feats), feats), :]


def student_kernel(
    log_protos, place_ref, all_ref, logs_ref, factor_ref, feat_ref, w_ref, exp_ref, *refs
):
    grad_ref, token_ref, scaled, lse, prob = refs[-5:]

    @pl.when(pl.program_id(0) == 0)
    def _():
        own = exp_ref.shape[0]
        quarter = own // LANES
        relative_logs(place_ref, logs_ref, lse, 1, log_protos)
        for a in range(quarter):
            lanes = slice(a * LANES, (a + 1) * LANES)
            factor = factor_ref[quarter + a : quarter + a + 1, :] * 2.0**log_protos
            scaled[:, lanes] = (feat_ref[:, lanes].astype(F32) * factor).astype(BF16)
        token_ref[...] = jnp.zeros(token_ref.shape, F32)

    probabilities(place_ref, all_ref, w_ref, lse, SCALE_STUDENT, prob, None)
    own = exp_ref.shape[0]
    grad_ref[...] = jnp.dot(scaled[...], exp_ref[...], preferred_element_type=F32) + jnp.dot(
        feat_ref[:, own:], prob[...], preferred_element_type=F32
    )


def as_three(value):
    high = value.astype(BF16)
    rest = value - high.astype(F32)
    middle = rest.astype(BF16)
    return high, middle, (rest - middle.astype(F32)).astype(BF16)


def last_kernel(
    place_ref, all_ref, logs_ref, cols_ref, factor_ref, token_ref, s_unit, student_ref, exp_ref, w_ref,
    prob_ref, scale_ref, out_ref, scales, rows, back, scaled, lse, sums,
):
    step = pl.program_id(0)
    own, others = exp_ref.shape[0], prob_ref.shape[0]
    groups = all_ref.shape[0]
    tiles = (own + others) // LANES
    quarter = own // LANES

    @pl.when(step == 0)
    def _():
        scales[...] = column_scales(cols_ref, scales.shape[0])
        scale_ref[...] = scales[...]
        rows[...] = jnp.zeros(rows.shape, F32)
        back[...] = jnp.zeros(back.shape, F32)
        relative_logs(place_ref, logs_ref, lse, 0)

    first = step * (w_ref.shape[1] // LANES)
    add_row_sums(rows, exp_ref, 0, scales, first, 32)

    def use(g, n, values):
        here = slice(g * own, (g + 1) * own)
        values = [
            tile * scales[pl.ds(first + n // LANES + k, 1), :] for k, tile in enumerate(values)
        ]
        rows[here, :] += add_up(values)
        if g == groups // 2:
            for k, tile in enumerate(values):
                scaled[:, n + k * LANES : n + (k + 1) * LANES] = tile.astype(BF16)

    probabilities(place_ref, all_ref, w_ref, lse, SCALE_TEACHER, prob_ref, use)
    back[...] += nt_dot(scaled[...], w_ref[...])

    @pl.when(step == pl.num_programs(0) - 1)
    def _():
        sums[...] = jnp.zeros(sums.shape, F32)
        pack_rows(sums.at[:tiles], jnp.sum(rows[...], axis=1, keepdims=True))
        sums[:quarter, :] = sums[:quarter, :] * factor_ref[:quarter, :]
        inner = jnp.sum(s_unit[...].astype(F32) * back[...], axis=1, keepdims=True)
        pack_rows(sums.at[tiles : tiles + quarter], inner)
        parts = out_ref.shape[0]
        share = own // parts
        for k, term in enumerate(as_three(sums[...])):
            for p in range(parts):
                out_ref[p, 2 * share :, k * LANES : (k + 1) * LANES] = term
        for p in range(parts):
            here = slice(p * share, (p + 1) * share)
            out_ref[p, : 2 * share, :] = jnp.concatenate(
                [student_ref[here, :], back[here, :].astype(BF16)], axis=0
            )
            out_ref[p, 2 * share :, 3 * LANES :] = jnp.zeros(
                (sums.shape[0], out_ref.shape[2] - 3 * LANES), BF16
            )


def total_sums(message_ref, first):
    parts = message_ref.shape[0]
    each = [
        add_up([t.astype(F32) for t in lane_tiles(message_ref[p, first:, : 3 * LANES])[::-1]])
        for p in range(parts)
    ]
    return add_up(each)


def rows_kernel(tiles, protos, place_ref, s_ref, message_ref, logs_ref, out_ref, loss_ref, sums_ref, weight):
    parts = message_ref.shape[0]
    share, own = out_ref.shape[1], weight.shape[0]
    quarter = own // LANES
    first = tiles // 2
    totals = total_sums(message_ref, 2 * share)
    sums_ref[...] = totals
    scale = 1.0 / totals[first : first + quarter, :]
    spread_rows(weight, scale)
    mine = pl.ds(pl.multiple_of(place_ref[1] * share, share), share)
    total = add_up([message_ref[p, :share, :].astype(F32) for p in range(parts)])
    paired = add_up([message_ref[p, share : 2 * share, :].astype(F32) for p in range(parts)])
    total = total - paired * (weight[mine, :1] * protos)
    unit, length = unit_rows(s_ref[mine, :])
    out_ref[0] = (total - unit * jnp.sum(unit * total, axis=-1, keepdims=True)) / length
    repeat(out_ref)
    height = logs_ref.shape[1] - 8
    logs = logs_ref[pl.ds(place_ref[0], 1)][0][height + quarter : height + 2 * quarter, :]
    terms = logs / LOG2E - totals[tiles : tiles + quarter, :] * scale / TEMP_STUDENT
    loss_ref[...] = jnp.broadcast_to(jnp.sum(terms), loss_ref.shape)


def grad_kernel(protos, exp_ref, prob_ref, feat_ref, part_ref, scale_ref, sums_ref, factor_ref, out_ref, scaled):
    own = exp_ref.shape[0]

    @pl.when(pl.program_id(0) == 0)
    def _():
        tiles = (own + prob_ref.shape[0]) // LANES
        rows = protos / sums_ref[:tiles, :]
        for a in range(tiles):
            other = (a + tiles // 2) % tiles
            feat = feat_ref[:, other * LANES : (other + 1) * LANES].astype(F32)
            row = rows[a : a + 1, :]
            if a < own // LANES:
                row = row * factor_ref[a : a + 1, :]
            scaled[:, a * LANES : (a + 1) * LANES] = (feat * row).astype(BF16)

    paired = jnp.dot(scaled[:, :own], exp_ref[...], preferred_element_type=F32)
    paired = paired + jnp.dot(scaled[:, own:], prob_ref[...], preferred_element_type=F32)
    first = pl.program_id(0) * (out_ref.shape[1] // LANES)
    for t, tile in enumerate(lane_tiles(paired)):
        lanes = slice(t * LANES, (t + 1) * LANES)
        scale = scale_ref[pl.ds(first + t, 1), :]
        out_ref[:, lanes] = (part_ref[:, lanes] - tile * scale).astype(BF16)


def whole(array):
    rank = len(array.shape)
    return pl.BlockSpec(array.shape, lambda i: (0,) * rank)


def fixed(*shape):
    return pl.BlockSpec(shape, lambda i: (0,) * len(shape))


def columns(rows, cols, first=0):
    return pl.BlockSpec((rows, cols), lambda i: (0, first + i))


SMEM = pl.BlockSpec(memory_space=pltpu.SMEM)
VMEM = pl.BlockSpec(memory_space=pltpu.VMEM)
ANY = pl.BlockSpec(memory_space=pl.ANY)


def params():
    return pltpu.CompilerParams(vmem_limit_bytes=VMEM_MIB * 2**20)


def cost(flops, nbytes, exps=0):
    return pl.CostEstimate(flops=int(flops), bytes_accessed=int(nbytes), transcendentals=int(exps))


def exchange(value, axis):
    return lax.all_to_all(value, axis, 0, 0)


def local(teacher_feats, student_feats, proto_weight):
    parts, groups = lax.axis_size("proto"), lax.axis_size("batch")
    own, width = teacher_feats.shape
    local_protos = proto_weight.shape[1]
    rows = own * groups
    others = rows - own
    protos = local_protos * parts
    feats = width // groups
    share = own // parts
    tiles = rows // LANES
    height = local_protos // LANES
    place = jnp.stack([lax.axis_index("batch"), lax.axis_index("proto")]).astype(jnp.int32)
    struct = jax.ShapeDtypeStruct
    weight_bytes = 2 * width * local_protos
    exp_bytes = 2 * own * local_protos
    others_bytes = 2 * others * local_protos
    spread = pltpu.VMEM((own, LANES), F32)
    unit = struct((own, width), BF16)
    all_units = struct((groups, own, width), BF16)
    token = struct((8, LANES), F32)

    t_unit, s_unit, s_all = pl.pallas_call(
        unit_kernel,
        out_shape=[unit, unit, all_units],
        compiler_params=params(),
        cost_estimate=cost(8 * own * width, 12 * own * width),
        name="unit_rows",
    )(teacher_feats, student_feats)
    s_all = exchange(s_all, "batch")

    exps = struct((own, local_protos), BF16)
    t_exp, s_exp, stats = pl.pallas_call(
        stats_kernel,
        in_specs=[VMEM, VMEM, ANY],
        out_specs=[ANY, ANY, VMEM],
        out_shape=[exps, exps, struct((parts, 4 * own // LANES, LANES), F32)],
        scratch_shapes=[
            pltpu.VMEM((width, local_protos), BF16),
            pltpu.VMEM((2, own, local_protos), BF16),
            pltpu.VMEM((2, own, local_protos), F32),
            pltpu.VMEM((2, own, LANES), F32),
            pltpu.VMEM((2, own, LANES), F32),
            pltpu.SemaphoreType.DMA((local_protos // WIDE,)),
            pltpu.SemaphoreType.DMA((2,)),
        ],
        compiler_params=params(),
        cost_estimate=cost(4 * own * width * local_protos, weight_bytes),
        name="own_rows",
    )(t_unit, s_unit, proto_weight)
    stats = exchange(stats, "proto")

    half_sweep = 2048
    sweep_grid = (local_protos // half_sweep,)
    first_shape = (groups, height + 8, LANES)
    factor, cols = pl.pallas_call(
        first_column_kernel,
        grid=sweep_grid,
        in_specs=[SMEM, whole(stats), columns(own, half_sweep)],
        out_specs=[fixed(8, LANES), fixed(*first_shape)],
        out_shape=[token, struct(first_shape, F32)],
        scratch_shapes=[spread],
        compiler_params=params(),
        cost_estimate=cost(2 * own * local_protos, exp_bytes),
        name="first_columns",
    )(place, stats, t_exp)

    back_student, t_all = pl.pallas_call(
        functools.partial(own_back_kernel, float(protos)),
        grid=sweep_grid,
        in_specs=[
            fixed(8, LANES), whole(t_unit), columns(width, half_sweep), columns(own, half_sweep),
        ],
        out_specs=[fixed(own, width), fixed(groups, own, width)],
        out_shape=[unit, all_units],
        scratch_shapes=[pltpu.VMEM((own, width), F32)],
        compiler_params=params(),
        cost_estimate=cost(2 * own * width * local_protos, weight_bytes),
        name="own_back",
    )(factor, t_unit, proto_weight, s_exp)
    t_all = exchange(t_all, "batch")
    cols = exchange(cols, "batch")
    logs = cols

    feat = pl.pallas_call(
        feature_kernel,
        in_specs=[SMEM, VMEM],
        out_specs=VMEM,
        out_shape=struct((feats, rows), BF16),
        scratch_shapes=[pltpu.VMEM((width, rows), BF16)],
        compiler_params=params(),
        cost_estimate=cost(8 * rows * width, 2 * rows * width),
        name="features",
    )(place, s_all)

    def student_piece(first, count, grad, before):
        out_struct = struct((feats, local_protos), F32)
        prior = [] if grad is None else [grad]
        return pl.pallas_call(
            functools.partial(student_kernel, math.log2(protos)),
            grid=(count,),
            in_specs=[
                SMEM, whole(s_all), whole(logs), whole(factor), whole(feat),
                columns(width, WIDE, first), columns(own, WIDE, first), ANY,
            ]
            + [ANY] * len(prior),
            out_specs=[columns(feats, WIDE, first), fixed(8, LANES)],
            out_shape=[out_struct, token],
            scratch_shapes=[
                pltpu.VMEM((feats, own), BF16),
                pltpu.VMEM((others, LANES), F32),
                pltpu.VMEM((others, WIDE), BF16),
            ],
            input_output_aliases={8: 0} if prior else {},
            compiler_params=params(),
            cost_estimate=cost(
                2.5 * rows * width * WIDE * count, 2 * width * WIDE * count
            ),
            name="student_side",
        )(place, s_all, logs, factor, feat, proto_weight, s_exp, before, *prior)

    grad_part, first, done = None, 0, None
    counts = [1, 2, 1, 2, 2]
    chunks = local_protos // WIDE
    for turn in range(SWEEPS - 1):
        sums = pl.pallas_call(
            row_kernel,
            grid=sweep_grid,
            in_specs=[whole(cols), fixed(8, LANES), ANY, columns(own, half_sweep)],
            out_specs=fixed(parts, 8, LANES),
            out_shape=struct((parts, 8, LANES), F32),
            scratch_shapes=[pltpu.VMEM((height, LANES), F32), spread],
            compiler_params=params(),
            cost_estimate=cost(2 * own * local_protos, exp_bytes),
            name="rows",
        )(cols, factor, back_student if done is None else done, t_exp)
        count = counts[2 * turn] * chunks // 8
        grad_part, done = student_piece(first, count, grad_part, sums)
        first += count
        sums = exchange(sums, "proto")
        cols = pl.pallas_call(
            column_kernel,
            grid=sweep_grid,
            in_specs=[whole(sums), fixed(8, LANES), ANY, columns(own, half_sweep)],
            out_specs=fixed(groups, height, LANES),
            out_shape=struct((groups, height, LANES), F32),
            scratch_shapes=[spread],
            compiler_params=params(),
            cost_estimate=cost(2 * own * local_protos, exp_bytes),
            name="columns",
        )(sums, factor, done, t_exp)
        count = counts[2 * turn + 1] * chunks // 8
        grad_part, done = student_piece(first, count, grad_part, cols)
        first += count
        cols = exchange(cols, "batch")

    grid = (chunks,)
    sum_rows = -(-(tiles + own // LANES) // 16) * 16
    message_shape = (parts, 2 * share + sum_rows, width)
    prob, col_scale, message = pl.pallas_call(
        last_kernel,
        grid=grid,
        in_specs=[
            SMEM, whole(t_all), whole(logs), whole(cols), whole(factor), ANY, whole(s_unit),
            whole(back_student), columns(own, WIDE), columns(width, WIDE),
        ],
        out_specs=[columns(others, WIDE), fixed(height, LANES), fixed(*message_shape)],
        out_shape=[
            struct((others, local_protos), BF16),
            struct((height, LANES), F32),
            struct(message_shape, BF16),
        ],
        scratch_shapes=[
            pltpu.VMEM((height, LANES), F32),
            pltpu.VMEM((rows, LANES), F32),
            pltpu.VMEM((own, width), F32),
            pltpu.VMEM((own, WIDE), BF16),
            pltpu.VMEM((others, LANES), F32),
            pltpu.VMEM((sum_rows, LANES), F32),
        ],
        compiler_params=params(),
        cost_estimate=cost(2 * rows * width * local_protos, others_bytes),
        name="last_rows",
    )(place, t_all, logs, cols, factor, done, s_unit, back_student, t_exp, proto_weight)
    grad_part, done = student_piece(first, chunks - first, grad_part, message)
    message = exchange(message, "proto")

    grad_rows, loss_part, sums = pl.pallas_call(
        functools.partial(rows_kernel, tiles, float(protos)),
        in_specs=[SMEM] + [VMEM] * 3,
        out_specs=[VMEM] * 3,
        out_shape=[
            struct((parts, share, width), F32),
            struct((groups, 8, LANES), F32),
            struct((sum_rows, LANES), F32),
        ],
        scratch_shapes=[spread],
        compiler_params=params(),
        name="row_grads",
    )(place, student_feats, message, logs)
    grad_rows = exchange(grad_rows, "proto").reshape(own, width)
    loss = jnp.sum(exchange(loss_part, "batch")[:, 0, 0]) / rows

    grad_weight = pl.pallas_call(
        functools.partial(grad_kernel, float(protos)),
        grid=grid,
        in_specs=[
            columns(own, WIDE), columns(others, WIDE), whole(feat), columns(feats, WIDE),
            whole(col_scale), whole(sums), fixed(8, LANES),
        ],
        out_specs=columns(feats, WIDE),
        out_shape=struct((feats, local_protos), BF16),
        scratch_shapes=[pltpu.VMEM((feats, rows), BF16)],
        compiler_params=params(),
        cost_estimate=cost(2 * feats * rows * local_protos, others_bytes),
        name="weight_grads",
    )(t_exp, prob, feat, grad_part, col_scale, sums, factor)
    return grad_weight, grad_rows, loss


def solution(mesh):
    return jax.shard_map(
        local,
        mesh=mesh,
        in_specs=(P("batch", None), P("batch", None), P(None, "proto")),
        out_specs=(P("batch", "proto"), P("batch", None), P()),
        check_vma=False,
    )
```

time: 208 us -> 219 us (1.053)
  Pallas kernels: 69.9 us -> 102 us
  local copies, waits for them, and re-layouts: 29.9 us -> 3.34 us
  waiting for transfers between devices: 14.7 us -> 35.7 us
  between operations: 15.9 us -> 2.51 us
  blocking collectives: 58.3 us -> 46.2 us
  starting transfers between devices: 16.9 us -> 26.5 us
    pallas_call x10 -> x16, Pallas kernels: 60.3 us -> 90.2 us  [the longest x5 24.5 us: student_piece(): pl.pallas_call(functools.partial(student_kernel, math.log2(protos)), grid...]
    unnamed x37 -> x13, local copies, waits for them, and re-layouts: 29.9 us -> 3.34 us
    all_to_all x4 -> x7, waiting for transfers between devices: 13.3 us -> 35.7 us  [exchange(): return lax.all_to_all(value, axis, 0, 0)]
    all_to_all x6 -> x4, blocking collectives: 58.3 us -> 46.2 us  [exchange(): return lax.all_to_all(value, axis, 0, 0)]
    all_to_all x4 -> x7, starting transfers between devices: 16.8 us -> 26.5 us  [exchange(): return lax.all_to_all(value, axis, 0, 0)]
  transfers between devices with their start and end apart: 6 -> 7, of which waited for: 2 -> 5; matrix products, arithmetic and copies ran while one was open for 0% -> 1% of each run, Pallas kernels for 27% -> 25%
where the time goes in v3:
time: 219 us; the launch traced here: 217 us
  Pallas kernels  102 us (47%)
  blocking collectives  46.2 us (21%)
  waiting for transfers between devices  35.7 us (16%)
  starting transfers between devices  26.5 us (12%)
  local copies, waits for them, and re-layouts  3.34 us (2%)
  between operations  2.51 us (1%)
    all_to_all x4, blocking collectives, exchange(): return lax.all_to_all(value, axis, 0, 0)  46.2 us
    all_to_all x7, waiting for transfers between devices, exchange(): return lax.all_to_all(value, axis, 0, 0)  35.7 us
    all_to_all x7, starting transfers between devices, exchange(): return lax.all_to_all(value, axis, 0, 0)  26.5 us
    pallas_call x5, Pallas kernels, student_piece(): pl.pallas_call(functools.partial(student_kernel, math.log2(protos)), grid...  24.5 us
    pallas_call x1, Pallas kernels, local(): pl.pallas_call(last_kernel, grid=grid, in_specs=[SMEM, whole(t_all), whol...  17.9 us
    pallas_call x1, Pallas kernels, local(): pl.pallas_call(stats_kernel, in_specs=[VMEM, VMEM, ANY], out_specs=[ANY,...  12.6 us
    pallas_call x1, Pallas kernels, local(): pl.pallas_call(functools.partial(grad_kernel, float(protos)), grid=grid,...  11.6 us
    pallas_call x2, Pallas kernels, local(): pl.pallas_call(row_kernel, grid=sweep_grid, in_specs=[whole(cols), fixed(...  8.16 us
  transfers between devices with their start and end apart: 7, of which 5 were waited for; matrix products, arithmetic and copies ran while one was open for 1% of the time, Pallas kernels for 25%

profile of v3, /device:TPU:0, one launch (start us, length us, event | category | flops | bytes accessed | tf_op | source)
XLA Modules:
  0.0 217.3 jit_solution(6615308164324709687)
XLA Ops:
  3.0 12.6 %own_rows.1 = (bf16[256,8192]{1,0:T(8,128)(2,1)}, bf16[256,8192]{1,0:T(8,128)(2,1)}, f32[8,8,128]{2,1,0:T(8,128)}) custom-call(bf16[256,512]{1,0:T(8,128)(2,1)} %get-tuple-element.28.t_ref.t_unit, bf16[256,512]{1,0:T(8,128)(2,1)} %get-tuple-element.29.s_ref.s_unit, bf16[512,8192]{1,0:T(8,128)(2,1)} %w_ref.13), custom_call_target="tpu_custom_call" | custom-call | flops 4294967296 | bytes 8388608 | tf_op jit(solution)/shard_map/own_rows/pallas_call | solution.py:508
  15.7 5.2 %all-to-all-start = ((f32[8,8,128]{2,1,0:T(8,128)}), f32[8,8,128]{2,1,0:T(8,128)S(1)}, u32[]{:S(2)}, u32[]{:S(2)}) async-start(f32[8,8,128]{2,1,0:T(8,128)} %get-tuple-element.31), calls=%async_computation | async-start | bytes 65536 | tf_op jit(solution)/shard_map/all_to_all | solution.py:474
  21.5 4.2 %all-to-all-done.stats_ref = f32[8,8,128]{2,1,0:T(8,128)S(1)} async-done(((f32[8,8,128]{2,1,0:T(8,128)}), f32[8,8,128]{2,1,0:T(8,128)S(1)}, u32[]{:S(2)}, u32[]{:S(2)}) %all-to-all-start) | async-done | bytes 32800 | tf_op jit(solution)/shard_map/all_to_all | solution.py:474
  26.3 4.1 %first_columns.1 = (f32[8,128]{1,0:T(8,128)}, f32[4,72,128]{2,1,0:T(8,128)}) custom-call(s32[2]{0:T(128)} %pad_add_fusion.place_ref, f32[8,8,128]{2,1,0:T(8,128)} %copy-done.3, bf16[256,8192]{1,0:T(8,128)(2,1)} %get-tuple-element.30.exp_ref), custom_call_target="tpu_custom_call" | custom-call | flops 4194304 | bytes 4194304 | tf_op jit(solution)/shard_map/first_columns/pallas_call | solution.py:531
  30.4 11.6 %all_to_all.55.cols_ref.logs_ref = f32[4,72,128]{2,1,0:T(8,128)} all-to-all(f32[4,72,128]{2,1,0:T(8,128)} %get-tuple-element.35), channel_id=1, replica_groups=mesh['proto'=8,'batch'=4] {'batch'}, dimensions={0} | all-to-all | bytes 294912 | tf_op jit(solution)/shard_map/all_to_all | solution.py:474
  42.0 3.5 %all-to-all-start.4 = ((bf16[4,256,512]{2,1,0:T(8,128)(2,1)}), bf16[4,256,512]{2,1,0:T(8,128)(2,1)S(1)}, u32[]{:S(2)}, u32[]{:S(2)}) async-start(bf16[4,256,512]{2,1,0:T(8,128)(2,1)} %get-tuple-element.37), calls=%async_computation.4 | async-start | bytes 2097152 | tf_op jit(solution)/shard_map/all_to_all | solution.py:474
  45.6 7.8 %own_back.1 = (bf16[256,512]{1,0:T(8,128)(2,1)}, bf16[4,256,512]{2,1,0:T(8,128)(2,1)}) custom-call(f32[8,128]{1,0:T(8,128)} %get-tuple-element.32.factor_ref, bf16[256,512]{1,0:T(8,128)(2,1)} %get-tuple-element.28.t_ref.t_unit, bf16[512,8192]{1,0:T(8,128)(2,1)} %w_ref.13, bf16[256,8192]{1,0:T(8,128)(2,1)} %get-tuple-element.33.exp_ref), custom_call_target="tpu_custom_call" | custom-call | flops 2147483648 | bytes 8388608 | tf_op jit(solution)/shard_map/own_back/pallas_call | solution.py:543
  53.3 4.1 %rows.2.refs_0_ = f32[8,8,128]{2,1,0:T(8,128)} custom-call(f32[4,72,128]{2,1,0:T(8,128)} %all_to_all.55.cols_ref.logs_ref, f32[8,128]{1,0:T(8,128)} %get-tuple-element.32.factor_ref, bf16[256,512]{1,0:T(8,128)(2,1)} %get-tuple-element.36.token_ref.student_ref, bf16[256,8192]{1,0:T(8,128)(2,1)} %get-tuple-element.30.exp_ref), custom_call_target="tpu_custom_call" | custom-call | flops 4194304 | bytes 4194304 | tf_op jit(solution)/shard_map/rows/pallas_call | solution.py:601
  57.4 12.7 %all-to-all-done.4.all_ref = bf16[4,256,512]{2,1,0:T(8,128)(2,1)S(1)} async-done(((bf16[4,256,512]{2,1,0:T(8,128)(2,1)}), bf16[4,256,512]{2,1,0:T(8,128)(2,1)S(1)}, u32[]{:S(2)}, u32[]{:S(2)}) %all-to-all-start.4) | async-done | bytes 1048608 | tf_op jit(solution)/shard_map/all_to_all | solution.py:474
  75.8 4.0 %student_side.5 = (f32[128,8192]{1,0:T(8,128)}, f32[8,128]{1,0:T(8,128)}) custom-call(s32[2]{0:T(128)} %pad_add_fusion.place_ref, bf16[4,256,512]{2,1,0:T(8,128)(2,1)} %copy-done, f32[4,72,128]{2,1,0:T(8,128)} %all_to_all.55.cols_ref.logs_ref, f32[8,128]{1,0:T(8,128)} %get-tuple-element.32.factor_ref, bf16[128,1024]{1,0:T(8,128)(2,1)} %features.1.feat_ref, ...), custom_call_target="tpu_custom_call" | custom-call | flops 1342177280 | bytes 1048576 | tf_op jit(solution)/shard_map/student_side/pallas_call | solution.py:574
  80.4 4.1 %columns.2.refs_0_ = f32[4,64,128]{2,1,0:T(8,128)} custom-call(f32[8,8,128]{2,1,0:T(8,128)} %copy-done.4, f32[8,128]{1,0:T(8,128)} %get-tuple-element.32.factor_ref, f32[8,128]{1,0:T(8,128)} %get-tuple-element.38.token_ref, bf16[256,8192]{1,0:T(8,128)(2,1)} %get-tuple-element.30.exp_ref), custom_call_target="tpu_custom_call" | custom-call | flops 4194304 | bytes 4194304 | tf_op jit(solution)/shard_map/columns/pallas_call | solution.py:616
  88.0 5.5 %student_side.6 = (f32[128,8192]{1,0:T(8,128)}, f32[8,128]{1,0:T(8,128)}) custom-call(s32[2]{0:T(128)} %pad_add_fusion.place_ref, bf16[4,256,512]{2,1,0:T(8,128)(2,1)} %copy-done, f32[4,72,128]{2,1,0:T(8,128)} %all_to_all.55.cols_ref.logs_ref, f32[8,128]{1,0:T(8,128)} %get-tuple-element.32.factor_ref, ...), custom_call_target="tpu_custom_call", output_to_operand_aliasing={{0}: (8, {})} | custom-call | flops 2684354560 | bytes 2097152 | tf_op jit(solution)/shard_map/student_side/pallas_call | solution.py:574
  95.0 4.1 %rows.3.refs_0_ = f32[8,8,128]{2,1,0:T(8,128)} custom-call(f32[4,64,128]{2,1,0:T(8,128)} %copy-done.2, f32[8,128]{1,0:T(8,128)} %get-tuple-element.32.factor_ref, f32[8,128]{1,0:T(8,128)} %get-tuple-element.40.token_ref, bf16[256,8192]{1,0:T(8,128)(2,1)} %get-tuple-element.30.exp_ref), custom_call_target="tpu_custom_call" | custom-call | flops 4194304 | bytes 4194304 | tf_op jit(solution)/shard_map/rows/pallas_call | solution.py:601
  99.1 8.9 %all_to_all.56.sums_ref = f32[8,8,128]{2,1,0:T(8,128)} all-to-all(f32[8,8,128]{2,1,0:T(8,128)} %rows.3.refs_0_), channel_id=1, replica_groups=mesh['proto'=8,'batch'=4] {'proto'}, dimensions={0} | all-to-all | bytes 65536 | tf_op jit(solution)/shard_map/all_to_all | solution.py:474
  108.0 4.1 %all-to-all-start.1 = ((bf16[4,256,512]{2,1,0:T(8,128)(2,1)}), bf16[4,256,512]{2,1,0:T(8,128)(2,1)S(1)}, u32[]{:S(2)}, u32[]{:S(2)}) async-start(bf16[4,256,512]{2,1,0:T(8,128)(2,1)} %get-tuple-element.34), calls=%async_computation.1 | async-start | bytes 2097152 | tf_op jit(solution)/shard_map/all_to_all | solution.py:474
  112.1 4.0 %student_side.7 = (f32[128,8192]{1,0:T(8,128)}, f32[8,128]{1,0:T(8,128)}) custom-call(s32[2]{0:T(128)} %pad_add_fusion.place_ref, bf16[4,256,512]{2,1,0:T(8,128)(2,1)} %copy-done, f32[4,72,128]{2,1,0:T(8,128)} %all_to_all.55.cols_ref.logs_ref, f32[8,128]{1,0:T(8,128)} %get-tuple-element.32.factor_ref, ...), custom_call_target="tpu_custom_call", output_to_operand_aliasing={{0}: (8, {})} | custom-call | flops 1342177280 | bytes 1048576 | tf_op jit(solution)/shard_map/student_side/pallas_call | solution.py:574
  116.1 4.1 %columns.3.refs_0_ = f32[4,64,128]{2,1,0:T(8,128)} custom-call(f32[8,8,128]{2,1,0:T(8,128)} %all_to_all.56.sums_ref, f32[8,128]{1,0:T(8,128)} %get-tuple-element.32.factor_ref, f32[8,128]{1,0:T(8,128)} %get-tuple-element.42.token_ref, bf16[256,8192]{1,0:T(8,128)(2,1)} %get-tuple-element.30.exp_ref), custom_call_target="tpu_custom_call" | custom-call | flops 4194304 | bytes 4194304 | tf_op jit(solution)/shard_map/columns/pallas_call | solution.py:616
  120.2 17.6 %all-to-all-done.1.all_ref = bf16[4,256,512]{2,1,0:T(8,128)(2,1)S(1)} async-done(((bf16[4,256,512]{2,1,0:T(8,128)(2,1)}), bf16[4,256,512]{2,1,0:T(8,128)(2,1)S(1)}, u32[]{:S(2)}, u32[]{:S(2)}) %all-to-all-start.1) | async-done | bytes 1048608 | tf_op jit(solution)/shard_map/all_to_all | solution.py:474
  141.1 5.5 %student_side.8 = (f32[128,8192]{1,0:T(8,128)}, f32[8,128]{1,0:T(8,128)}) custom-call(s32[2]{0:T(128)} %pad_add_fusion.place_ref, bf16[4,256,512]{2,1,0:T(8,128)(2,1)} %copy-done, f32[4,72,128]{2,1,0:T(8,128)} %all_to_all.55.cols_ref.logs_ref, f32[8,128]{1,0:T(8,128)} %get-tuple-element.32.factor_ref, ...), custom_call_target="tpu_custom_call", output_to_operand_aliasing={{0}: (8, {})} | custom-call | flops 2684354560 | bytes 2097152 | tf_op jit(solution)/shard_map/student_side/pallas_call | solution.py:574
  147.6 17.9 %last_rows.1 = (bf16[768,8192]{1,0:T(8,128)(2,1)}, f32[64,128]{1,0:T(8,128)}, bf16[8,80,512]{2,1,0:T(8,128)(2,1)}) custom-call(s32[2]{0:T(128)} %pad_add_fusion.place_ref, bf16[4,256,512]{2,1,0:T(8,128)(2,1)} %copy-done.1, f32[4,72,128]{2,1,0:T(8,128)} %all_to_all.55.cols_ref.logs_ref, f32[4,64,128]{2,1,0:T(8,128)} %copy-done.5, ...), custom_call_target="tpu_custom_call" | custom-call | flops 8589934592 | bytes 12582912 | tf_op jit(solution)/shard_map/last_rows/pallas_call | solution.py:635
  165.5 15.3 %all_to_all.57.message_ref = bf16[8,80,512]{2,1,0:T(8,128)(2,1)} all-to-all(bf16[8,80,512]{2,1,0:T(8,128)(2,1)} %get-tuple-element.46.refs_0_), channel_id=1, replica_groups=mesh['proto'=8,'batch'=4] {'proto'}, dimensions={0} | all-to-all | bytes 1310720 | tf_op jit(solution)/shard_map/all_to_all | solution.py:474
  183.2 10.2 %all_to_all.58 = f32[4,8,128]{2,1,0:T(8,128)S(1)} all-to-all(f32[4,8,128]{2,1,0:T(8,128)} %get-tuple-element.52), channel_id=1, replica_groups=mesh['proto'=8,'batch'=4] {'batch'}, dimensions={0} | all-to-all | bytes 32768 | tf_op jit(solution)/shard_map/all_to_all | solution.py:474
  196.9 5.5 %student_side.9 = (f32[128,8192]{1,0:T(8,128)}, f32[8,128]{1,0:T(8,128)}) custom-call(s32[2]{0:T(128)} %pad_add_fusion.place_ref, bf16[4,256,512]{2,1,0:T(8,128)(2,1)} %copy-done, f32[4,72,128]{2,1,0:T(8,128)} %all_to_all.55.cols_ref.logs_ref, f32[8,128]{1,0:T(8,128)} %get-tuple-element.32.factor_ref, ...), custom_call_target="tpu_custom_call", output_to_operand_aliasing={{0}: (8, {})} | custom-call | flops 2684354560 | bytes 2097152 | tf_op jit(solution)/shard_map/student_side/pallas_call | solution.py:574
  202.4 11.6 %weight_grads.1 = bf16[128,8192]{1,0:T(8,128)(2,1)} custom-call(bf16[256,8192]{1,0:T(8,128)(2,1)} %get-tuple-element.30.exp_ref, bf16[768,8192]{1,0:T(8,128)(2,1)} %get-tuple-element.45.prob_ref, bf16[128,1024]{1,0:T(8,128)(2,1)} %features.1.feat_ref, f32[128,8192]{1,0:T(8,128)} %get-tuple-element.48.part_ref, f32[64,128]{1,0:T(8,128)} %get-tuple-element.49.scale_ref, ...), custom_call_target="tpu_custom_call" | custom-call | flops 2147483648 | bytes 12582912 | tf_op jit(solution)/shard_map/weight_grads/pallas_call | solution.py:679
  (26 shorter events, 26.6 us)
Async XLA Ops:
  15.7 10.0 %all-to-all-start = ((f32[8,8,128]{2,1,0:T(8,128)}), f32[8,8,128]{2,1,0:T(8,128)S(1)}, u32[]{:S(2)}, u32[]{:S(2)}) async-start(f32[8,8,128]{2,1,0:T(8,128)} %get-tuple-element.31), calls=%async_computation | async-start | bytes 65536 | tf_op jit(solution)/shard_map/all_to_all | solution.py:474
  25.7 0.6 copy-start.3
  42.0 28.1 %all-to-all-start.4 = ((bf16[4,256,512]{2,1,0:T(8,128)(2,1)}), bf16[4,256,512]{2,1,0:T(8,128)(2,1)S(1)}, u32[]{:S(2)}, u32[]{:S(2)}) async-start(bf16[4,256,512]{2,1,0:T(8,128)(2,1)} %get-tuple-element.37), calls=%async_computation.4 | async-start | bytes 2097152 | tf_op jit(solution)/shard_map/all_to_all | solution.py:474
  70.1 3.4 %copy-start = (bf16[4,256,512]{2,1,0:T(8,128)(2,1)}, bf16[4,256,512]{2,1,0:T(8,128)(2,1)S(1)}, u32[]{:S(2)}) copy-start(bf16[4,256,512]{2,1,0:T(8,128)(2,1)S(1)} %all-to-all-done.4.all_ref) | copy-start | bytes 3145732
  70.1 9.7 %all-to-all-start.3 = ((f32[8,8,128]{2,1,0:T(8,128)}), f32[8,8,128]{2,1,0:T(8,128)S(1)}, u32[]{:S(2)}, u32[]{:S(2)}) async-start(f32[8,8,128]{2,1,0:T(8,128)} %rows.2.refs_0_), calls=%async_computation.3 | async-start | bytes 65536 | tf_op jit(solution)/shard_map/all_to_all | solution.py:474
  79.8 0.6 copy-start.4
  84.5 9.8 %all-to-all-start.5 = ((f32[4,64,128]{2,1,0:T(8,128)}), f32[4,64,128]{2,1,0:T(8,128)S(1)}, u32[]{:S(2)}, u32[]{:S(2)}) async-start(f32[4,64,128]{2,1,0:T(8,128)} %columns.2.refs_0_), calls=%async_computation.5 | async-start | bytes 262144 | tf_op jit(solution)/shard_map/all_to_all | solution.py:474
  94.3 0.7 copy-start.2
  108.0 29.7 %all-to-all-start.1 = ((bf16[4,256,512]{2,1,0:T(8,128)(2,1)}), bf16[4,256,512]{2,1,0:T(8,128)(2,1)S(1)}, u32[]{:S(2)}, u32[]{:S(2)}) async-start(bf16[4,256,512]{2,1,0:T(8,128)(2,1)} %get-tuple-element.34), calls=%async_computation.1 | async-start | bytes 2097152 | tf_op jit(solution)/shard_map/all_to_all | solution.py:474
  137.7 8.8 %copy-start.1 = (bf16[4,256,512]{2,1,0:T(8,128)(2,1)}, bf16[4,256,512]{2,1,0:T(8,128)(2,1)S(1)}, u32[]{:S(2)}) copy-start(bf16[4,256,512]{2,1,0:T(8,128)(2,1)S(1)} %all-to-all-done.1.all_ref) | copy-start | bytes 3145732
  137.7 9.2 %all-to-all-start.7 = ((f32[4,64,128]{2,1,0:T(8,128)}), f32[4,64,128]{2,1,0:T(8,128)S(1)}, u32[]{:S(2)}, u32[]{:S(2)}) async-start(f32[4,64,128]{2,1,0:T(8,128)} %columns.3.refs_0_), calls=%async_computation.7 | async-start | bytes 262144 | tf_op jit(solution)/shard_map/all_to_all | solution.py:474
  147.0 0.7 copy-start.5
  193.4 21.9 %all-to-all-start.9 = ((f32[8,32,512]{2,1,0:T(8,128)}), f32[8,32,512]{2,1,0:T(8,128)S(1)}, u32[]{:S(2)}, u32[]{:S(2)}) async-start(f32[8,32,512]{2,1,0:T(8,128)} %get-tuple-element.51), calls=%async_computation.9 | async-start | bytes 1048576 | tf_op jit(solution)/shard_map/all_to_all | solution.py:474

commit v4 on v0

v4 whole, which is shorter than its diff:
```python
import functools
import math

import jax
import jax.numpy as jnp
from jax import lax
from jax.experimental import pallas as pl
from jax.experimental.pallas import tpu as pltpu
from jax.sharding import PartitionSpec as P

SWEEPS = 3
TEMP_TEACHER = 0.04
TEMP_STUDENT = 0.1
LOG2E = math.log2(math.e)
SCALE_TEACHER = LOG2E / TEMP_TEACHER
SCALE_STUDENT = LOG2E / TEMP_STUDENT
LANES = 128
WIDE = 1024
F32 = jnp.float32
BF16 = jnp.bfloat16


def unit_rows(values):
    wide = values.astype(F32)
    length = jnp.sqrt(jnp.sum(wide * wide, axis=-1, keepdims=True) + 1e-06)
    return wide / length, length


def diagonal():
    shape = (LANES, LANES)
    return lax.broadcasted_iota(jnp.int32, shape, 0) == lax.broadcasted_iota(jnp.int32, shape, 1)


def to_column(row):
    spread = jnp.where(diagonal(), jnp.broadcast_to(row, (LANES, LANES)), 0.0)
    return jnp.sum(spread, axis=1, keepdims=True)


def to_row(column):
    spread = jnp.where(diagonal(), jnp.broadcast_to(column, (LANES, LANES)), 0.0)
    return jnp.sum(spread, axis=0, keepdims=True)


def spread_rows(ref, rows):
    for a in range(rows.shape[0]):
        ref[a * LANES : (a + 1) * LANES, :] = jnp.broadcast_to(
            to_column(rows[a : a + 1, :]), (LANES, LANES)
        )


def pack_rows(ref, columns):
    for a in range(columns.shape[0] // LANES):
        ref[a : a + 1, :] = to_row(columns[a * LANES : (a + 1) * LANES, :])


def lane_tiles(values):
    return [values[:, t * LANES : (t + 1) * LANES] for t in range(values.shape[1] // LANES)]


def fold(values):
    return functools.reduce(jnp.add, lane_tiles(values))


def column_sums(values):
    rows, cols = values.shape
    return jnp.sum(values.reshape(rows // 8, 8, cols), axis=0)


def nt_dot(a, b):
    return lax.dot_general(a, b, (((1,), (1,)), ((), ())), preferred_element_type=F32)


def add_up(values):
    return functools.reduce(jnp.add, values)


def repeat(out_ref):
    for p in range(1, out_ref.shape[0]):
        out_ref[p] = out_ref[0]


def w_loads(w_hbm, w_ref, sems, first=0):
    return [
        pltpu.make_async_copy(
            w_hbm.at[:, (first + k) * WIDE : (first + k + 1) * WIDE],
            w_ref.at[:, k * WIDE : (k + 1) * WIDE],
            sems.at[k],
        )
        for k in range(w_ref.shape[1] // WIDE)
    ]


def stats_kernel(
    t_ref, s_ref, w_hbm, t_exp, s_exp, out_ref, w_ref, unit, logits, top, total, w_sem
):
    chunk = 512
    cols = w_ref.shape[1]
    pieces = [slice(c, c + chunk) for c in range(0, cols, chunk)]
    quarter = out_ref.shape[1] // 4
    outs = (t_exp, s_exp)
    scales = (SCALE_TEACHER, SCALE_STUDENT)
    loads = w_loads(w_hbm, w_ref, w_sem)
    for load in loads:
        load.start()
    for which, ref in enumerate((t_ref, s_ref)):
        unit[which] = unit_rows(ref[...])[0].astype(BF16)
    top[...] = jnp.full(top.shape, -1e30, F32)
    total[...] = jnp.zeros(total.shape, F32)

    def product(which, here):
        values = jnp.dot(unit[which], w_ref[:, here], preferred_element_type=F32) * scales[which]
        top[which] = functools.reduce(jnp.maximum, lane_tiles(values), top[which])
        return values

    def peak(which):
        return jnp.max(top[which], axis=1, keepdims=True)

    def raised(which, here, shift):
        values = jnp.exp2(logits[:, here] - shift)
        outs[which][:, here] = values.astype(BF16)
        total[which] += fold(values)

    for here in pieces:
        if here.start % WIDE == 0:
            loads[here.start // WIDE].wait()
        logits[:, here] = product(0, here)
    peaks = [peak(0)]
    shift = jnp.broadcast_to(peaks[0], (peaks[0].shape[0], chunk))
    for here in pieces:
        values = product(1, here)
        raised(0, here, shift)
        logits[:, here] = values
    peaks.append(peak(1))
    shift = jnp.broadcast_to(peaks[1], (peaks[1].shape[0], chunk))
    for here in pieces:
        raised(1, here, shift)
    for which in range(2):
        sums = jnp.sum(total[which], axis=1, keepdims=True)
        for k, column in enumerate((peaks[which], sums)):
            first = (2 * which + k) * quarter
            pack_rows(out_ref.at[0, first : first + quarter], column)
    repeat(out_ref)


def merged(stats_ref, which):
    parts, height, _ = stats_ref.shape
    quarter = height // 4
    first = 2 * which * quarter
    tops = [stats_ref[p, first : first + quarter, :] for p in range(parts)]
    top = functools.reduce(jnp.maximum, tops)
    sums = [
        stats_ref[p, first + quarter : first + 2 * quarter, :] * jnp.exp2(tops[p] - top)
        for p in range(parts)
    ]
    return top + jnp.log2(add_up(sums))


def column_pass(exp_ref, weight, out_ref):
    rows, cols = exp_ref.shape
    for a in range(0, cols, WIDE):
        sums = jnp.zeros((8, WIDE), F32)
        for g in range(0, rows, 16):
            shift = weight[g : g + 16, :]
            tiles = lane_tiles(exp_ref[g : g + 16, a : a + WIDE].astype(F32))
            sums = sums + column_sums(jnp.concatenate([tile * shift for tile in tiles], axis=1))
        sums = jnp.sum(sums, axis=0, keepdims=True)
        block = jnp.concatenate(lane_tiles(sums), axis=0)
        for g in range(out_ref.shape[0]):
            out_ref[g, a // LANES : (a + WIDE) // LANES, :] = block


def first_column_kernel(place_ref, stats_ref, exp_ref, *refs):
    factor_ref, out_ref, weight = refs[-3:]
    quarter = stats_ref.shape[1] // 4
    height = out_ref.shape[1] - 8
    own = stats_ref[pl.ds(place_ref[1], 1)][0]
    factor_ref[...] = jnp.zeros(factor_ref.shape, F32)
    logs = jnp.zeros((8, LANES), F32)
    rows = []
    for which in range(2):
        log_sum = merged(stats_ref, which)
        here = slice(which * quarter, (which + 1) * quarter)
        factor_ref[here, :] = jnp.exp2(
            own[2 * which * quarter : (2 * which + 1) * quarter, :] - log_sum
        )
        rows.append(log_sum)
    rows.append(jnp.zeros((8 - 2 * quarter, LANES), F32))
    logs = jnp.concatenate(rows, axis=0)
    for g in range(out_ref.shape[0]):
        out_ref[g, height:, :] = logs
    spread_rows(weight, factor_ref[:quarter, :])
    column_pass(exp_ref, weight, out_ref)


def column_kernel(sums_ref, factor_ref, exp_ref, *refs):
    out_ref, weight = refs[-2:]
    quarter = weight.shape[0] // LANES
    scale = 1.0 / add_up([sums_ref[p, :quarter, :] for p in range(sums_ref.shape[0])])
    spread_rows(weight, scale * factor_ref[:quarter, :])
    column_pass(exp_ref, weight, out_ref)


def column_scales(cols_ref, height):
    return 1.0 / add_up([cols_ref[g, :height, :] for g in range(cols_ref.shape[0])])


def row_sums(ref, scales, step):
    sums = []
    for g in range(0, ref.shape[0], step):
        total = jnp.zeros((step, LANES), F32)
        for t, tile in enumerate(lane_tiles(ref[g : g + step, :].astype(F32))):
            total = total + tile * scales[t : t + 1, :]
        sums.append(jnp.sum(total, axis=1, keepdims=True))
    return jnp.concatenate(sums, axis=0)


def row_kernel(cols_ref, factor_ref, exp_ref, *refs):
    out_ref, scales = refs[-2:]
    scales[...] = column_scales(cols_ref, scales.shape[0])
    quarter = exp_ref.shape[0] // LANES
    out_ref[0] = jnp.zeros(out_ref.shape[1:], F32)
    pack_rows(out_ref.at[0, :quarter], row_sums(exp_ref, scales, 32))
    out_ref[0, :quarter, :] = out_ref[0, :quarter, :] * factor_ref[:quarter, :]
    repeat(out_ref)


def own_back_kernel(protos, factor_ref, exp_ref, w_hbm, back_ref, w_ref, back, w_sem):
    loads = w_loads(w_hbm, w_ref, w_sem)
    for load in loads:
        load.start()
    back[...] = jnp.zeros(back.shape, F32)
    for k, load in enumerate(loads):
        load.wait()
        here = slice(k * WIDE, (k + 1) * WIDE)
        back[...] += nt_dot(exp_ref[:, here], w_ref[:, here])
    quarter = back.shape[0] // LANES
    for a in range(quarter):
        here = slice(a * LANES, (a + 1) * LANES)
        factor = to_column(factor_ref[quarter + a : quarter + a + 1, :] * protos)
        back_ref[here, :] = (back[here, :] * factor).astype(BF16)


def relative(place_ref, g, groups):
    return pl.ds(lax.rem(place_ref[0] + g, groups), 1)


def relative_logs(place_ref, logs_ref, lse, which, shift=0.0):
    groups = logs_ref.shape[0]
    own = lse.shape[0] // (groups - 1)
    quarter = own // LANES
    height = logs_ref.shape[1] - 8
    for g in range(1, groups):
        there = logs_ref[relative(place_ref, g, groups)][0]
        first = height + which * quarter
        spread_rows(lse.at[(g - 1) * own : g * own], there[first : first + quarter, :] - shift)


def student_rows_kernel(log_protos, place_ref, logs_ref, factor_ref, own_ref, *refs):
    groups = logs_ref.shape[0]
    raw, (unit_ref, lse_ref, feat_ref, scaled_ref, turned) = refs[: groups - 1], refs[-5:]
    own = own_ref.shape[0]
    quarter, feats = own // LANES, feat_ref.shape[0]
    for g in range(groups):
        half = unit_rows((raw[g - 1] if g else own_ref)[...])[0].astype(BF16)
        if g:
            unit_ref[(g - 1) * own : g * own, :] = half
        half = half.astype(F32)
        for a in range(0, own, LANES):
            first = g * own + a
            turned[:, first : first + LANES] = jnp.transpose(half[a : a + LANES, :]).astype(BF16)
    feat = turned[pl.ds(pl.multiple_of(place_ref[0] * feats, feats), feats), :]
    feat_ref[...] = feat
    for a in range(quarter):
        lanes = slice(a * LANES, (a + 1) * LANES)
        factor = factor_ref[quarter + a : quarter + a + 1, :] * 2.0**log_protos
        scaled_ref[:, lanes] = (feat[:, lanes].astype(F32) * factor).astype(BF16)
    relative_logs(place_ref, logs_ref, lse_ref, 1, log_protos)


def probabilities(unit, own, w, lse, scale, use):
    for g in range(unit.shape[0] // own):
        here = slice(g * own, (g + 1) * own)
        for n in range(0, WIDE, 512):
            logits = jnp.dot(unit[here, :], w[:, n : n + 512], preferred_element_type=F32)
            shift = lse[here, :]
            use(g, n, [jnp.exp2(tile * scale - shift) for tile in lane_tiles(logits)])


def student_kernel(first, count, unit, lse, feat_ref, scaled_ref, exp_ref, w_hbm, *refs):
    grad_ref, token_ref, prob, w_ref, w_sem = refs[-5:]
    own = exp_ref.shape[0]
    loads = w_loads(w_hbm, w_ref, w_sem, first)
    for load in loads:
        load.start()
    token_ref[...] = jnp.zeros(token_ref.shape, F32)
    for k, load in enumerate(loads):
        load.wait()
        here = slice((first + k) * WIDE, (first + k + 1) * WIDE)
        slot = prob.at[k % 2]

        def use(g, n, tiles):
            for t, tile in enumerate(tiles):
                lanes = slice(n + t * LANES, n + (t + 1) * LANES)
                slot[g * own : (g + 1) * own, lanes] = tile.astype(BF16)

        probabilities(unit, own, w_ref.at[:, k * WIDE : (k + 1) * WIDE], lse, SCALE_STUDENT, use)
        grad_ref[:, here] = jnp.dot(
            scaled_ref[...], exp_ref[:, here], preferred_element_type=F32
        ) + jnp.dot(feat_ref[:, own:], slot[...], preferred_element_type=F32)


def as_three(value):
    high = value.astype(BF16)
    rest = value - high.astype(F32)
    middle = rest.astype(BF16)
    return high, middle, (rest - middle.astype(F32)).astype(BF16)


def last_kernel(groups, place_ref, logs_ref, cols_ref, factor_ref, own_ref, student_ref, exp_ref, w_hbm, *refs):
    raw = refs[: groups - 1]
    prob_ref, scale_ref, out_ref, unit, lse, rows, back, scaled, sums, w_ref, w_sem = refs[-11:]
    own, others = exp_ref.shape[0], prob_ref.shape[0]
    tiles = (own + others) // LANES
    quarter = own // LANES
    loads = w_loads(w_hbm, w_ref, w_sem)
    for load in loads:
        load.start()
    scale_ref[...] = column_scales(cols_ref, scale_ref.shape[0])
    rows[...] = jnp.zeros(rows.shape, F32)
    back[...] = jnp.zeros(back.shape, F32)
    relative_logs(place_ref, logs_ref, lse, 0)
    for g in range(groups - 1):
        unit[g * own : (g + 1) * own, :] = unit_rows(raw[g][...])[0].astype(BF16)

    @pl.loop(0, len(loads))
    def _(k):
        here = pl.ds(pl.multiple_of(k * WIDE, WIDE), WIDE)
        pltpu.make_async_copy(w_hbm.at[:, here], w_ref.at[:, here], w_sem.at[k]).wait()
        scales = scale_ref[pl.ds(pl.multiple_of(k * (WIDE // LANES), 8), WIDE // LANES), :]

        def use(g, n, tiles):
            first = n // LANES
            for t, tile in enumerate(tiles):
                lanes = pl.ds(pl.multiple_of(k * WIDE + n + t * LANES, LANES), LANES)
                prob_ref[g * own : (g + 1) * own, lanes] = tile.astype(BF16)
            tiles = [
                tile * scales[first + t : first + t + 1, :] for t, tile in enumerate(tiles)
            ]
            rows[g * own : (g + 1) * own, :] += add_up(tiles)
            if g == groups // 2 - 1:
                for t, tile in enumerate(tiles):
                    scaled[:, n + t * LANES : n + (t + 1) * LANES] = tile.astype(BF16)

        probabilities(unit, own, w_ref.at[:, here], lse, SCALE_TEACHER, use)
        back[...] += nt_dot(scaled[...], w_ref[:, here])

    sums[...] = jnp.zeros(sums.shape, F32)
    pack_rows(sums.at[:quarter], row_sums(exp_ref, scale_ref, 32))
    sums[:quarter, :] = sums[:quarter, :] * factor_ref[:quarter, :]
    pack_rows(sums.at[quarter:tiles], jnp.sum(rows[...], axis=1, keepdims=True))
    half = unit_rows(own_ref[...])[0].astype(BF16).astype(F32)
    inner = jnp.sum(half * back[...], axis=1, keepdims=True)
    pack_rows(sums.at[tiles : tiles + quarter], inner)
    parts = out_ref.shape[0]
    share = own // parts
    terms = list(as_three(sums[...]))
    terms.append(jnp.zeros((sums.shape[0], out_ref.shape[2] - 3 * LANES), BF16))
    terms = jnp.concatenate(terms, axis=1)
    for p in range(parts):
        here = slice(p * share, (p + 1) * share)
        out_ref[p] = jnp.concatenate(
            [student_ref[here, :], back[here, :].astype(BF16), terms], axis=0
        )


def total_sums(message_ref, first):
    parts = message_ref.shape[0]
    each = [
        add_up([t.astype(F32) for t in lane_tiles(message_ref[p, first:, : 3 * LANES])[::-1]])
        for p in range(parts)
    ]
    return add_up(each)


def rows_kernel(tiles, protos, place_ref, s_ref, message_ref, logs_ref, *refs):
    out_ref, loss_ref, sums_ref, weight = refs[-4:]
    parts = message_ref.shape[0]
    share, own = out_ref.shape[1], weight.shape[0]
    quarter = own // LANES
    first = tiles // 2
    totals = total_sums(message_ref, 2 * share)
    sums_ref[...] = totals
    scale = 1.0 / totals[first : first + quarter, :]
    spread_rows(weight, scale)
    mine = pl.ds(pl.multiple_of(place_ref[1] * share, share), share)
    total = add_up([message_ref[p, :share, :].astype(F32) for p in range(parts)])
    paired = add_up([message_ref[p, share : 2 * share, :].astype(F32) for p in range(parts)])
    total = total - paired * (weight[mine, :1] * protos)
    unit, length = unit_rows(s_ref[mine, :])
    out_ref[0] = (total - unit * jnp.sum(unit * total, axis=-1, keepdims=True)) / length
    repeat(out_ref)
    height = logs_ref.shape[1] - 8
    logs = logs_ref[pl.ds(place_ref[0], 1)][0][height + quarter : height + 2 * quarter, :]
    terms = logs / LOG2E - totals[tiles : tiles + quarter, :] * scale / TEMP_STUDENT
    loss_ref[...] = jnp.broadcast_to(jnp.sum(terms), loss_ref.shape)


def grad_kernel(protos, exp_ref, prob_ref, feat_ref, part_ref, scale_ref, sums_ref, factor_ref, out_hbm, scaled, out, sem):
    own = exp_ref.shape[0]
    tiles = (own + prob_ref.shape[0]) // LANES
    rows = protos / sums_ref[:tiles, :]
    for a in range(tiles):
        other = (a + tiles // 2) % tiles
        feat = feat_ref[:, other * LANES : (other + 1) * LANES].astype(F32)
        row = rows[a : a + 1, :]
        if a < own // LANES:
            row = row * factor_ref[a : a + 1, :]
        scaled[:, a * LANES : (a + 1) * LANES] = (feat * row).astype(BF16)
    copies = []
    for k in range(out.shape[1] // WIDE):
        here = slice(k * WIDE, (k + 1) * WIDE)
        paired = jnp.dot(scaled[:, :own], exp_ref[:, here], preferred_element_type=F32)
        paired = paired + jnp.dot(scaled[:, own:], prob_ref[:, here], preferred_element_type=F32)
        for t, tile in enumerate(lane_tiles(paired)):
            lanes = slice(k * WIDE + t * LANES, k * WIDE + (t + 1) * LANES)
            scale = scale_ref[lanes.start // LANES : lanes.stop // LANES, :]
            out[:, lanes] = (part_ref[:, lanes] - tile * scale).astype(BF16)
        copies.append(pltpu.make_async_copy(out.at[:, here], out_hbm.at[:, here], sem.at[k]))
        copies[-1].start()
    for copy in copies:
        copy.wait()


SMEM = pl.BlockSpec(memory_space=pltpu.SMEM)
VMEM = pl.BlockSpec(memory_space=pltpu.VMEM)
ANY = pl.BlockSpec(memory_space=pl.ANY)


def params(nbytes):
    return pltpu.CompilerParams(vmem_limit_bytes=int(nbytes) + 8 * 2**20)


def cost(flops, nbytes, exps=0):
    return pl.CostEstimate(flops=int(flops), bytes_accessed=int(nbytes), transcendentals=int(exps))


def exchange(value, axis):
    return lax.all_to_all(value, axis, 0, 0)


def following(value, axis):
    n = lax.axis_size(axis)
    return [lax.ppermute(value, axis, [(i, (i - s) % n) for i in range(n)]) for s in range(1, n)]


def tree_sum(value, axis):
    n = lax.axis_size(axis)
    values = [value] + [
        lax.ppermute(value, axis, [(i, i ^ s) for i in range(n)]) for s in range(1, n)
    ]
    while len(values) > 1:
        values = [a + b for a, b in zip(values[::2], values[1::2])]
    return values[0]


def local(teacher_feats, student_feats, proto_weight):
    parts, groups = lax.axis_size("proto"), lax.axis_size("batch")
    own, width = teacher_feats.shape
    local_protos = proto_weight.shape[1]
    rows = own * groups
    others = rows - own
    protos = local_protos * parts
    feats = width // groups
    share = own // parts
    tiles = rows // LANES
    height = local_protos // LANES
    chunks = local_protos // WIDE
    place = jnp.stack([lax.axis_index("batch"), lax.axis_index("proto")]).astype(jnp.int32)
    struct = jax.ShapeDtypeStruct
    weight_bytes = 2 * width * local_protos
    exp_bytes = 2 * own * local_protos
    others_bytes = 2 * others * local_protos
    spread = pltpu.VMEM((own, LANES), F32)
    w_buffer = pltpu.VMEM((width, local_protos), BF16)
    w_sems = pltpu.SemaphoreType.DMA((chunks,))
    weight_here = pltpu.with_memory_space_constraint(proto_weight, pltpu.HBM)
    token = struct((8, LANES), F32)

    s_all = following(student_feats, "batch")
    t_all = following(teacher_feats, "batch")

    exps = pltpu.VMEM((own, local_protos), BF16)
    t_exp, s_exp, stats = pl.pallas_call(
        stats_kernel,
        in_specs=[VMEM, VMEM, ANY],
        out_specs=[VMEM, VMEM, VMEM],
        out_shape=[exps, exps, struct((parts, 4 * own // LANES, LANES), F32)],
        scratch_shapes=[
            w_buffer,
            pltpu.VMEM((2, own, width), BF16),
            pltpu.VMEM((own, local_protos), F32),
            pltpu.VMEM((2, own, LANES), F32),
            pltpu.VMEM((2, own, LANES), F32),
            w_sems,
        ],
        compiler_params=params(weight_bytes + 2 * exp_bytes),
        cost_estimate=cost(4 * own * width * local_protos, weight_bytes),
        name="own_rows",
    )(teacher_feats, student_feats, weight_here)
    stats = exchange(stats, "proto")

    def pinned(value):
        return pltpu.with_memory_space_constraint(value, pltpu.VMEM)

    first_shape = (groups, height + 8, LANES)
    factor, cols = pl.pallas_call(
        first_column_kernel,
        in_specs=[SMEM, VMEM, VMEM] + [ANY] * (groups - 1),
        out_specs=[VMEM, VMEM],
        out_shape=[token, struct(first_shape, F32)],
        scratch_shapes=[spread],
        compiler_params=params(0),
        cost_estimate=cost(2 * own * local_protos, exp_bytes),
        name="first_columns",
    )(place, stats, pinned(t_exp), *s_all)

    back_student = pl.pallas_call(
        functools.partial(own_back_kernel, float(protos)),
        in_specs=[VMEM, VMEM, ANY],
        out_specs=VMEM,
        out_shape=struct((own, width), BF16),
        scratch_shapes=[w_buffer, pltpu.VMEM((own, width), F32), w_sems],
        compiler_params=params(weight_bytes),
        cost_estimate=cost(2 * own * width * local_protos, weight_bytes),
        name="own_back",
    )(factor, pinned(s_exp), weight_here)
    cols = exchange(cols, "batch")
    logs = cols

    done = [back_student]
    counts = [1, 2, 1, 2, 2]
    grad_part, first = None, 0
    unit = lse = feat = scaled = None
    for turn in range(SWEEPS - 1):
        sums = pl.pallas_call(
            row_kernel,
            in_specs=[VMEM] * 3 + [ANY] * len(done),
            out_specs=VMEM,
            out_shape=struct((parts, 8, LANES), F32),
            scratch_shapes=[pltpu.VMEM((height, LANES), F32)],
            compiler_params=params(0),
            cost_estimate=cost(2 * own * local_protos, exp_bytes),
            name="rows",
        )(cols, factor, pinned(t_exp), *done)
        if turn == 0:
            unit, lse, feat, scaled = pl.pallas_call(
                functools.partial(student_rows_kernel, math.log2(protos)),
                in_specs=[SMEM, VMEM, VMEM, VMEM] + [VMEM] * (groups - 1) + [ANY],
                out_specs=[VMEM] * 4,
                out_shape=[
                    struct((others, width), BF16),
                    struct((others, LANES), F32),
                    struct((feats, rows), BF16),
                    struct((feats, own), BF16),
                ],
                scratch_shapes=[pltpu.VMEM((width, rows), BF16)],
                compiler_params=params(2 * rows * width),
                cost_estimate=cost(8 * rows * width, 2 * rows * width),
                name="student_rows",
            )(place, logs, factor, student_feats, *s_all, sums)

        def student_piece(turn, before):
            nonlocal grad_part, first
            count = counts[turn] * chunks // 8
            if turn == 2 * (SWEEPS - 1):
                count = chunks - first
            prior = [] if grad_part is None else [pinned(grad_part)]
            grad_part, token_out = pl.pallas_call(
                functools.partial(student_kernel, first, count),
                in_specs=[VMEM] * 5 + [ANY] + [ANY] + [VMEM] * len(prior),
                out_specs=[VMEM, VMEM],
                out_shape=[pltpu.VMEM((feats, local_protos), F32), token],
                scratch_shapes=[
                    pltpu.VMEM((2, others, WIDE), BF16),
                    pltpu.VMEM((width, count * WIDE), BF16),
                    pltpu.SemaphoreType.DMA((count,)),
                ],
                input_output_aliases={7: 0} if prior else {},
                compiler_params=params(8 * 2**20),
                cost_estimate=cost(
                    2.5 * rows * width * WIDE * count, 2 * width * WIDE * count
                ),
                name="student_side",
            )(unit, lse, feat, scaled, pinned(s_exp), weight_here, before, *prior)
            first += count
            return token_out

        done = [student_piece(2 * turn, sums)]
        sums = exchange(sums, "proto")
        late = t_all if turn == 0 else []
        cols = pl.pallas_call(
            column_kernel,
            in_specs=[VMEM] * 3 + [ANY] * (len(done) + len(late)),
            out_specs=VMEM,
            out_shape=struct((groups, height, LANES), F32),
            scratch_shapes=[spread],
            compiler_params=params(0),
            cost_estimate=cost(2 * own * local_protos, exp_bytes),
            name="columns",
        )(sums, factor, pinned(t_exp), *done, *late)
        done = [student_piece(2 * turn + 1, cols)]
        cols = exchange(cols, "batch")

    sum_rows = -(-(tiles + own // LANES) // 16) * 16
    message_shape = (parts, 2 * share + sum_rows, width)
    prob, col_scale, message = pl.pallas_call(
        functools.partial(last_kernel, groups),
        in_specs=[SMEM] + [VMEM] * 6 + [ANY] + [VMEM] * (groups - 1) + [ANY] * len(done),
        out_specs=[VMEM] * 3,
        out_shape=[
            pltpu.VMEM((others, local_protos), BF16),
            struct((height, LANES), F32),
            struct(message_shape, BF16),
        ],
        scratch_shapes=[
            pltpu.VMEM((others, width), BF16),
            pltpu.VMEM((others, LANES), F32),
            pltpu.VMEM((others, LANES), F32),
            pltpu.VMEM((own, width), F32),
            pltpu.VMEM((own, WIDE), BF16),
            pltpu.VMEM((sum_rows, LANES), F32),
            w_buffer,
            w_sems,
        ],
        compiler_params=params(weight_bytes),
        cost_estimate=cost(2 * rows * width * local_protos, others_bytes),
        name="last_rows",
    )(
        place, logs, cols, factor, student_feats, back_student, pinned(t_exp), weight_here,
        *t_all, *done,
    )
    done = [student_piece(2 * (SWEEPS - 1), message)]
    message = exchange(message, "proto")

    grad_rows, loss_part, sums = pl.pallas_call(
        functools.partial(rows_kernel, tiles, float(protos)),
        in_specs=[SMEM] + [VMEM] * 3 + [ANY] * len(done),
        out_specs=[VMEM] * 3,
        out_shape=[struct((parts, share, width), F32), token, struct((sum_rows, LANES), F32)],
        scratch_shapes=[spread],
        compiler_params=params(0),
        name="row_grads",
    )(place, student_feats, message, logs, *done)
    grad_rows = exchange(grad_rows, "proto").reshape(own, width)
    loss = tree_sum(loss_part, "batch")[0, 0] / rows

    grad_weight = pl.pallas_call(
        functools.partial(grad_kernel, float(protos)),
        in_specs=[VMEM] * 7,
        out_specs=ANY,
        out_shape=struct((feats, local_protos), BF16),
        scratch_shapes=[
            pltpu.VMEM((feats, rows), BF16), pltpu.VMEM((feats, local_protos), BF16), w_sems,
        ],
        compiler_params=params(2 * feats * local_protos),
        cost_estimate=cost(2 * feats * rows * local_protos, others_bytes),
        name="weight_grads",
    )(pinned(t_exp), pinned(prob), feat, pinned(grad_part), col_scale, sums, factor)
    return grad_weight, grad_rows, loss


def solution(mesh):
    return jax.shard_map(
        local,
        mesh=mesh,
        in_specs=(P("batch", None), P("batch", None), P(None, "proto")),
        out_specs=(P("batch", "proto"), P("batch", None), P()),
        check_vma=False,
    )
```

time: 886 us -> 189 us (0.21)
  waiting for transfers between devices: 596 us -> 8.18 us
  blocking collectives: 154 us -> 0 us
  matrix products: 74.2 us -> 0 us
  Pallas kernels: 0 us -> 65 us
  local copies, waits for them, and re-layouts: 5.17 us -> 64.7 us
  starting transfers between devices: 0.15 us -> 46.5 us
  other arithmetic: 30.4 us -> 0.08 us
  between operations: 17.8 us -> 2.72 us
    ppermute x1 -> x9, waiting for transfers between devices: 362 us -> 2.42 us  [the longest x6 2.41 us: following(): lax.ppermute(value, axis, [(i, (i - s) % n) for i in range(n)])]
    reduce_scatter x1 -> x0, waiting for transfers between devices: 234 us -> none  [local(): lax.psum_scatter(lax.dot_general(student_half, dlogits, (((0,), (0,)), ((...]
    psum x8 -> x0, blocking collectives: 139 us -> none  [the longest x3 51.1 us: local(): lax.psum(jnp.dot(row_scale, prob, precision=lax.Precision.HIGHEST).astype...]
    dot_general x10 -> x0, matrix products: 74.2 us -> none  [the longest x3 26.7 us: local(): jnp.dot(prob, col_scale, precision=lax.Precision.HIGHEST)]
    pallas_call x0 -> x16, Pallas kernels: none -> 65 us  [the longest x1 18.7 us: local(): pl.pallas_call(functools.partial(last_kernel, groups), in_specs=[SMEM] +...]
    unnamed x14 -> x59, local copies, waits for them, and re-layouts: 5.17 us -> 64.2 us
    all_to_all x0 -> x8, starting transfers between devices: none -> 30 us  [exchange(): return lax.all_to_all(value, axis, 0, 0)]
    ppermute x1 -> x9, starting transfers between devices: 0.07 us -> 16.4 us  [the longest x6 11.9 us: following(): lax.ppermute(value, axis, [(i, (i - s) % n) for i in range(n)])]
  transfers between devices with their start and end apart: 3 -> 17, of which waited for: 3 -> 3; matrix products, arithmetic and copies ran while one was open for 2% -> 0% of each run, Pallas kernels for 0% -> 20%
where the time goes in v4:
time: 189 us; the launch traced here: 187 us
  Pallas kernels  65 us (34%)
  local copies, waits for them, and re-layouts  64.7 us (34%)
  starting transfers between devices  46.5 us (25%)
  waiting for transfers between devices  8.18 us (4%)
  between operations  2.72 us (1%)
    unnamed x59, local copies, waits for them, and re-layouts  64.2 us
    all_to_all x8, starting transfers between devices, exchange(): return lax.all_to_all(value, axis, 0, 0)  30 us
    pallas_call x1, Pallas kernels, local(): pl.pallas_call(functools.partial(last_kernel, groups), in_specs=[SMEM] +...  18.7 us
    pallas_call x5, Pallas kernels, student_piece(): pl.pallas_call(functools.partial(student_kernel, first, count), in_specs=...  16.4 us
    ppermute x6, starting transfers between devices, following(): lax.ppermute(value, axis, [(i, (i - s) % n) for i in range(n)])  11.9 us
    pallas_call x1, Pallas kernels, local(): pl.pallas_call(stats_kernel, in_specs=[VMEM, VMEM, ANY], out_specs=[VMEM,...  10.4 us
    all_to_all x8, waiting for transfers between devices, exchange(): return lax.all_to_all(value, axis, 0, 0)  5.76 us
    ppermute x3, starting transfers between devices, tree_sum(): lax.ppermute(value, axis, [(i, i ^ s) for i in range(n)])  4.51 us
  transfers between devices with their start and end apart: 17, of which 3 were waited for; matrix products, arithmetic and copies ran while one was open for 0% of the time, Pallas kernels for 20%

profile of v4, /device:TPU:0, one launch (start us, length us, event | category | flops | bytes accessed | tf_op | source)
XLA Modules:
  0.0 187.2 jit_solution(5167196267092371650)
XLA Ops:
  0.6 3.1 %collective-permute-start.2 = (bf16[256,512]{1,0:T(8,128)(2,1)}, bf16[256,512]{1,0:T(8,128)(2,1)S(1)}, u32[]{:S(2)}, u32[]{:S(2)}) collective-permute-start(bf16[256,512]{1,0:T(8,128)(2,1)} %s_ref.3), channel_id=1, source_target_pairs={{0,1},{1,2},{2,3},{3,0},{4,5},{5,6},{6,7},{7,4},{8,9},{9,10},{10,1... | collective-permute-start | bytes 786440 | tf_op jit(solution)/shard_map/ppermute | solution.py:453
  3.7 2.6 %collective-permute-start.1 = (bf16[256,512]{1,0:T(8,128)(2,1)}, bf16[256,512]{1,0:T(8,128)(2,1)S(1)}, u32[]{:S(2)}, u32[]{:S(2)}) collective-permute-start(bf16[256,512]{1,0:T(8,128)(2,1)} %s_ref.3), channel_id=1, source_target_pairs={{0,2},{1,3},{2,0},{3,1},{4,6},{5,7},{6,4},{7,5},{8,10},{9,11},{10,... | collective-permute-start | bytes 786440 | tf_op jit(solution)/shard_map/ppermute | solution.py:453
  8.6 10.4 %own_rows.1 = (bf16[256,8192]{1,0:T(8,128)(2,1)S(1)}, bf16[256,8192]{1,0:T(8,128)(2,1)S(1)}, f32[8,8,128]{2,1,0:T(8,128)}) custom-call(bf16[256,512]{1,0:T(8,128)(2,1)} %t_ref.1, bf16[256,512]{1,0:T(8,128)(2,1)S(1)} %copy-done.27, bf16[512,8192]{1,0:T(8,128)(2,1)} %w_hbm.15), custom_call_target="tpu_custom_call" | custom-call | flops 4294967296 | bytes 8388608 | tf_op jit(solution)/shard_map/own_rows/pallas_call | solution.py:493
  23.0 3.7 %all-to-all-start = ((f32[8,8,128]{2,1,0:T(8,128)}), f32[8,8,128]{2,1,0:T(8,128)S(1)}, u32[]{:S(2)}, u32[]{:S(2)}) async-start(f32[8,8,128]{2,1,0:T(8,128)} %get-tuple-element.29), calls=%async_computation | async-start | bytes 65536 | tf_op jit(solution)/shard_map/all_to_all | solution.py:448
  26.8 4.8 %all-to-all-done.stats_ref = f32[8,8,128]{2,1,0:T(8,128)S(1)} async-done(((f32[8,8,128]{2,1,0:T(8,128)}), f32[8,8,128]{2,1,0:T(8,128)S(1)}, u32[]{:S(2)}, u32[]{:S(2)}) %all-to-all-start) | async-done | bytes 32800 | tf_op jit(solution)/shard_map/all_to_all | solution.py:448
  35.9 3.3 %all-to-all-start.1 = ((f32[4,72,128]{2,1,0:T(8,128)}), f32[4,72,128]{2,1,0:T(8,128)S(1)}, u32[]{:S(2)}, u32[]{:S(2)}) async-start(f32[4,72,128]{2,1,0:T(8,128)} %get-tuple-element.30), calls=%async_computation.1 | async-start | bytes 294912 | tf_op jit(solution)/shard_map/all_to_all | solution.py:448
  39.3 3.8 %collective-permute-start.3 = (bf16[256,512]{1,0:T(8,128)(2,1)}, bf16[256,512]{1,0:T(8,128)(2,1)S(1)}, u32[]{:S(2)}, u32[]{:S(2)}) collective-permute-start(bf16[256,512]{1,0:T(8,128)(2,1)} %t_ref.1), channel_id=1, source_target_pairs={{0,3},{1,0},{2,1},{3,2},{4,7},{5,4},{6,5},{7,6},{8,11},{9,8},{10,9... | collective-permute-start | bytes 786440 | tf_op jit(solution)/shard_map/ppermute | solution.py:453
  46.4 4.3 %own_back.1.refs_0_.student_ref = bf16[256,512]{1,0:T(8,128)(2,1)S(1)} custom-call(f32[8,128]{1,0:T(8,128)S(1)} %get-tuple-element.31.factor_ref, bf16[256,8192]{1,0:T(8,128)(2,1)S(1)} %copy-done.9, bf16[512,8192]{1,0:T(8,128)(2,1)} %w_hbm.15), custom_call_target="tpu_custom_call" | custom-call | flops 2147483648 | bytes 8388608 | tf_op jit(solution)/shard_map/own_back/pallas_call | solution.py:527
  54.5 3.3 %all-to-all-start.2 = ((f32[8,8,128]{2,1,0:T(8,128)}), f32[8,8,128]{2,1,0:T(8,128)S(1)}, u32[]{:S(2)}, u32[]{:S(2)}) async-start(f32[8,8,128]{2,1,0:T(8,128)} %rows.2.refs_3_.refs_0_), calls=%async_computation.2 | async-start | bytes 65536 | tf_op jit(solution)/shard_map/all_to_all | solution.py:448
  61.5 2.5 %student_side.5 = (f32[128,8192]{1,0:T(8,128)S(1)}, f32[8,128]{1,0:T(8,128)S(1)}) custom-call(bf16[768,512]{1,0:T(8,128)(2,1)S(1)} %get-tuple-element.33.unit, f32[768,128]{1,0:T(8,128)S(1)} %get-tuple-element.34.lse, bf16[128,1024]{1,0:T(8,128)(2,1)S(1)} %get-tuple-element.35.feat_ref, bf16[128,256]{1,0:T(8,128)(2,1)S(1)} %get-tuple-element.36.scaled_ref, ...), custom_call_target="tpu_custom_call" | custom-call | flops 1342177280 | bytes 1048576 | tf_op jit(solution)/shard_map/student_side/pallas_call | solution.py:578
  72.2 3.3 %all-to-all-start.3 = ((f32[4,64,128]{2,1,0:T(8,128)}), f32[4,64,128]{2,1,0:T(8,128)S(1)}, u32[]{:S(2)}, u32[]{:S(2)}) async-start(f32[4,64,128]{2,1,0:T(8,128)} %columns.2.refs_0_), calls=%async_computation.3 | async-start | bytes 262144 | tf_op jit(solution)/shard_map/all_to_all | solution.py:448
  79.9 3.8 %student_side.6 = (f32[128,8192]{1,0:T(8,128)S(1)}, f32[8,128]{1,0:T(8,128)S(1)}) custom-call(bf16[768,512]{1,0:T(8,128)(2,1)S(1)} %get-tuple-element.33.unit, f32[768,128]{1,0:T(8,128)S(1)} %get-tuple-element.34.lse, bf16[128,1024]{1,0:T(8,128)(2,1)S(1)} %get-tuple-element.35.feat_ref, ...), custom_call_target="tpu_custom_call", output_to_operand_aliasing={{0}: (7, {})} | custom-call | flops 2684354560 | bytes 2097152 | tf_op jit(solution)/shard_map/student_side/pallas_call | solution.py:578
  89.6 3.6 %all-to-all-start.4 = ((f32[8,8,128]{2,1,0:T(8,128)}), f32[8,8,128]{2,1,0:T(8,128)S(1)}, u32[]{:S(2)}, u32[]{:S(2)}) async-start(f32[8,8,128]{2,1,0:T(8,128)} %rows.3.refs_0_), calls=%async_computation.4 | async-start | bytes 65536 | tf_op jit(solution)/shard_map/all_to_all | solution.py:448
  97.5 2.5 %student_side.7 = (f32[128,8192]{1,0:T(8,128)S(1)}, f32[8,128]{1,0:T(8,128)S(1)}) custom-call(bf16[768,512]{1,0:T(8,128)(2,1)S(1)} %get-tuple-element.33.unit, f32[768,128]{1,0:T(8,128)S(1)} %get-tuple-element.34.lse, bf16[128,1024]{1,0:T(8,128)(2,1)S(1)} %get-tuple-element.35.feat_ref, ...), custom_call_target="tpu_custom_call", output_to_operand_aliasing={{0}: (7, {})} | custom-call | flops 1342177280 | bytes 1048576 | tf_op jit(solution)/shard_map/student_side/pallas_call | solution.py:578
  105.8 5.1 %all-to-all-start.5 = ((f32[4,64,128]{2,1,0:T(8,128)}), f32[4,64,128]{2,1,0:T(8,128)S(1)}, u32[]{:S(2)}, u32[]{:S(2)}) async-start(f32[4,64,128]{2,1,0:T(8,128)} %columns.3.refs_0_), calls=%async_computation.5 | async-start | bytes 262144 | tf_op jit(solution)/shard_map/all_to_all | solution.py:448
  115.3 3.8 %student_side.8 = (f32[128,8192]{1,0:T(8,128)S(1)}, f32[8,128]{1,0:T(8,128)S(1)}) custom-call(bf16[768,512]{1,0:T(8,128)(2,1)S(1)} %get-tuple-element.33.unit, f32[768,128]{1,0:T(8,128)S(1)} %get-tuple-element.34.lse, bf16[128,1024]{1,0:T(8,128)(2,1)S(1)} %get-tuple-element.35.feat_ref, ...), custom_call_target="tpu_custom_call", output_to_operand_aliasing={{0}: (7, {})} | custom-call | flops 2684354560 | bytes 2097152 | tf_op jit(solution)/shard_map/student_side/pallas_call | solution.py:578
  123.2 18.7 %last_rows.1 = (bf16[768,8192]{1,0:T(8,128)(2,1)S(1)}, f32[64,128]{1,0:T(8,128)S(1)}, bf16[8,80,512]{2,1,0:T(8,128)(2,1)}) custom-call(s32[2]{0:T(128)S(1)} %pad_add_fusion.place_ref, f32[4,72,128]{2,1,0:T(8,128)S(1)} %all-to-all-done.1.cols_ref.logs_ref, f32[4,64,128]{2,1,0:T(8,128)S(1)} %all-to-all-done.5.cols_ref, ...), custom_call_target="tpu_custom_call" | custom-call | flops 8589934592 | bytes 12582912 | tf_op jit(solution)/shard_map/last_rows/pallas_call | solution.py:616
  142.0 4.6 %copy-done.25 = bf16[768,8192]{1,0:T(8,128)(2,1)} copy-done((bf16[768,8192]{1,0:T(8,128)(2,1)}, bf16[768,8192]{1,0:T(8,128)(2,1)S(1)}, u32[]{:S(2)}) %copy-start.25) | copy-done | bytes 12582936
  146.5 3.9 %all-to-all-start.6 = ((bf16[8,80,512]{2,1,0:T(8,128)(2,1)}), bf16[8,80,512]{2,1,0:T(8,128)(2,1)S(1)}, u32[]{:S(2)}, u32[]{:S(2)}) async-start(bf16[8,80,512]{2,1,0:T(8,128)(2,1)} %get-tuple-element.45.refs_0_), calls=%async_computation.6 | async-start | bytes 1310720 | tf_op jit(solution)/shard_map/all_to_all | solution.py:448
  154.8 3.8 %student_side.9 = (f32[128,8192]{1,0:T(8,128)S(1)}, f32[8,128]{1,0:T(8,128)S(1)}) custom-call(bf16[768,512]{1,0:T(8,128)(2,1)S(1)} %get-tuple-element.33.unit, f32[768,128]{1,0:T(8,128)S(1)} %get-tuple-element.34.lse, bf16[128,1024]{1,0:T(8,128)(2,1)S(1)} %get-tuple-element.35.feat_ref, ...), custom_call_target="tpu_custom_call", output_to_operand_aliasing={{0}: (7, {})} | custom-call | flops 2684354560 | bytes 2097152 | tf_op jit(solution)/shard_map/student_side/pallas_call | solution.py:578
  163.3 3.8 %all-to-all-start.7 = ((f32[8,32,512]{2,1,0:T(8,128)}), f32[8,32,512]{2,1,0:T(8,128)S(1)}, u32[]{:S(2)}, u32[]{:S(2)}) async-start(f32[8,32,512]{2,1,0:T(8,128)} %get-tuple-element.51), calls=%async_computation.7 | async-start | bytes 1048576 | tf_op jit(solution)/shard_map/all_to_all | solution.py:448
  167.0 3.9 %collective-permute-start.8 = (f32[8,128]{1,0:T(8,128)S(1)}, f32[8,128]{1,0:T(8,128)S(1)}, u32[]{:S(2)}, u32[]{:S(2)}) collective-permute-start(f32[8,128]{1,0:T(8,128)S(1)} %get-tuple-element.52), channel_id=1, source_target_pairs={{0,3},{1,2},{2,1},{3,0},{4,7},{5,6},{6,5},{7,4},{8,11},{9,10},{10,... | collective-permute-start | bytes 12296 | tf_op jit(solution)/shard_map/ppermute | solution.py:459
  175.9 4.6 %copy-done.26 = bf16[768,8192]{1,0:T(8,128)(2,1)S(1)} copy-done((bf16[768,8192]{1,0:T(8,128)(2,1)S(1)}, bf16[768,8192]{1,0:T(8,128)(2,1)}, u32[]{:S(2)}) %copy-start.26) | copy-done | bytes 12582936
  180.5 3.5 %weight_grads.1 = bf16[128,8192]{1,0:T(8,128)(2,1)} custom-call(bf16[256,8192]{1,0:T(8,128)(2,1)S(1)} %copy-done.7, bf16[768,8192]{1,0:T(8,128)(2,1)S(1)} %copy-done.26, bf16[128,1024]{1,0:T(8,128)(2,1)S(1)} %get-tuple-element.35.feat_ref, f32[128,8192]{1,0:T(8,128)S(1)} %copy-done.24, f32[64,128]{1,0:T(8,128)S(1)} %get-tuple-element.48.scale_ref, ...), custom_call_target="tpu_custom_call" | custom-call | flops 2147483648 | bytes 12582912 | tf_op jit(solution)/shard_map/weight_grads/pallas_call | solution.py:657
  (88 shorter events, 74.0 us)
Async XLA Ops:
  0.6 30.9 %collective-permute-start.2 = (bf16[256,512]{1,0:T(8,128)(2,1)}, bf16[256,512]{1,0:T(8,128)(2,1)S(1)}, u32[]{:S(2)}, u32[]{:S(2)}) collective-permute-start(bf16[256,512]{1,0:T(8,128)(2,1)} %s_ref.3), channel_id=1, source_target_pairs={{0,1},{1,2},{2,3},{3,0},{4,5},{5,6},{6,7},{7,4},{8,9},{9,10},{10,1... | collective-permute-start | bytes 786440 | tf_op jit(solution)/shard_map/ppermute | solution.py:453
  3.7 27.9 %collective-permute-start.1 = (bf16[256,512]{1,0:T(8,128)(2,1)}, bf16[256,512]{1,0:T(8,128)(2,1)S(1)}, u32[]{:S(2)}, u32[]{:S(2)}) collective-permute-start(bf16[256,512]{1,0:T(8,128)(2,1)} %s_ref.3), channel_id=1, source_target_pairs={{0,2},{1,3},{2,0},{3,1},{4,6},{5,7},{6,4},{7,5},{8,10},{9,11},{10,... | collective-permute-start | bytes 786440 | tf_op jit(solution)/shard_map/ppermute | solution.py:453
  6.3 25.3 %collective-permute-start = (bf16[256,512]{1,0:T(8,128)(2,1)}, bf16[256,512]{1,0:T(8,128)(2,1)S(1)}, u32[]{:S(2)}, u32[]{:S(2)}) collective-permute-start(bf16[256,512]{1,0:T(8,128)(2,1)} %s_ref.3), channel_id=1, source_target_pairs={{0,3},{1,0},{2,1},{3,2},{4,7},{5,4},{6,5},{7,6},{8,11},{9,8},{10,9... | collective-permute-start | bytes 786440 | tf_op jit(solution)/shard_map/ppermute | solution.py:453
  23.0 8.6 %all-to-all-start = ((f32[8,8,128]{2,1,0:T(8,128)}), f32[8,8,128]{2,1,0:T(8,128)S(1)}, u32[]{:S(2)}, u32[]{:S(2)}) async-start(f32[8,8,128]{2,1,0:T(8,128)} %get-tuple-element.29), calls=%async_computation | async-start | bytes 65536 | tf_op jit(solution)/shard_map/all_to_all | solution.py:448
  31.6 2.2 %copy-start.1 = (bf16[256,8192]{1,0:T(8,128)(2,1)S(1)}, bf16[256,8192]{1,0:T(8,128)(2,1)}, u32[]{:S(2)}) copy-start(bf16[256,8192]{1,0:T(8,128)(2,1)} %copy-done) | copy-start | bytes 12582916
  35.9 14.7 %all-to-all-start.1 = ((f32[4,72,128]{2,1,0:T(8,128)}), f32[4,72,128]{2,1,0:T(8,128)S(1)}, u32[]{:S(2)}, u32[]{:S(2)}) async-start(f32[4,72,128]{2,1,0:T(8,128)} %get-tuple-element.30), calls=%async_computation.1 | async-start | bytes 294912 | tf_op jit(solution)/shard_map/all_to_all | solution.py:448
  39.3 26.7 %collective-permute-start.3 = (bf16[256,512]{1,0:T(8,128)(2,1)}, bf16[256,512]{1,0:T(8,128)(2,1)S(1)}, u32[]{:S(2)}, u32[]{:S(2)}) collective-permute-start(bf16[256,512]{1,0:T(8,128)(2,1)} %t_ref.1), channel_id=1, source_target_pairs={{0,3},{1,0},{2,1},{3,2},{4,7},{5,4},{6,5},{7,6},{8,11},{9,8},{10,9... | collective-permute-start | bytes 786440 | tf_op jit(solution)/shard_map/ppermute | solution.py:453
  43.1 22.9 %collective-permute-start.5 = (bf16[256,512]{1,0:T(8,128)(2,1)}, bf16[256,512]{1,0:T(8,128)(2,1)}, u32[]{:S(2)}, u32[]{:S(2)}) collective-permute-start(bf16[256,512]{1,0:T(8,128)(2,1)} %t_ref.1), channel_id=1, source_target_pairs={{0,1},{1,2},{2,3},{3,0},{4,5},{5,6},{6,7},{7,4},{8,9},{9,10},{10,1... | collective-permute-start | bytes 786440 | tf_op jit(solution)/shard_map/ppermute | solution.py:453
  43.1 25.3 %collective-permute-start.4 = (bf16[256,512]{1,0:T(8,128)(2,1)}, bf16[256,512]{1,0:T(8,128)(2,1)}, u32[]{:S(2)}, u32[]{:S(2)}) collective-permute-start(bf16[256,512]{1,0:T(8,128)(2,1)} %t_ref.1), channel_id=1, source_target_pairs={{0,2},{1,3},{2,0},{3,1},{4,6},{5,7},{6,4},{7,5},{8,10},{9,11},{10,... | collective-permute-start | bytes 786440 | tf_op jit(solution)/shard_map/ppermute | solution.py:453
  50.7 2.2 %copy-start.2 = (bf16[256,8192]{1,0:T(8,128)(2,1)S(1)}, bf16[256,8192]{1,0:T(8,128)(2,1)}, u32[]{:S(2)}) copy-start(bf16[256,8192]{1,0:T(8,128)(2,1)} %copy-done) | copy-start | bytes 12582916
  52.8 5.0 %copy-start.28 = (bf16[256,512]{1,0:T(8,128)(2,1)S(1)}, bf16[256,512]{1,0:T(8,128)(2,1)}, u32[]{:S(2)}) copy-start(bf16[256,512]{1,0:T(8,128)(2,1)} %s_ref.3) | copy-start | bytes 786436
  54.5 13.9 %all-to-all-start.2 = ((f32[8,8,128]{2,1,0:T(8,128)}), f32[8,8,128]{2,1,0:T(8,128)S(1)}, u32[]{:S(2)}, u32[]{:S(2)}) async-start(f32[8,8,128]{2,1,0:T(8,128)} %rows.2.refs_3_.refs_0_), calls=%async_computation.2 | async-start | bytes 65536 | tf_op jit(solution)/shard_map/all_to_all | solution.py:448
  59.3 2.2 %copy-start.10 = (bf16[256,8192]{1,0:T(8,128)(2,1)S(1)}, bf16[256,8192]{1,0:T(8,128)(2,1)}, u32[]{:S(2)}) copy-start(bf16[256,8192]{1,0:T(8,128)(2,1)} %copy-done.8) | copy-start | bytes 12582916
  68.4 2.2 %copy-start.3 = (bf16[256,8192]{1,0:T(8,128)(2,1)S(1)}, bf16[256,8192]{1,0:T(8,128)(2,1)}, u32[]{:S(2)}) copy-start(bf16[256,8192]{1,0:T(8,128)(2,1)} %copy-done) | copy-start | bytes 12582916
  72.2 13.5 %all-to-all-start.3 = ((f32[4,64,128]{2,1,0:T(8,128)}), f32[4,64,128]{2,1,0:T(8,128)S(1)}, u32[]{:S(2)}, u32[]{:S(2)}) async-start(f32[4,64,128]{2,1,0:T(8,128)} %columns.2.refs_0_), calls=%async_computation.3 | async-start | bytes 262144 | tf_op jit(solution)/shard_map/all_to_all | solution.py:448
  89.6 12.5 %all-to-all-start.4 = ((f32[8,8,128]{2,1,0:T(8,128)}), f32[8,8,128]{2,1,0:T(8,128)S(1)}, u32[]{:S(2)}, u32[]{:S(2)}) async-start(f32[8,8,128]{2,1,0:T(8,128)} %rows.3.refs_0_), calls=%async_computation.4 | async-start | bytes 65536 | tf_op jit(solution)/shard_map/all_to_all | solution.py:448
  105.8 15.2 %all-to-all-start.5 = ((f32[4,64,128]{2,1,0:T(8,128)}), f32[4,64,128]{2,1,0:T(8,128)S(1)}, u32[]{:S(2)}, u32[]{:S(2)}) async-start(f32[4,64,128]{2,1,0:T(8,128)} %columns.3.refs_0_), calls=%async_computation.5 | async-start | bytes 262144 | tf_op jit(solution)/shard_map/all_to_all | solution.py:448
  141.9 4.6 %copy-start.25 = (bf16[768,8192]{1,0:T(8,128)(2,1)}, bf16[768,8192]{1,0:T(8,128)(2,1)S(1)}, u32[]{:S(2)}) copy-start(bf16[768,8192]{1,0:T(8,128)(2,1)S(1)} %get-tuple-element.44.prob_ref) | copy-start | bytes 37748740
  146.5 15.1 %all-to-all-start.6 = ((bf16[8,80,512]{2,1,0:T(8,128)(2,1)}), bf16[8,80,512]{2,1,0:T(8,128)(2,1)S(1)}, u32[]{:S(2)}, u32[]{:S(2)}) async-start(bf16[8,80,512]{2,1,0:T(8,128)(2,1)} %get-tuple-element.45.refs_0_), calls=%async_computation.6 | async-start | bytes 1310720 | tf_op jit(solution)/shard_map/all_to_all | solution.py:448
  163.3 22.0 %all-to-all-start.7 = ((f32[8,32,512]{2,1,0:T(8,128)}), f32[8,32,512]{2,1,0:T(8,128)S(1)}, u32[]{:S(2)}, u32[]{:S(2)}) async-start(f32[8,32,512]{2,1,0:T(8,128)} %get-tuple-element.51), calls=%async_computation.7 | async-start | bytes 1048576 | tf_op jit(solution)/shard_map/all_to_all | solution.py:448
  167.0 17.0 %collective-permute-start.8 = (f32[8,128]{1,0:T(8,128)S(1)}, f32[8,128]{1,0:T(8,128)S(1)}, u32[]{:S(2)}, u32[]{:S(2)}) collective-permute-start(f32[8,128]{1,0:T(8,128)S(1)} %get-tuple-element.52), channel_id=1, source_target_pairs={{0,3},{1,2},{2,1},{3,0},{4,7},{5,6},{6,5},{7,4},{8,11},{9,10},{10,... | collective-permute-start | bytes 12296 | tf_op jit(solution)/shard_map/ppermute | solution.py:459
  170.9 13.1 %collective-permute-start.7 = (f32[8,128]{1,0:T(8,128)S(1)}, f32[8,128]{1,0:T(8,128)S(1)}, u32[]{:S(2)}, u32[]{:S(2)}) collective-permute-start(f32[8,128]{1,0:T(8,128)S(1)} %get-tuple-element.52), channel_id=1, source_target_pairs={{0,2},{1,3},{2,0},{3,1},{4,6},{5,7},{6,4},{7,5},{8,10},{9,11},{10,... | collective-permute-start | bytes 12296 | tf_op jit(solution)/shard_map/ppermute | solution.py:459
  170.9 13.1 %collective-permute-start.6 = (f32[8,128]{1,0:T(8,128)S(1)}, f32[8,128]{1,0:T(8,128)S(1)}, u32[]{:S(2)}, u32[]{:S(2)}) collective-permute-start(f32[8,128]{1,0:T(8,128)S(1)} %get-tuple-element.52), channel_id=1, source_target_pairs={{0,1},{1,0},{2,3},{3,2},{4,5},{5,4},{6,7},{7,6},{8,9},{9,8},{10,11... | collective-permute-start | bytes 12296 | tf_op jit(solution)/shard_map/ppermute | solution.py:459
  175.9 4.6 %copy-start.26 = (bf16[768,8192]{1,0:T(8,128)(2,1)S(1)}, bf16[768,8192]{1,0:T(8,128)(2,1)}, u32[]{:S(2)}) copy-start(bf16[768,8192]{1,0:T(8,128)(2,1)} %copy-done.25) | copy-start | bytes 37748740
  (22 other events, 45.6 us)

commit v5 on v4

v5 whole, which is shorter than its diff:
```python
import functools
import math

import jax
import jax.numpy as jnp
from jax import lax
from jax.experimental import pallas as pl
from jax.experimental.pallas import tpu as pltpu
from jax.sharding import PartitionSpec as P

SWEEPS = 3
TEMP_TEACHER = 0.04
TEMP_STUDENT = 0.1
LOG2E = math.log2(math.e)
SCALE_TEACHER = LOG2E / TEMP_TEACHER
SCALE_STUDENT = LOG2E / TEMP_STUDENT
LANES = 128
WIDE = 1024
F32 = jnp.float32
BF16 = jnp.bfloat16


def unit_rows(values):
    wide = values.astype(F32)
    length = jnp.sqrt(jnp.sum(wide * wide, axis=-1, keepdims=True) + 1e-06)
    return wide / length, length


def diagonal():
    shape = (LANES, LANES)
    return lax.broadcasted_iota(jnp.int32, shape, 0) == lax.broadcasted_iota(jnp.int32, shape, 1)


def to_column(row):
    spread = jnp.where(diagonal(), jnp.broadcast_to(row, (LANES, LANES)), 0.0)
    return jnp.sum(spread, axis=1, keepdims=True)


def to_row(column):
    spread = jnp.where(diagonal(), jnp.broadcast_to(column, (LANES, LANES)), 0.0)
    return jnp.sum(spread, axis=0, keepdims=True)


def spread_rows(ref, rows):
    for a in range(rows.shape[0]):
        ref[a * LANES : (a + 1) * LANES, :] = jnp.broadcast_to(
            to_column(rows[a : a + 1, :]), (LANES, LANES)
        )


def pack_rows(ref, columns):
    for a in range(columns.shape[0] // LANES):
        ref[a : a + 1, :] = to_row(columns[a * LANES : (a + 1) * LANES, :])


def lane_tiles(values):
    return [values[:, t * LANES : (t + 1) * LANES] for t in range(values.shape[1] // LANES)]


def fold(values):
    return functools.reduce(jnp.add, lane_tiles(values))


def column_sums(values):
    rows, cols = values.shape
    return jnp.sum(values.reshape(rows // 8, 8, cols), axis=0)


def nt_dot(a, b):
    return lax.dot_general(a, b, (((1,), (1,)), ((), ())), preferred_element_type=F32)


def add_up(values):
    return functools.reduce(jnp.add, values)


def repeat(out_ref):
    for p in range(1, out_ref.shape[0]):
        out_ref[p] = out_ref[0]


def chunk_copies(source, target, sems, first=0, back=0):
    count = min(source.shape[1], target.shape[1]) // WIDE
    return [
        pltpu.make_async_copy(
            source.at[:, (first + k) * WIDE : (first + k + 1) * WIDE],
            target.at[:, (back + k) * WIDE : (back + k + 1) * WIDE],
            sems.at[k],
        )
        for k in range(count)
    ]


def start(*copies):
    for each in zip(*copies):
        for copy in each:
            copy.start()


def chunk(k):
    return slice(k * WIDE, (k + 1) * WIDE)


def stats_kernel(
    t_ref, s_ref, w_hbm, t_out, s_out, out_ref,
    w_ref, unit, exps, logits, top, total, w_sem, t_sem, s_sem,
):
    piece = 512
    cols = w_ref.shape[1]
    pieces = [slice(c, c + piece) for c in range(0, cols, piece)]
    quarter = out_ref.shape[1] // 4
    scales = (SCALE_TEACHER, SCALE_STUDENT)
    loads = chunk_copies(w_hbm, w_ref, w_sem)
    start(loads)
    stores = [
        chunk_copies(exps.at[0], t_out, t_sem), chunk_copies(exps.at[1], s_out, s_sem),
    ]
    for which, ref in enumerate((t_ref, s_ref)):
        unit[which] = unit_rows(ref[...])[0].astype(BF16)
    top[...] = jnp.full(top.shape, -1e30, F32)
    total[...] = jnp.zeros(total.shape, F32)

    def product(which, here):
        values = jnp.dot(unit[which], w_ref[:, here], preferred_element_type=F32) * scales[which]
        top[which] = functools.reduce(jnp.maximum, lane_tiles(values), top[which])
        return values

    def peak(which):
        return jnp.max(top[which], axis=1, keepdims=True)

    def raised(which, here, shift):
        values = jnp.exp2(logits[:, here] - shift)
        exps[which, :, here] = values.astype(BF16)
        total[which] += fold(values)
        if here.stop % WIDE == 0:
            stores[which][here.stop // WIDE - 1].start()

    for here in pieces:
        if here.start % WIDE == 0:
            loads[here.start // WIDE].wait()
        logits[:, here] = product(0, here)
    peaks = [peak(0)]
    shift = jnp.broadcast_to(peaks[0], (peaks[0].shape[0], piece))
    for here in pieces:
        values = product(1, here)
        raised(0, here, shift)
        logits[:, here] = values
    peaks.append(peak(1))
    shift = jnp.broadcast_to(peaks[1], (peaks[1].shape[0], piece))
    for here in pieces:
        raised(1, here, shift)
    for which in range(2):
        sums = jnp.sum(total[which], axis=1, keepdims=True)
        for k, column in enumerate((peaks[which], sums)):
            first = (2 * which + k) * quarter
            pack_rows(out_ref.at[0, first : first + quarter], column)
    repeat(out_ref)
    for copy in stores[0] + stores[1]:
        copy.wait()


def merged(stats_ref, which):
    parts, height, _ = stats_ref.shape
    quarter = height // 4
    first = 2 * which * quarter
    tops = [stats_ref[p, first : first + quarter, :] for p in range(parts)]
    top = functools.reduce(jnp.maximum, tops)
    sums = [
        stats_ref[p, first + quarter : first + 2 * quarter, :] * jnp.exp2(tops[p] - top)
        for p in range(parts)
    ]
    return top + jnp.log2(add_up(sums))


def column_pass(loads, exp_ref, weight, out_ref):
    for k, load in enumerate(loads):
        load.wait()
        sums = jnp.zeros((8, WIDE), F32)
        for g in range(0, exp_ref.shape[0], 16):
            shift = weight[g : g + 16, :]
            tiles = lane_tiles(exp_ref[g : g + 16, chunk(k)].astype(F32))
            sums = sums + column_sums(jnp.concatenate([tile * shift for tile in tiles], axis=1))
        sums = jnp.sum(sums, axis=0, keepdims=True)
        block = jnp.concatenate(lane_tiles(sums), axis=0)
        for g in range(out_ref.shape[0]):
            out_ref[g, k * (WIDE // LANES) : (k + 1) * (WIDE // LANES), :] = block


def first_column_kernel(place_ref, stats_ref, exp_hbm, *refs):
    factor_ref, out_ref, weight, exp_ref, sem = refs[-5:]
    loads = chunk_copies(exp_hbm, exp_ref, sem)
    start(loads)
    quarter = stats_ref.shape[1] // 4
    height = out_ref.shape[1] - 8
    own = stats_ref[pl.ds(place_ref[1], 1)][0]
    factor_ref[...] = jnp.zeros(factor_ref.shape, F32)
    rows = []
    for which in range(2):
        log_sum = merged(stats_ref, which)
        here = slice(which * quarter, (which + 1) * quarter)
        factor_ref[here, :] = jnp.exp2(
            own[2 * which * quarter : (2 * which + 1) * quarter, :] - log_sum
        )
        rows.append(log_sum)
    rows.append(jnp.zeros((8 - 2 * quarter, LANES), F32))
    logs = jnp.concatenate(rows, axis=0)
    for g in range(out_ref.shape[0]):
        out_ref[g, height:, :] = logs
    spread_rows(weight, factor_ref[:quarter, :])
    column_pass(loads, exp_ref, weight, out_ref)


def column_kernel(sums_ref, factor_ref, exp_hbm, *refs):
    out_ref, weight, exp_ref, sem = refs[-4:]
    loads = chunk_copies(exp_hbm, exp_ref, sem)
    start(loads)
    quarter = weight.shape[0] // LANES
    scale = 1.0 / add_up([sums_ref[p, :quarter, :] for p in range(sums_ref.shape[0])])
    spread_rows(weight, scale * factor_ref[:quarter, :])
    column_pass(loads, exp_ref, weight, out_ref)


def column_scales(cols_ref, height):
    return 1.0 / add_up([cols_ref[g, :height, :] for g in range(cols_ref.shape[0])])


def add_row_sums(rows, ref, scales, k):
    for g in range(0, ref.shape[0], 32):
        total = rows[g : g + 32, :]
        for t, tile in enumerate(lane_tiles(ref[g : g + 32, chunk(k)].astype(F32))):
            first = k * (WIDE // LANES) + t
            total = total + tile * scales[first : first + 1, :]
        rows[g : g + 32, :] = total


def row_kernel(cols_ref, factor_ref, exp_hbm, *refs):
    out_ref, scales, rows, exp_ref, sem = refs[-5:]
    loads = chunk_copies(exp_hbm, exp_ref, sem)
    start(loads)
    scales[...] = column_scales(cols_ref, scales.shape[0])
    rows[...] = jnp.zeros(rows.shape, F32)
    quarter = rows.shape[0] // LANES
    out_ref[0] = jnp.zeros(out_ref.shape[1:], F32)
    for k, load in enumerate(loads):
        load.wait()
        add_row_sums(rows, exp_ref, scales, k)
    pack_rows(out_ref.at[0, :quarter], jnp.sum(rows[...], axis=1, keepdims=True))
    out_ref[0, :quarter, :] = out_ref[0, :quarter, :] * factor_ref[:quarter, :]
    repeat(out_ref)


def own_back_kernel(before_ref, exp_hbm, w_hbm, back_ref, exp_ref, w_ref, exp_sem, w_sem):
    exp_loads = chunk_copies(exp_hbm, exp_ref, exp_sem)
    w_loads = chunk_copies(w_hbm, w_ref, w_sem)
    start(exp_loads, w_loads)
    back_ref[...] = jnp.zeros(back_ref.shape, F32)
    for k in range(len(w_loads)):
        exp_loads[k].wait()
        w_loads[k].wait()
        back_ref[...] += nt_dot(exp_ref[:, chunk(k)], w_ref[:, chunk(k)])


def relative(place_ref, g, groups):
    return pl.ds(lax.rem(place_ref[0] + g, groups), 1)


def relative_logs(place_ref, logs_ref, lse, which, shift=0.0):
    groups = logs_ref.shape[0]
    own = lse.shape[0] // (groups - 1)
    quarter = own // LANES
    height = logs_ref.shape[1] - 8
    for g in range(1, groups):
        there = logs_ref[relative(place_ref, g, groups)][0]
        first = height + which * quarter
        spread_rows(lse.at[(g - 1) * own : g * own], there[first : first + quarter, :] - shift)


def student_rows_kernel(log_protos, place_ref, factor_ref, own_ref, *refs):
    unit_ref, feat_ref, scaled_ref, turned = refs[-4:]
    own = own_ref.shape[0]
    groups = turned.shape[1] // own
    raw = refs[: groups - 1]
    quarter, feats = own // LANES, feat_ref.shape[0]
    for g in range(groups):
        half = unit_rows((raw[g - 1] if g else own_ref)[...])[0].astype(BF16)
        if g:
            unit_ref[(g - 1) * own : g * own, :] = half
        half = half.astype(F32)
        for a in range(0, own, LANES):
            first = g * own + a
            turned[:, first : first + LANES] = jnp.transpose(half[a : a + LANES, :]).astype(BF16)
    feat = turned[pl.ds(pl.multiple_of(place_ref[0] * feats, feats), feats), :]
    feat_ref[...] = feat
    for a in range(quarter):
        lanes = slice(a * LANES, (a + 1) * LANES)
        factor = factor_ref[quarter + a : quarter + a + 1, :] * 2.0**log_protos
        scaled_ref[:, lanes] = (feat[:, lanes].astype(F32) * factor).astype(BF16)


def probabilities(unit, own, w, lse, scale, use):
    blocks = [(g, n) for g in range(unit.shape[0] // own) for n in range(0, WIDE, 512)]

    def product(g, n):
        return jnp.dot(
            unit[g * own : (g + 1) * own, :], w[:, n : n + 512], preferred_element_type=F32
        )

    logits = product(*blocks[0])
    for i, (g, n) in enumerate(blocks):
        later = product(*blocks[i + 1]) if i + 1 < len(blocks) else None
        shift = lse[g * own : (g + 1) * own, :]
        use(g, n, [jnp.exp2(tile * scale - shift) for tile in lane_tiles(logits)])
        logits = later


def student_kernel(
    log_protos, first, place_ref, logs_ref, unit, feat_ref, scaled_ref, exp_hbm, w_hbm, *refs
):
    grad_hbm, token_ref, lse, prob, exp_ref, w_ref, grad, exp_sem, w_sem, grad_sem = refs[-10:]
    own = exp_ref.shape[0]
    exp_loads = chunk_copies(exp_hbm, exp_ref, exp_sem, first)
    w_loads = chunk_copies(w_hbm, w_ref, w_sem, first)
    stores = chunk_copies(grad, grad_hbm, grad_sem)
    start(w_loads, exp_loads)
    token_ref[...] = jnp.zeros(token_ref.shape, F32)
    relative_logs(place_ref, logs_ref, lse, 1, log_protos)
    for k in range(len(w_loads)):
        w_loads[k].wait()
        slot = prob.at[k % 2]

        def use(g, n, tiles):
            for t, tile in enumerate(tiles):
                lanes = slice(n + t * LANES, n + (t + 1) * LANES)
                slot[g * own : (g + 1) * own, lanes] = tile.astype(BF16)

        probabilities(unit, own, w_ref.at[:, chunk(k)], lse, SCALE_STUDENT, use)
        exp_loads[k].wait()
        grad[:, chunk(k)] = jnp.dot(
            scaled_ref[...], exp_ref[:, chunk(k)], preferred_element_type=F32
        ) + jnp.dot(feat_ref[:, own:], slot[...], preferred_element_type=F32)
        stores[k].start()
    for store in stores:
        store.wait()


def as_three(value):
    high = value.astype(BF16)
    rest = value - high.astype(F32)
    middle = rest.astype(BF16)
    return high, middle, (rest - middle.astype(F32)).astype(BF16)


def last_kernel(groups, place_ref, logs_ref, cols_ref, factor_ref, own_ref, student_ref, exp_hbm, w_hbm, *refs):
    raw = refs[: groups - 1]
    (
        prob_hbm, scale_ref, out_ref, unit, lse, rows, own_rows, back, scaled, sums,
        exp_ref, w_ref, prob_ref, exp_sem, w_sem, prob_sem,
    ) = refs[-16:]
    own, others = exp_ref.shape[0], prob_ref.shape[0]
    tiles = (own + others) // LANES
    quarter = own // LANES
    loads = chunk_copies(w_hbm, w_ref, w_sem)
    exp_loads = chunk_copies(exp_hbm, exp_ref, exp_sem)
    start(loads)
    start(exp_loads)
    scale_ref[...] = column_scales(cols_ref, scale_ref.shape[0])
    rows[...] = jnp.zeros(rows.shape, F32)
    back[...] = jnp.zeros(back.shape, F32)
    relative_logs(place_ref, logs_ref, lse, 0)
    for g in range(groups - 1):
        unit[g * own : (g + 1) * own, :] = unit_rows(raw[g][...])[0].astype(BF16)

    @pl.loop(0, len(loads))
    def _(k):
        here = pl.ds(pl.multiple_of(k * WIDE, WIDE), WIDE)
        pltpu.make_async_copy(w_hbm.at[:, here], w_ref.at[:, here], w_sem.at[k]).wait()
        scales = scale_ref[pl.ds(pl.multiple_of(k * (WIDE // LANES), 8), WIDE // LANES), :]

        def use(g, n, tiles):
            first = n // LANES
            for t, tile in enumerate(tiles):
                lanes = pl.ds(pl.multiple_of(k * WIDE + n + t * LANES, LANES), LANES)
                prob_ref[g * own : (g + 1) * own, lanes] = tile.astype(BF16)
            tiles = [
                tile * scales[first + t : first + t + 1, :] for t, tile in enumerate(tiles)
            ]
            rows[g * own : (g + 1) * own, :] += add_up(tiles)
            if g == groups // 2 - 1:
                for t, tile in enumerate(tiles):
                    scaled[:, n + t * LANES : n + (t + 1) * LANES] = tile.astype(BF16)

        probabilities(unit, own, w_ref.at[:, here], lse, SCALE_TEACHER, use)
        pltpu.make_async_copy(prob_ref.at[:, here], prob_hbm.at[:, here], prob_sem.at[k]).start()
        back[...] += nt_dot(scaled[...], w_ref[:, here])

    sums[...] = jnp.zeros(sums.shape, F32)
    own_rows[...] = jnp.zeros(own_rows.shape, F32)
    for k, load in enumerate(exp_loads):
        load.wait()
        add_row_sums(own_rows, exp_ref, scale_ref, k)
    pack_rows(sums.at[:quarter], jnp.sum(own_rows[...], axis=1, keepdims=True))
    sums[:quarter, :] = sums[:quarter, :] * factor_ref[:quarter, :]
    pack_rows(sums.at[quarter:tiles], jnp.sum(rows[...], axis=1, keepdims=True))
    half = unit_rows(own_ref[...])[0].astype(BF16).astype(F32)
    inner = jnp.sum(half * back[...], axis=1, keepdims=True)
    pack_rows(sums.at[tiles : tiles + quarter], inner)
    parts = out_ref.shape[0]
    share = own // parts
    protos = 1.0 * out_ref.shape[0] * w_ref.shape[1]
    student = []
    for a in range(quarter):
        factor = to_column(factor_ref[quarter + a : quarter + a + 1, :] * protos)
        student.append(student_ref[a * LANES : (a + 1) * LANES, :] * factor)
    student = jnp.concatenate(student, axis=0).astype(BF16)
    terms = list(as_three(sums[...]))
    terms.append(jnp.zeros((sums.shape[0], out_ref.shape[2] - 3 * LANES), BF16))
    terms = jnp.concatenate(terms, axis=1)
    for p in range(parts):
        here = slice(p * share, (p + 1) * share)
        out_ref[p] = jnp.concatenate(
            [student[here, :], back[here, :].astype(BF16), terms], axis=0
        )
    for store in chunk_copies(prob_ref, prob_hbm, prob_sem):
        store.wait()


def total_sums(message_ref, first):
    parts = message_ref.shape[0]
    each = [
        add_up([t.astype(F32) for t in lane_tiles(message_ref[p, first:, : 3 * LANES])[::-1]])
        for p in range(parts)
    ]
    return add_up(each)


def rows_kernel(tiles, protos, place_ref, s_ref, message_ref, logs_ref, *refs):
    out_ref, loss_ref, sums_ref, weight = refs[-4:]
    parts = message_ref.shape[0]
    share, own = out_ref.shape[1], weight.shape[0]
    quarter = own // LANES
    first = tiles // 2
    totals = total_sums(message_ref, 2 * share)
    sums_ref[...] = totals
    scale = 1.0 / totals[first : first + quarter, :]
    spread_rows(weight, scale)
    mine = pl.ds(pl.multiple_of(place_ref[1] * share, share), share)
    total = add_up([message_ref[p, :share, :].astype(F32) for p in range(parts)])
    paired = add_up([message_ref[p, share : 2 * share, :].astype(F32) for p in range(parts)])
    total = total - paired * (weight[mine, :1] * protos)
    unit, length = unit_rows(s_ref[mine, :])
    out_ref[0] = (total - unit * jnp.sum(unit * total, axis=-1, keepdims=True)) / length
    repeat(out_ref)
    height = logs_ref.shape[1] - 8
    logs = logs_ref[pl.ds(place_ref[0], 1)][0][height + quarter : height + 2 * quarter, :]
    terms = logs / LOG2E - totals[tiles : tiles + quarter, :] * scale / TEMP_STUDENT
    loss_ref[...] = jnp.broadcast_to(jnp.sum(terms), loss_ref.shape)


def grad_kernel(counts, protos, exp_hbm, prob_hbm, feat_ref, scale_ref, sums_ref, factor_ref, *refs):
    parts = refs[: len(counts)]
    out_hbm, scaled, exp_ref, prob_ref, part_ref, out, exp_sem, prob_sem, part_sem, sem = refs[-10:]
    exp_loads = chunk_copies(exp_hbm, exp_ref, exp_sem)
    prob_loads = chunk_copies(prob_hbm, prob_ref, prob_sem)
    part_loads, first = [], 0
    for count, part in zip(counts, parts):
        part_loads += chunk_copies(part, part_ref, part_sem.at[first : first + count], 0, first)
        first += count
    start(exp_loads, prob_loads, part_loads)
    own = exp_ref.shape[0]
    tiles = (own + prob_ref.shape[0]) // LANES
    rows = protos / sums_ref[:tiles, :]
    for a in range(tiles):
        other = (a + tiles // 2) % tiles
        feat = feat_ref[:, other * LANES : (other + 1) * LANES].astype(F32)
        row = rows[a : a + 1, :]
        if a < own // LANES:
            row = row * factor_ref[a : a + 1, :]
        scaled[:, a * LANES : (a + 1) * LANES] = (feat * row).astype(BF16)
    stores = chunk_copies(out, out_hbm, sem)
    for k, store in enumerate(stores):
        exp_loads[k].wait()
        prob_loads[k].wait()
        paired = jnp.dot(scaled[:, :own], exp_ref[:, chunk(k)], preferred_element_type=F32)
        paired = paired + jnp.dot(
            scaled[:, own:], prob_ref[:, chunk(k)], preferred_element_type=F32
        )
        part_loads[k].wait()
        for t, tile in enumerate(lane_tiles(paired)):
            lanes = slice(k * WIDE + t * LANES, k * WIDE + (t + 1) * LANES)
            scale = scale_ref[lanes.start // LANES : lanes.stop // LANES, :]
            out[:, lanes] = (part_ref[:, lanes] - tile * scale).astype(BF16)
        store.start()
    for store in stores:
        store.wait()


SMEM = pl.BlockSpec(memory_space=pltpu.SMEM)
VMEM = pl.BlockSpec(memory_space=pltpu.VMEM)
ANY = pl.BlockSpec(memory_space=pl.ANY)


def params(nbytes):
    return pltpu.CompilerParams(vmem_limit_bytes=int(nbytes) + 8 * 2**20)


def cost(flops, nbytes, exps=0):
    return pl.CostEstimate(flops=int(flops), bytes_accessed=int(nbytes), transcendentals=int(exps))


def exchange(value, axis):
    return lax.all_to_all(value, axis, 0, 0)


def following(value, axis):
    n = lax.axis_size(axis)
    return [lax.ppermute(value, axis, [(i, (i - s) % n) for i in range(n)]) for s in range(1, n)]


def tree_sum(value, axis):
    n = lax.axis_size(axis)
    values = [value] + [
        lax.ppermute(value, axis, [(i, i ^ s) for i in range(n)]) for s in range(1, n)
    ]
    while len(values) > 1:
        values = [a + b for a, b in zip(values[::2], values[1::2])]
    return values[0]


def local(teacher_feats, student_feats, proto_weight):
    parts, groups = lax.axis_size("proto"), lax.axis_size("batch")
    own, width = teacher_feats.shape
    local_protos = proto_weight.shape[1]
    rows = own * groups
    others = rows - own
    protos = local_protos * parts
    feats = width // groups
    share = own // parts
    tiles = rows // LANES
    height = local_protos // LANES
    chunks = local_protos // WIDE
    place = jnp.stack([lax.axis_index("batch"), lax.axis_index("proto")]).astype(jnp.int32)
    struct = jax.ShapeDtypeStruct
    weight_bytes = 2 * width * local_protos
    exp_bytes = 2 * own * local_protos
    others_bytes = 2 * others * local_protos
    spread = pltpu.VMEM((own, LANES), F32)
    w_buffer = pltpu.VMEM((width, local_protos), BF16)
    exp_buffer = pltpu.VMEM((own, local_protos), BF16)
    sems = pltpu.SemaphoreType.DMA((chunks,))
    log_protos = math.log2(protos)
    token = struct((8, LANES), F32)

    def far(value):
        return pltpu.with_memory_space_constraint(value, pltpu.HBM)

    weight = far(proto_weight)
    s_all = following(student_feats, "batch")
    t_all = following(teacher_feats, "batch")

    exps = pltpu.HBM((own, local_protos), BF16)
    t_exp, s_exp, stats = pl.pallas_call(
        stats_kernel,
        in_specs=[VMEM, VMEM, ANY],
        out_specs=[ANY, ANY, VMEM],
        out_shape=[exps, exps, struct((parts, 4 * own // LANES, LANES), F32)],
        scratch_shapes=[
            w_buffer,
            pltpu.VMEM((2, own, width), BF16),
            pltpu.VMEM((2, own, local_protos), BF16),
            pltpu.VMEM((own, local_protos), F32),
            pltpu.VMEM((2, own, LANES), F32),
            pltpu.VMEM((2, own, LANES), F32),
            sems, sems, sems,
        ],
        compiler_params=params(weight_bytes + 4 * exp_bytes),
        cost_estimate=cost(4 * own * width * local_protos, weight_bytes),
        name="own_rows",
    )(teacher_feats, student_feats, weight)
    t_exp, s_exp = far(t_exp), far(s_exp)

    back_student = pl.pallas_call(
        own_back_kernel,
        in_specs=[ANY] * 3,
        out_specs=VMEM,
        out_shape=struct((own, width), F32),
        scratch_shapes=[exp_buffer, w_buffer, sems, sems],
        compiler_params=params(weight_bytes + exp_bytes),
        cost_estimate=cost(2 * own * width * local_protos, weight_bytes),
        name="own_back",
    )(stats, s_exp, weight)
    stats = exchange(stats, "proto")

    first_shape = (groups, height + 8, LANES)
    factor, cols = pl.pallas_call(
        first_column_kernel,
        in_specs=[SMEM, VMEM, ANY, ANY] + [ANY] * (groups - 1),
        out_specs=[VMEM, VMEM],
        out_shape=[token, struct(first_shape, F32)],
        scratch_shapes=[spread, exp_buffer, sems],
        compiler_params=params(exp_bytes),
        cost_estimate=cost(2 * own * local_protos, exp_bytes),
        name="first_columns",
    )(place, stats, t_exp, back_student, *s_all)

    unit, feat, scaled = pl.pallas_call(
        functools.partial(student_rows_kernel, log_protos),
        in_specs=[SMEM, VMEM, VMEM] + [VMEM] * (groups - 1) + [ANY],
        out_specs=[VMEM] * 3,
        out_shape=[
            struct((others, width), BF16), struct((feats, rows), BF16), struct((feats, own), BF16),
        ],
        scratch_shapes=[pltpu.VMEM((width, rows), BF16)],
        compiler_params=params(2 * rows * width),
        cost_estimate=cost(8 * rows * width, 2 * rows * width),
        name="student_rows",
    )(place, factor, student_feats, *s_all, cols)
    cols = exchange(cols, "batch")
    logs = cols

    counts = [c * chunks // 8 for c in (1, 2, 1, 2, 2)]
    grad_parts = []

    def student_piece(before):
        turn = len(grad_parts)
        first, count = sum(counts[:turn]), counts[turn]
        grad_part, done = pl.pallas_call(
            functools.partial(student_kernel, log_protos, first),
            in_specs=[SMEM] + [VMEM] * 4 + [ANY] * 3,
            out_specs=[ANY, VMEM],
            out_shape=[pltpu.HBM((feats, count * WIDE), F32), token],
            scratch_shapes=[
                pltpu.VMEM((others, LANES), F32),
                pltpu.VMEM((2, others, WIDE), BF16),
                pltpu.VMEM((own, count * WIDE), BF16),
                pltpu.VMEM((width, count * WIDE), BF16),
                pltpu.VMEM((feats, count * WIDE), F32),
            ]
            + [pltpu.SemaphoreType.DMA((count,))] * 3,
            compiler_params=params(8 * 2**20),
            cost_estimate=cost(2.5 * rows * width * WIDE * count, 2 * width * WIDE * count),
            name="student_side",
        )(place, logs, unit, feat, scaled, s_exp, weight, before)
        grad_parts.append(far(grad_part))
        return done

    done = unit
    for turn in range(SWEEPS - 1):
        sums = pl.pallas_call(
            row_kernel,
            in_specs=[VMEM, VMEM, ANY, ANY],
            out_specs=VMEM,
            out_shape=struct((parts, 8, LANES), F32),
            scratch_shapes=[pltpu.VMEM((height, LANES), F32), spread, exp_buffer, sems],
            compiler_params=params(exp_bytes),
            cost_estimate=cost(2 * own * local_protos, exp_bytes),
            name="rows",
        )(cols, factor, t_exp, done)
        done = student_piece(sums)
        sums = exchange(sums, "proto")
        late = t_all if turn == 0 else []
        cols = pl.pallas_call(
            column_kernel,
            in_specs=[VMEM, VMEM, ANY, ANY] + [ANY] * len(late),
            out_specs=VMEM,
            out_shape=struct((groups, height, LANES), F32),
            scratch_shapes=[spread, exp_buffer, sems],
            compiler_params=params(exp_bytes),
            cost_estimate=cost(2 * own * local_protos, exp_bytes),
            name="columns",
        )(sums, factor, t_exp, done, *late)
        done = student_piece(cols)
        cols = exchange(cols, "batch")

    sum_rows = -(-(tiles + own // LANES) // 16) * 16
    message_shape = (parts, 2 * share + sum_rows, width)
    prob, col_scale, message = pl.pallas_call(
        functools.partial(last_kernel, groups),
        in_specs=[SMEM] + [VMEM] * 5 + [ANY] * 2 + [VMEM] * (groups - 1) + [ANY],
        out_specs=[ANY, VMEM, VMEM],
        out_shape=[
            pltpu.HBM((others, local_protos), BF16),
            struct((height, LANES), F32),
            struct(message_shape, BF16),
        ],
        scratch_shapes=[
            pltpu.VMEM((others, width), BF16),
            pltpu.VMEM((others, LANES), F32),
            pltpu.VMEM((others, LANES), F32),
            spread,
            pltpu.VMEM((own, width), F32),
            pltpu.VMEM((own, WIDE), BF16),
            pltpu.VMEM((sum_rows, LANES), F32),
            exp_buffer,
            w_buffer,
            pltpu.VMEM((others, local_protos), BF16),
            sems, sems, sems,
        ],
        compiler_params=params(weight_bytes + exp_bytes + others_bytes),
        cost_estimate=cost(2 * rows * width * local_protos, others_bytes),
        name="last_rows",
    )(
        place, logs, cols, factor, student_feats, back_student, t_exp, weight, *t_all, done,
    )
    done = student_piece(message)
    message = exchange(message, "proto")

    grad_rows, loss_part, sums = pl.pallas_call(
        functools.partial(rows_kernel, tiles, float(protos)),
        in_specs=[SMEM] + [VMEM] * 3 + [ANY],
        out_specs=[VMEM] * 3,
        out_shape=[struct((parts, share, width), F32), token, struct((sum_rows, LANES), F32)],
        scratch_shapes=[spread],
        compiler_params=params(0),
        name="row_grads",
    )(place, student_feats, message, logs, done)
    grad_rows = exchange(grad_rows, "proto").reshape(own, width)
    loss = tree_sum(loss_part, "batch")[0, 0] / rows

    grad_weight = pl.pallas_call(
        functools.partial(grad_kernel, counts, float(protos)),
        in_specs=[ANY] * 2 + [VMEM] * 4 + [ANY] * len(counts),
        out_specs=ANY,
        out_shape=struct((feats, local_protos), BF16),
        scratch_shapes=[
            pltpu.VMEM((feats, rows), BF16),
            exp_buffer,
            pltpu.VMEM((others, local_protos), BF16),
            pltpu.VMEM((feats, local_protos), F32),
            pltpu.VMEM((feats, local_protos), BF16),
            sems, sems, sems, sems,
        ],
        compiler_params=params(exp_bytes + others_bytes + 6 * feats * local_protos),
        cost_estimate=cost(2 * feats * rows * local_protos, others_bytes),
        name="weight_grads",
    )(t_exp, far(prob), feat, col_scale, sums, factor, *grad_parts)
    return grad_weight, grad_rows, loss


def solution(mesh):
    return jax.shard_map(
        local,
        mesh=mesh,
        in_specs=(P("batch", None), P("batch", None), P(None, "proto")),
        out_specs=(P("batch", "proto"), P("batch", None), P()),
        check_vma=False,
    )
```

time: 189 us -> 163 us (0.86)
  local copies, waits for them, and re-layouts: 64.7 us -> 2.3 us
  Pallas kernels: 65 us -> 90.5 us
  waiting for transfers between devices: 8.18 us -> 19.5 us
    unnamed x59 -> x5, local copies, waits for them, and re-layouts: 64.2 us -> 1.79 us
    pallas_call x14, Pallas kernels: 44.7 us -> 69.2 us  [the longest x5 24.9 us: student_piece(): pl.pallas_call(functools.partial(student_kernel, log_protos, first), in_s...]
    ppermute x6, waiting for transfers between devices: 2.41 us -> 10.9 us  [following(): lax.ppermute(value, axis, [(i, (i - s) % n) for i in range(n)])]
    all_to_all x8, waiting for transfers between devices: 5.76 us -> 8.54 us  [exchange(): return lax.all_to_all(value, axis, 0, 0)]
  transfers between devices with their start and end apart: 17 -> 17, of which waited for: 3 -> 7; matrix products, arithmetic and copies ran while one was open for 0% -> 0% of each run, Pallas kernels for 20% -> 35%
where the time goes in v5:
time: 163 us; the launch traced here: 162 us
  Pallas kernels  90.5 us (56%)
  starting transfers between devices  46.9 us (29%)
  waiting for transfers between devices  19.5 us (12%)
  between operations  2.64 us (2%)
  local copies, waits for them, and re-layouts  2.3 us (1%)
    all_to_all x8, starting transfers between devices, exchange(): return lax.all_to_all(value, axis, 0, 0)  30.6 us
    pallas_call x5, Pallas kernels, student_piece(): pl.pallas_call(functools.partial(student_kernel, log_protos, first), in_s...  24.9 us
    pallas_call x1, Pallas kernels, local(): pl.pallas_call(functools.partial(last_kernel, groups), in_specs=[SMEM] +...  19.6 us
    pallas_call x1, Pallas kernels, local(): pl.pallas_call(stats_kernel, in_specs=[VMEM, VMEM, ANY], out_specs=[ANY,...  12.9 us
    ppermute x6, starting transfers between devices, following(): lax.ppermute(value, axis, [(i, (i - s) % n) for i in range(n)])  11.9 us
    ppermute x6, waiting for transfers between devices, following(): lax.ppermute(value, axis, [(i, (i - s) % n) for i in range(n)])  10.9 us
    pallas_call x1, Pallas kernels, local(): pl.pallas_call(functools.partial(grad_kernel, counts, float(protos)), in_...  9.04 us
    all_to_all x8, waiting for transfers between devices, exchange(): return lax.all_to_all(value, axis, 0, 0)  8.54 us
  transfers between devices with their start and end apart: 17, of which 7 were waited for; matrix products, arithmetic and copies ran while one was open for 0% of the time, Pallas kernels for 35%

profile of v5, /device:TPU:0, one launch (start us, length us, event | category | flops | bytes accessed | tf_op | source)
XLA Modules:
  0.0 162.0 jit_solution(8314676169008139716)
XLA Ops:
  0.6 3.1 %collective-permute-start.2 = (bf16[256,512]{1,0:T(8,128)(2,1)}, bf16[256,512]{1,0:T(8,128)(2,1)S(1)}, u32[]{:S(2)}, u32[]{:S(2)}) collective-permute-start(bf16[256,512]{1,0:T(8,128)(2,1)} %s_ref.3), channel_id=1, source_target_pairs={{0,1},{1,2},{2,3},{3,0},{4,5},{5,6},{6,7},{7,4},{8,9},{9,10},{10,1... | collective-permute-start | bytes 786440 | tf_op jit(solution)/shard_map/ppermute | solution.py:516
  8.6 12.9 %own_rows.1 = (bf16[256,8192]{1,0:T(8,128)(2,1)}, bf16[256,8192]{1,0:T(8,128)(2,1)}, f32[8,8,128]{2,1,0:T(8,128)}) custom-call(bf16[256,512]{1,0:T(8,128)(2,1)} %t_ref.1, bf16[256,512]{1,0:T(8,128)(2,1)S(1)} %copy-done, bf16[512,8192]{1,0:T(8,128)(2,1)} %w_hbm.15), custom_call_target="tpu_custom_call" | custom-call | flops 4294967296 | bytes 8388608 | tf_op jit(solution)/shard_map/own_rows/pallas_call | solution.py:561
  21.6 3.7 %all-to-all-start = ((f32[8,8,128]{2,1,0:T(8,128)}), f32[8,8,128]{2,1,0:T(8,128)S(1)}, u32[]{:S(2)}, u32[]{:S(2)}) async-start(f32[8,8,128]{2,1,0:T(8,128)} %get-tuple-element.28.before_ref), calls=%async_computation | async-start | bytes 65536 | tf_op jit(solution)/shard_map/all_to_all | solution.py:511
  25.3 5.3 %own_back.1.refs_0_.student_ref = f32[256,512]{1,0:T(8,128)S(1)} custom-call(f32[8,8,128]{2,1,0:T(8,128)} %get-tuple-element.28.before_ref, bf16[256,8192]{1,0:T(8,128)(2,1)} %get-tuple-element.29.exp_hbm, bf16[512,8192]{1,0:T(8,128)(2,1)} %w_hbm.15), custom_call_target="tpu_custom_call" | custom-call | flops 2147483648 | bytes 8388608 | tf_op jit(solution)/shard_map/own_back/pallas_call | solution.py:581
  30.7 3.6 %first_columns.1 = (f32[8,128]{1,0:T(8,128)S(1)}, f32[4,72,128]{2,1,0:T(8,128)}) custom-call(s32[2]{0:T(128)S(1)} %pad_add_fusion.place_ref, f32[8,8,128]{2,1,0:T(8,128)S(1)} %all-to-all-done.stats_ref, bf16[256,8192]{1,0:T(8,128)(2,1)} %get-tuple-element.27.exp_hbm, f32[256,512]{1,0:T(8,128)S(1)} %own_back.1.refs_0_.student_ref, ...), custom_call_target="tpu_custom_call" | custom-call | flops 4194304 | bytes 4194304 | tf_op jit(solution)/shard_map/first_columns/pallas_call | solution.py:594
  34.3 3.3 %all-to-all-start.1 = ((f32[4,72,128]{2,1,0:T(8,128)}), f32[4,72,128]{2,1,0:T(8,128)S(1)}, u32[]{:S(2)}, u32[]{:S(2)}) async-start(f32[4,72,128]{2,1,0:T(8,128)} %get-tuple-element.30.refs_3_), calls=%async_computation.1 | async-start | bytes 294912 | tf_op jit(solution)/shard_map/all_to_all | solution.py:511
  37.7 3.8 %collective-permute-start.3 = (bf16[256,512]{1,0:T(8,128)(2,1)}, bf16[256,512]{1,0:T(8,128)(2,1)S(1)}, u32[]{:S(2)}, u32[]{:S(2)}) collective-permute-start(bf16[256,512]{1,0:T(8,128)(2,1)} %t_ref.1), channel_id=1, source_target_pairs={{0,3},{1,0},{2,1},{3,2},{4,7},{5,4},{6,5},{7,6},{8,11},{9,8},{10,9... | collective-permute-start | bytes 786440 | tf_op jit(solution)/shard_map/ppermute | solution.py:516
  48.3 4.3 %all-to-all-start.2 = ((f32[8,8,128]{2,1,0:T(8,128)}), f32[8,8,128]{2,1,0:T(8,128)S(1)}, u32[]{:S(2)}, u32[]{:S(2)}) async-start(f32[8,8,128]{2,1,0:T(8,128)} %rows.2.refs_0_), calls=%async_computation.2 | async-start | bytes 65536 | tf_op jit(solution)/shard_map/all_to_all | solution.py:511
  52.6 4.1 %student_side.5 = (f32[128,1024]{1,0:T(8,128)}, f32[8,128]{1,0:T(8,128)S(1)}) custom-call(s32[2]{0:T(128)S(1)} %pad_add_fusion.place_ref, f32[4,72,128]{2,1,0:T(8,128)S(1)} %all-to-all-done.1.cols_ref.logs_ref, bf16[768,512]{1,0:T(8,128)(2,1)S(1)} %get-tuple-element.32.refs_0_.unit, bf16[128,1024]{1,0:T(8,128)(2,1)S(1)} %get-tuple-element.33.feat_ref, ...), custom_call_target="tpu_custom_call" | custom-call | flops 1342177280 | bytes 1048576 | tf_op jit(solution)/shard_map/student_side/pallas_call | solution.py:626
  56.8 10.7 %collective-permute-done.4.refs_2_.refs_1_ = bf16[256,512]{1,0:T(8,128)(2,1)} collective-permute-done((bf16[256,512]{1,0:T(8,128)(2,1)}, bf16[256,512]{1,0:T(8,128)(2,1)}, u32[]{:S(2)}, u32[]{:S(2)}) %collective-permute-start.4) | collective-permute-done | bytes 262176 | tf_op jit(solution)/shard_map/ppermute | solution.py:516
  70.6 3.3 %all-to-all-start.3 = ((f32[4,64,128]{2,1,0:T(8,128)}), f32[4,64,128]{2,1,0:T(8,128)S(1)}, u32[]{:S(2)}, u32[]{:S(2)}) async-start(f32[4,64,128]{2,1,0:T(8,128)} %columns.2.refs_0_), calls=%async_computation.3 | async-start | bytes 262144 | tf_op jit(solution)/shard_map/all_to_all | solution.py:511
  73.9 5.6 %student_side.6 = (f32[128,2048]{1,0:T(8,128)}, f32[8,128]{1,0:T(8,128)S(1)}) custom-call(s32[2]{0:T(128)S(1)} %pad_add_fusion.place_ref, f32[4,72,128]{2,1,0:T(8,128)S(1)} %all-to-all-done.1.cols_ref.logs_ref, bf16[768,512]{1,0:T(8,128)(2,1)S(1)} %get-tuple-element.32.refs_0_.unit, bf16[128,1024]{1,0:T(8,128)(2,1)S(1)} %get-tuple-element.33.feat_ref, ...), custom_call_target="tpu_custom_call" | custom-call | flops 2684354560 | bytes 2097152 | tf_op jit(solution)/shard_map/student_side/pallas_call | solution.py:626
  80.0 3.0 %rows.3.refs_0_ = f32[8,8,128]{2,1,0:T(8,128)} custom-call(f32[4,64,128]{2,1,0:T(8,128)S(1)} %all-to-all-done.3.cols_ref, f32[8,128]{1,0:T(8,128)S(1)} %get-tuple-element.31.factor_ref, bf16[256,8192]{1,0:T(8,128)(2,1)} %get-tuple-element.27.exp_hbm, f32[8,128]{1,0:T(8,128)S(1)} %get-tuple-element.36.refs_0_), custom_call_target="tpu_custom_call" | custom-call | flops 4194304 | bytes 4194304 | tf_op jit(solution)/shard_map/rows/pallas_call | solution.py:648
  83.0 3.8 %all-to-all-start.4 = ((f32[8,8,128]{2,1,0:T(8,128)}), f32[8,8,128]{2,1,0:T(8,128)S(1)}, u32[]{:S(2)}, u32[]{:S(2)}) async-start(f32[8,8,128]{2,1,0:T(8,128)} %rows.3.refs_0_), calls=%async_computation.4 | async-start | bytes 65536 | tf_op jit(solution)/shard_map/all_to_all | solution.py:511
  86.8 4.1 %student_side.7 = (f32[128,1024]{1,0:T(8,128)}, f32[8,128]{1,0:T(8,128)S(1)}) custom-call(s32[2]{0:T(128)S(1)} %pad_add_fusion.place_ref, f32[4,72,128]{2,1,0:T(8,128)S(1)} %all-to-all-done.1.cols_ref.logs_ref, bf16[768,512]{1,0:T(8,128)(2,1)S(1)} %get-tuple-element.32.refs_0_.unit, bf16[128,1024]{1,0:T(8,128)(2,1)S(1)} %get-tuple-element.33.feat_ref, ...), custom_call_target="tpu_custom_call" | custom-call | flops 1342177280 | bytes 1048576 | tf_op jit(solution)/shard_map/student_side/pallas_call | solution.py:626
  94.7 4.7 %all-to-all-start.5 = ((f32[4,64,128]{2,1,0:T(8,128)}), f32[4,64,128]{2,1,0:T(8,128)S(1)}, u32[]{:S(2)}, u32[]{:S(2)}) async-start(f32[4,64,128]{2,1,0:T(8,128)} %columns.3.refs_0_), calls=%async_computation.5 | async-start | bytes 262144 | tf_op jit(solution)/shard_map/all_to_all | solution.py:511
  99.4 5.6 %student_side.8 = (f32[128,2048]{1,0:T(8,128)}, f32[8,128]{1,0:T(8,128)S(1)}) custom-call(s32[2]{0:T(128)S(1)} %pad_add_fusion.place_ref, f32[4,72,128]{2,1,0:T(8,128)S(1)} %all-to-all-done.1.cols_ref.logs_ref, bf16[768,512]{1,0:T(8,128)(2,1)S(1)} %get-tuple-element.32.refs_0_.unit, bf16[128,1024]{1,0:T(8,128)(2,1)S(1)} %get-tuple-element.33.feat_ref, ...), custom_call_target="tpu_custom_call" | custom-call | flops 2684354560 | bytes 2097152 | tf_op jit(solution)/shard_map/student_side/pallas_call | solution.py:626
  105.4 19.6 %last_rows.1 = (bf16[768,8192]{1,0:T(8,128)(2,1)}, f32[64,128]{1,0:T(8,128)S(1)}, bf16[8,80,512]{2,1,0:T(8,128)(2,1)}) custom-call(s32[2]{0:T(128)S(1)} %pad_add_fusion.place_ref, f32[4,72,128]{2,1,0:T(8,128)S(1)} %all-to-all-done.1.cols_ref.logs_ref, f32[4,64,128]{2,1,0:T(8,128)S(1)} %all-to-all-done.5.cols_ref, f32[8,128]{1,0:T(8,128)S(1)} %get-tuple-element.31.factor_ref, ...), custom_call_target="tpu_custom_call" | custom-call | flops 8589934592 | bytes 12582912 | tf_op jit(solution)/shard_map/last_rows/pallas_call | solution.py:676
  125.1 3.6 %all-to-all-start.6 = ((bf16[8,80,512]{2,1,0:T(8,128)(2,1)}), bf16[8,80,512]{2,1,0:T(8,128)(2,1)S(1)}, u32[]{:S(2)}, u32[]{:S(2)}) async-start(bf16[8,80,512]{2,1,0:T(8,128)(2,1)} %get-tuple-element.41.refs_0_), calls=%async_computation.6 | async-start | bytes 1310720 | tf_op jit(solution)/shard_map/all_to_all | solution.py:511
  128.7 5.6 %student_side.9 = (f32[128,2048]{1,0:T(8,128)}, f32[8,128]{1,0:T(8,128)S(1)}) custom-call(s32[2]{0:T(128)S(1)} %pad_add_fusion.place_ref, f32[4,72,128]{2,1,0:T(8,128)S(1)} %all-to-all-done.1.cols_ref.logs_ref, bf16[768,512]{1,0:T(8,128)(2,1)S(1)} %get-tuple-element.32.refs_0_.unit, bf16[128,1024]{1,0:T(8,128)(2,1)S(1)} %get-tuple-element.33.feat_ref, ...), custom_call_target="tpu_custom_call" | custom-call | flops 2684354560 | bytes 2097152 | tf_op jit(solution)/shard_map/student_side/pallas_call | solution.py:626
  134.3 5.5 %all-to-all-done.6.message_ref = bf16[8,80,512]{2,1,0:T(8,128)(2,1)S(1)} async-done(((bf16[8,80,512]{2,1,0:T(8,128)(2,1)}), bf16[8,80,512]{2,1,0:T(8,128)(2,1)S(1)}, u32[]{:S(2)}, u32[]{:S(2)}) %all-to-all-start.6) | async-done | bytes 655392 | tf_op jit(solution)/shard_map/all_to_all | solution.py:511
  141.6 3.8 %all-to-all-start.7 = ((f32[8,32,512]{2,1,0:T(8,128)}), f32[8,32,512]{2,1,0:T(8,128)S(1)}, u32[]{:S(2)}, u32[]{:S(2)}) async-start(f32[8,32,512]{2,1,0:T(8,128)} %get-tuple-element.49), calls=%async_computation.7 | async-start | bytes 1048576 | tf_op jit(solution)/shard_map/all_to_all | solution.py:511
  145.3 3.3 %collective-permute-start.8 = (f32[8,128]{1,0:T(8,128)S(1)}, f32[8,128]{1,0:T(8,128)S(1)}, u32[]{:S(2)}, u32[]{:S(2)}) collective-permute-start(f32[8,128]{1,0:T(8,128)S(1)} %get-tuple-element.50), channel_id=1, source_target_pairs={{0,3},{1,2},{2,1},{3,0},{4,7},{5,6},{6,5},{7,4},{8,11},{9,10},{10,... | collective-permute-start | bytes 12296 | tf_op jit(solution)/shard_map/ppermute | solution.py:522
  149.8 9.0 %weight_grads.1 = bf16[128,8192]{1,0:T(8,128)(2,1)} custom-call(bf16[256,8192]{1,0:T(8,128)(2,1)} %get-tuple-element.27.exp_hbm, bf16[768,8192]{1,0:T(8,128)(2,1)} %get-tuple-element.39.prob_hbm, bf16[128,1024]{1,0:T(8,128)(2,1)S(1)} %get-tuple-element.33.feat_ref, f32[64,128]{1,0:T(8,128)S(1)} %get-tuple-element.40.scale_ref, ...), custom_call_target="tpu_custom_call" | custom-call | flops 2147483648 | bytes 12582912 | tf_op jit(solution)/shard_map/weight_grads/pallas_call | solution.py:719
  (34 shorter events, 23.9 us)
Async XLA Ops:
  0.6 30.1 %collective-permute-start.2 = (bf16[256,512]{1,0:T(8,128)(2,1)}, bf16[256,512]{1,0:T(8,128)(2,1)S(1)}, u32[]{:S(2)}, u32[]{:S(2)}) collective-permute-start(bf16[256,512]{1,0:T(8,128)(2,1)} %s_ref.3), channel_id=1, source_target_pairs={{0,1},{1,2},{2,3},{3,0},{4,5},{5,6},{6,7},{7,4},{8,9},{9,10},{10,1... | collective-permute-start | bytes 786440 | tf_op jit(solution)/shard_map/ppermute | solution.py:516
  3.7 27.0 %collective-permute-start.1 = (bf16[256,512]{1,0:T(8,128)(2,1)}, bf16[256,512]{1,0:T(8,128)(2,1)S(1)}, u32[]{:S(2)}, u32[]{:S(2)}) collective-permute-start(bf16[256,512]{1,0:T(8,128)(2,1)} %s_ref.3), channel_id=1, source_target_pairs={{0,2},{1,3},{2,0},{3,1},{4,6},{5,7},{6,4},{7,5},{8,10},{9,11},{10,... | collective-permute-start | bytes 786440 | tf_op jit(solution)/shard_map/ppermute | solution.py:516
  6.3 24.4 %collective-permute-start = (bf16[256,512]{1,0:T(8,128)(2,1)}, bf16[256,512]{1,0:T(8,128)(2,1)S(1)}, u32[]{:S(2)}, u32[]{:S(2)}) collective-permute-start(bf16[256,512]{1,0:T(8,128)(2,1)} %s_ref.3), channel_id=1, source_target_pairs={{0,3},{1,0},{2,1},{3,2},{4,7},{5,4},{6,5},{7,6},{8,11},{9,8},{10,9... | collective-permute-start | bytes 786440 | tf_op jit(solution)/shard_map/ppermute | solution.py:516
  7.6 1.0 copy-start
  21.6 9.1 %all-to-all-start = ((f32[8,8,128]{2,1,0:T(8,128)}), f32[8,8,128]{2,1,0:T(8,128)S(1)}, u32[]{:S(2)}, u32[]{:S(2)}) async-start(f32[8,8,128]{2,1,0:T(8,128)} %get-tuple-element.28.before_ref), calls=%async_computation | async-start | bytes 65536 | tf_op jit(solution)/shard_map/all_to_all | solution.py:511
  30.6 12.0 %copy-start.1 = (bf16[256,512]{1,0:T(8,128)(2,1)S(1)}, bf16[256,512]{1,0:T(8,128)(2,1)}, u32[]{:S(2)}) copy-start(bf16[256,512]{1,0:T(8,128)(2,1)} %s_ref.3) | copy-start | bytes 786436
  34.3 10.9 %all-to-all-start.1 = ((f32[4,72,128]{2,1,0:T(8,128)}), f32[4,72,128]{2,1,0:T(8,128)S(1)}, u32[]{:S(2)}, u32[]{:S(2)}) async-start(f32[4,72,128]{2,1,0:T(8,128)} %get-tuple-element.30.refs_3_), calls=%async_computation.1 | async-start | bytes 294912 | tf_op jit(solution)/shard_map/all_to_all | solution.py:511
  37.7 19.0 %collective-permute-start.3 = (bf16[256,512]{1,0:T(8,128)(2,1)}, bf16[256,512]{1,0:T(8,128)(2,1)S(1)}, u32[]{:S(2)}, u32[]{:S(2)}) collective-permute-start(bf16[256,512]{1,0:T(8,128)(2,1)} %t_ref.1), channel_id=1, source_target_pairs={{0,3},{1,0},{2,1},{3,2},{4,7},{5,4},{6,5},{7,6},{8,11},{9,8},{10,9... | collective-permute-start | bytes 786440 | tf_op jit(solution)/shard_map/ppermute | solution.py:516
  41.5 15.4 %collective-permute-start.5 = (bf16[256,512]{1,0:T(8,128)(2,1)}, bf16[256,512]{1,0:T(8,128)(2,1)S(1)}, u32[]{:S(2)}, u32[]{:S(2)}) collective-permute-start(bf16[256,512]{1,0:T(8,128)(2,1)} %t_ref.1), channel_id=1, source_target_pairs={{0,1},{1,2},{2,3},{3,0},{4,5},{5,6},{6,7},{7,4},{8,9},{9,10},{10,1... | collective-permute-start | bytes 786440 | tf_op jit(solution)/shard_map/ppermute | solution.py:516
  41.5 26.1 %collective-permute-start.4 = (bf16[256,512]{1,0:T(8,128)(2,1)}, bf16[256,512]{1,0:T(8,128)(2,1)}, u32[]{:S(2)}, u32[]{:S(2)}) collective-permute-start(bf16[256,512]{1,0:T(8,128)(2,1)} %t_ref.1), channel_id=1, source_target_pairs={{0,2},{1,3},{2,0},{3,1},{4,6},{5,7},{6,4},{7,5},{8,10},{9,11},{10,... | collective-permute-start | bytes 786440 | tf_op jit(solution)/shard_map/ppermute | solution.py:516
  48.3 19.3 %all-to-all-start.2 = ((f32[8,8,128]{2,1,0:T(8,128)}), f32[8,8,128]{2,1,0:T(8,128)S(1)}, u32[]{:S(2)}, u32[]{:S(2)}) async-start(f32[8,8,128]{2,1,0:T(8,128)} %rows.2.refs_0_), calls=%async_computation.2 | async-start | bytes 65536 | tf_op jit(solution)/shard_map/all_to_all | solution.py:511
  70.6 9.4 %all-to-all-start.3 = ((f32[4,64,128]{2,1,0:T(8,128)}), f32[4,64,128]{2,1,0:T(8,128)S(1)}, u32[]{:S(2)}, u32[]{:S(2)}) async-start(f32[4,64,128]{2,1,0:T(8,128)} %columns.2.refs_0_), calls=%async_computation.3 | async-start | bytes 262144 | tf_op jit(solution)/shard_map/all_to_all | solution.py:511
  83.0 8.6 %all-to-all-start.4 = ((f32[8,8,128]{2,1,0:T(8,128)}), f32[8,8,128]{2,1,0:T(8,128)S(1)}, u32[]{:S(2)}, u32[]{:S(2)}) async-start(f32[8,8,128]{2,1,0:T(8,128)} %rows.3.refs_0_), calls=%async_computation.4 | async-start | bytes 65536 | tf_op jit(solution)/shard_map/all_to_all | solution.py:511
  94.7 10.8 %all-to-all-start.5 = ((f32[4,64,128]{2,1,0:T(8,128)}), f32[4,64,128]{2,1,0:T(8,128)S(1)}, u32[]{:S(2)}, u32[]{:S(2)}) async-start(f32[4,64,128]{2,1,0:T(8,128)} %columns.3.refs_0_), calls=%async_computation.5 | async-start | bytes 262144 | tf_op jit(solution)/shard_map/all_to_all | solution.py:511
  125.1 14.8 %all-to-all-start.6 = ((bf16[8,80,512]{2,1,0:T(8,128)(2,1)}), bf16[8,80,512]{2,1,0:T(8,128)(2,1)S(1)}, u32[]{:S(2)}, u32[]{:S(2)}) async-start(bf16[8,80,512]{2,1,0:T(8,128)(2,1)} %get-tuple-element.41.refs_0_), calls=%async_computation.6 | async-start | bytes 1310720 | tf_op jit(solution)/shard_map/all_to_all | solution.py:511
  141.6 18.5 %all-to-all-start.7 = ((f32[8,32,512]{2,1,0:T(8,128)}), f32[8,32,512]{2,1,0:T(8,128)S(1)}, u32[]{:S(2)}, u32[]{:S(2)}) async-start(f32[8,32,512]{2,1,0:T(8,128)} %get-tuple-element.49), calls=%async_computation.7 | async-start | bytes 1048576 | tf_op jit(solution)/shard_map/all_to_all | solution.py:511
  145.3 13.5 %collective-permute-start.8 = (f32[8,128]{1,0:T(8,128)S(1)}, f32[8,128]{1,0:T(8,128)S(1)}, u32[]{:S(2)}, u32[]{:S(2)}) collective-permute-start(f32[8,128]{1,0:T(8,128)S(1)} %get-tuple-element.50), channel_id=1, source_target_pairs={{0,3},{1,2},{2,1},{3,0},{4,7},{5,6},{6,5},{7,4},{8,11},{9,10},{10,... | collective-permute-start | bytes 12296 | tf_op jit(solution)/shard_map/ppermute | solution.py:522
  148.6 10.2 %collective-permute-start.7 = (f32[8,128]{1,0:T(8,128)S(1)}, f32[8,128]{1,0:T(8,128)S(1)}, u32[]{:S(2)}, u32[]{:S(2)}) collective-permute-start(f32[8,128]{1,0:T(8,128)S(1)} %get-tuple-element.50), channel_id=1, source_target_pairs={{0,2},{1,3},{2,0},{3,1},{4,6},{5,7},{6,4},{7,5},{8,10},{9,11},{10,... | collective-permute-start | bytes 12296 | tf_op jit(solution)/shard_map/ppermute | solution.py:522
  148.6 10.2 %collective-permute-start.6 = (f32[8,128]{1,0:T(8,128)S(1)}, f32[8,128]{1,0:T(8,128)S(1)}, u32[]{:S(2)}, u32[]{:S(2)}) collective-permute-start(f32[8,128]{1,0:T(8,128)S(1)} %get-tuple-element.50), channel_id=1, source_target_pairs={{0,1},{1,0},{2,3},{3,2},{4,5},{5,4},{6,7},{7,6},{8,9},{9,8},{10,11... | collective-permute-start | bytes 12296 | tf_op jit(solution)/shard_map/ppermute | solution.py:522
